TPU v7x, 128 devices: a whole 4x4x4 slice. The times are simulated.
128 devices in a mesh: region: 4 (over x), shard: 32 (over z, y, core).
Axes of the slice: x: 4, y: 4, z: 4, core: 2. Of those that a mesh axis runs over, the one named last changes fastest.
Arguments:
- features: bfloat16 [128, 512, 256], P(('region', 'shard')), may hold values from -6 to 6
- cotangent: bfloat16 [128, 512, 256], P(('region', 'shard')), may hold values from -6 to 6
- weight_one: bfloat16 [27, 256, 256], replicated, may hold values from -0.078125 to 0.078125
- weight_two: bfloat16 [27, 256, 256], replicated, may hold values from -0.078125 to 0.078125
- occupancy: int32 [128], P(('region', 'shard')), may hold values from 0 to 1, as said below
- neighbour_owner: int32 [128, 26], P(('region', 'shard')), may hold values from -1 to 127, as said below
- neighbour_slot: int32 [128, 26], P(('region', 'shard')), may hold values from -1 to 0, as said below
Outputs:
- output: bfloat16 [128, 512, 256], P(('region', 'shard'))
- grad_input: bfloat16 [128, 512, 256], P(('region', 'shard'))
- grad_weight_one: bfloat16 [27, 256, 256], replicated
- grad_weight_two: bfloat16 [27, 256, 256], replicated
Inputs may be any that keep to these rules, and one draw needn't show every extreme that they name: `occupancy`: live bricks fill the first slots of a device; a device may hold none; the first three and the last three devices have all 1 slots live. `neighbour_owner`: for each brick and offset, the device (numbered region-major) holding the neighbouring brick, or -1 where there is none. Neighbours lie on the same device or on a device at most two places earlier or later in that numbering, and two places is reached. Adjacency is symmetric: if brick b has neighbour n at offset o, then n has b at offset -o. Only live bricks have neighbours, and every neighbour is live. `neighbour_slot`: the neighbour's slot on its device, -1 exactly where neighbour_owner is -1.
All inputs are finite; a program needn't handle non-finite values.
Results may differ from a plain program's by a relative error of at most 0.0053.
Values may be sent and summed in bfloat16 or wider, within the bound.
No kernel may reach another device: no remote copies, remote signals or barrier semaphores. Data moves between devices by JAX's collectives and lax.ppermute only.
A program may use at most 128 MiB of HBM per device.

v0:
```python
from functools import partial

import jax
import jax.numpy as jnp
from jax import lax
from jax.sharding import PartitionSpec as P

BRICK_EDGE = 8


every_offset = [
    (step_x, step_y, step_z)
    for step_x in (-1, 0, 1)
    for step_y in (-1, 0, 1)
    for step_z in (-1, 0, 1)
]
reversed_offset = every_offset[::-1]
side_offsets = [entry for entry in every_offset if entry != (0, 0, 0)]


def shifted(array, axis, by):
    devices = lax.axis_size(axis)
    pairs = [(i, i + by) for i in range(devices) if 0 <= i + by < devices]
    return lax.ppermute(array, axis, pairs)


def source_range(direction):
    if direction > 0:
        return slice(0, 1)
    if direction < 0:
        return slice(BRICK_EDGE - 1, BRICK_EDGE)
    return slice(0, BRICK_EDGE)


def target_range(direction):
    if direction > 0:
        return slice(BRICK_EDGE + 1, BRICK_EDGE + 2)
    if direction < 0:
        return slice(0, 1)
    return slice(1, BRICK_EDGE + 1)


def framed(centre, sources, picked, present):
    channels = centre.shape[-1]
    edge_cells = BRICK_EDGE
    framed_grid = jnp.zeros(
        (edge_cells + 2, edge_cells + 2, edge_cells + 2, channels), centre.dtype
    )
    framed_grid = framed_grid.at[1 : edge_cells + 1, 1 : edge_cells + 1, 1 : edge_cells + 1].set(
        centre.reshape(edge_cells, edge_cells, edge_cells, channels)
    )
    for position, (step_x, step_y, step_z) in enumerate(side_offsets):
        source = lax.dynamic_index_in_dim(sources, picked[position], 0, keepdims=False)
        source = source.reshape(edge_cells, edge_cells, edge_cells, channels)
        pieces = source[source_range(step_x), source_range(step_y), source_range(step_z)]
        pieces = jnp.where(present[position], pieces, jnp.zeros_like(pieces))
        framed_grid = framed_grid.at[
            target_range(step_x), target_range(step_y), target_range(step_z)
        ].set(pieces)
    return framed_grid


def unfolded(framed_grid, offsets):
    edge_cells = BRICK_EDGE
    channels = framed_grid.shape[-1]
    patches = []
    for step_x, step_y, step_z in offsets:
        window = framed_grid[
            1 + step_x : 1 + step_x + edge_cells,
            1 + step_y : 1 + step_y + edge_cells,
            1 + step_z : 1 + step_z + edge_cells,
        ]
        patches.append(window.reshape(edge_cells**3, channels))
    return jnp.concatenate(patches, axis=1)


def on_device(
    features, cotangent, weight_one, weight_two, occupancy, neighbour_owner, neighbour_slot
):
    slot_count, voxels, channels = features.shape
    devices = lax.axis_size(("region", "shard"))
    own_index = lax.axis_index(("region", "shard"))
    live_mask = (jnp.arange(slot_count) < occupancy[0])[:, None, None]
    present = neighbour_owner >= 0
    picked = jnp.where(present, (neighbour_owner - own_index + 2) * slot_count + neighbour_slot, 0)

    def nearby(field_data):
        arrived = []
        for offset in (2, 1, -1, -2):
            arrived.append(shifted(field_data, ("region", "shard"), offset))
        return jnp.concatenate([arrived[0], arrived[1], field_data, arrived[2], arrived[3]], axis=0)

    def frames(field_data):
        return jax.vmap(framed, in_axes=(0, None, 0, 0))(
            field_data, nearby(field_data), picked, present
        )

    def columns(framed_all, offsets):
        stacked = jax.vmap(partial(unfolded, offsets=offsets))(framed_all)
        return stacked.reshape(slot_count * voxels, len(offsets) * channels)

    flat_one = weight_one.reshape(27 * channels, channels)
    flat_two = weight_two.reshape(27 * channels, channels)
    turned_one = jnp.transpose(weight_one, (0, 2, 1)).reshape(27 * channels, channels)
    turned_two = jnp.transpose(weight_two, (0, 2, 1)).reshape(27 * channels, channels)
    masked_in = jnp.where(live_mask, features, jnp.zeros_like(features))
    masked_cot = jnp.where(live_mask, cotangent, jnp.zeros_like(cotangent))
    grid_in = frames(masked_in)
    pre_act = jnp.dot(columns(grid_in, every_offset), flat_one, preferred_element_type=jnp.float32)
    hidden = jax.nn.silu(pre_act).astype(jnp.bfloat16).reshape(slot_count, voxels, channels)
    grid_hidden = frames(hidden)
    output = jnp.dot(
        columns(grid_hidden, every_offset), flat_two, preferred_element_type=jnp.float32
    )
    output = output.astype(jnp.bfloat16).reshape(slot_count, voxels, channels)
    grid_cot = frames(masked_cot)
    grad_hidden = jnp.dot(
        columns(grid_cot, reversed_offset), turned_two, preferred_element_type=jnp.float32
    )
    sigmoid_pre = jax.nn.sigmoid(pre_act)
    grad_pre = (grad_hidden * sigmoid_pre * (1.0 + pre_act * (1.0 - sigmoid_pre))).astype(
        jnp.bfloat16
    )
    grid_grad = frames(grad_pre.reshape(slot_count, voxels, channels))
    grad_input = jnp.dot(
        columns(grid_grad, reversed_offset), turned_one, preferred_element_type=jnp.float32
    )
    grad_input = grad_input.astype(jnp.bfloat16).reshape(slot_count, voxels, channels)
    contract = (((0,), (0,)), ((), ()))
    partial_two = lax.dot_general(
        columns(grid_hidden, every_offset),
        masked_cot.reshape(slot_count * voxels, channels),
        contract,
        preferred_element_type=jnp.float32,
    )
    partial_one = lax.dot_general(
        columns(grid_in, every_offset), grad_pre, contract, preferred_element_type=jnp.float32
    )
    grad_scale = float(slot_count * voxels * devices) ** (-0.5)
    summed_one, summed_two = lax.psum((partial_one, partial_two), ("region", "shard"))
    whole_one = (grad_scale * summed_one).astype(jnp.bfloat16)
    whole_two = (grad_scale * summed_two).astype(jnp.bfloat16)
    return (
        output,
        grad_input,
        whole_one.reshape(weight_one.shape),
        whole_two.reshape(weight_two.shape),
    )


def solution(mesh):
    in_specs = (
        P(("region", "shard"), None, None),
        P(("region", "shard"), None, None),
        P(),
        P(),
        P(("region", "shard")),
        P(("region", "shard"), None),
        P(("region", "shard"), None),
    )
    out_specs = (P(("region", "shard"), None, None), P(("region", "shard"), None, None), P(), P())
    return jax.shard_map(
        on_device, mesh=mesh, in_specs=in_specs, out_specs=out_specs, check_vma=False
    )
```

profile of v0, /device:TPU:1, one launch (start us, length us, event | category | flops | bytes accessed | tf_op | source)
XLA Modules:
  0.0 459.1 jit_solution(17829469345088715353)
XLA Ops:
  7.9 1.7 broadcast_select_fusion.1
  9.6 3.1 collective-permute-start
  12.7 5.0 %collective-permute-start.1 = (bf16[1,512,256]{2,1,0:T(8,128)(2,1)}, bf16[1,512,256]{2,1,0:T(8,128)(2,1)}, u32[]{:S(2)}, u32[]{:S(2)}) collective-permute-start(bf16[1,512,256]{2,1,0:T(8,128)(2,1)} %broadcast_select_fusion.1), channel_id=1, source_target_pairs={{0,1},{1,2},{2,3},{3,4},{4,5},{5,6},{6,7},{7,8},{8,9},{9,10},{10,1... | collective-permute-start | bytes 786440 | tf_op jit(solution)/shard_map/ppermute | solution.py:24
  17.7 1.9 collective-permute-start.2
  21.9 3.8 collective-permute-start.8
  62.1 5.7 %copy.11 = bf16[27,256,256]{1,2,0:T(8,128)(2,1)} copy(bf16[27,256,256]{2,1,0:T(8,128)(2,1)} %param.226) | data formatting | bytes 7077888 | tf_op args[3]
  85.2 4.4 collective-permute-start.9
  90.6 1.9 collective-permute-start.10
  105.5 2.1 constant_dynamic-slice_fusion.52
  112.7 1.7 broadcast_select_fusion.9
  135.6 2.0 copy-done.3
  137.6 2.8 multiply_convert_fusion.2
  140.3 4.7 %collective-permute-start.4 = (bf16[1,512,256]{2,1,0:T(8,128)(2,1)S(1)}, bf16[1,512,256]{2,1,0:T(8,128)(2,1)}, u32[]{:S(2)}, u32[]{:S(2)}) collective-permute-start(bf16[1,512,256]{2,1,0:T(8,128)(2,1)S(1)} %bitcast.477), channel_id=1, source_target_pairs={{0,2},{1,3},{2,4},{3,5},{4,6},{5,7},{6,8},{7,9},{8,10},{9,11},{10,... | collective-permute-start | bytes 786440 | tf_op jit(solution)/shard_map/ppermute | solution.py:24
  145.0 3.5 collective-permute-start.5
  149.5 1.9 collective-permute-start.6
  180.1 2.0 fusion.24
  182.4 4.9 %fusion.8 = f32[6912,256]{1,0:T(8,128)} fusion(bf16[512,256]{1,0:T(8,128)(2,1)S(1)} %fusion.24, bf16[1,512,6912]{2,1,0:T(8,128)(2,1)S(1)} %bitcast.354), kind=kOutput, calls=%fused_computation.8 | convolution fusion | flops 1811939328 | bytes 14417920 | tf_op jit(solution)/shard_map/dot_general | solution.py:136
  187.3 5.2 %collective-permute-start.12 = (bf16[1,512,256]{2,1,0:T(8,128)(2,1)S(1)}, bf16[1,512,256]{2,1,0:T(8,128)(2,1)S(1)}, u32[]{:S(2)}, u32[]{:S(2)}) collective-permute-start(bf16[1,512,256]{2,1,0:T(8,128)(2,1)S(1)} %bitcast.364), channel_id=1, source_target_pairs={{0,2},{1,3},{2,4},{3,5},{4,6},{5,7},{6,8},{7,9},{8,10},{9,11},{10,... | collective-permute-start | bytes 786440 | tf_op jit(solution)/shard_map/ppermute | solution.py:24
  192.7 3.9 collective-permute-start.13
  197.6 1.9 collective-permute-start.14
  204.1 1.7 collective-permute-done.14
  206.3 5.2 %collective-permute-done.15 = bf16[1,512,256]{2,1,0:T(8,128)(2,1)S(1)} collective-permute-done((bf16[1,512,256]{2,1,0:T(8,128)(2,1)S(1)}, bf16[1,512,256]{2,1,0:T(8,128)(2,1)S(1)}, u32[]{:S(2)}, u32[]{:S(2)}) %collective-permute-start.15) | collective-permute-done | bytes 262176 | tf_op jit(solution)/shard_map/ppermute | solution.py:24
  248.6 2.9 copy-done.1
  251.5 4.9 %fusion.4 = f32[6912,256]{1,0:T(8,128)} fusion(bf16[1,512,6912]{2,1,0:T(8,128)(2,1)S(1)} %constant_dynamic-update-slice_fusion.37, bf16[1,512,256]{2,1,0:T(8,128)(2,1)S(1)} %broadcast_select_fusion), kind=kOutput, calls=%fused_computation.4 | convolution fusion | flops 1811939328 | bytes 14417920 | tf_op jit(solution)/shard_map/dot_general | solution.py:130
  256.4 2.0 copy-done.4
  258.4 3.5 copy.12
  272.1 1.5 scatter.516
  288.2 2.7 fusion.30
  290.9 2.7 fusion.27
  293.6 150.5 %all-reduce.33.cloned.1.call-done = (f32[6912,256]{1,0:T(8,128)}, f32[6912,256]{1,0:T(8,128)}) async-done(((f32[6912,256]{1,0:T(8,128)}, f32[6912,256]{1,0:T(8,128)}), (f32[6912,256]{1,0:T(8,128)}, f32[6912,256]{1,0:T(8,128)})) %all-reduce.33.cloned.1.call-update) | async-done | bytes 14155792 | tf_op jit(solution)/shard_map/psum | solution.py:140
  444.1 5.6 %multiply_convert_fusion.1 = bf16[6912,256]{1,0:T(8,128)(2,1)} fusion(f32[6912,256]{1,0:T(8,128)} %get-tuple-element.2444), kind=kLoop, calls=%fused_computation.13 | loop fusion | flops 3538944 | bytes 10616832 | tf_op jit(solution)/shard_map/convert_element_type | solution.py:141
  449.7 2.5 multiply_convert_fusion
  (387 shorter events, 144.6 us)
Async XLA Ops:
  7.2 86.3 %copy-start.9 = (bf16[1,512,256]{2,1,0:T(8,128)(2,1)S(1)}, bf16[1,512,256]{2,1,0:T(8,128)(2,1)}, u32[]{:S(2)}) copy-start(bf16[1,512,256]{2,1,0:T(8,128)(2,1)} %param.223) | copy-start | bytes 786436
  7.2 436.9 %all-reduce.33.cloned.1.call-start = ((), (), s32[]{:S(2)}) async-start(), calls=%async_computation | async-start | bytes 28311552 | tf_op jit(solution)/shard_map/psum | solution.py:140
  9.6 74.9 %collective-permute-start = (bf16[1,512,256]{2,1,0:T(8,128)(2,1)}, bf16[1,512,256]{2,1,0:T(8,128)(2,1)S(1)}, u32[]{:S(2)}, u32[]{:S(2)}) collective-permute-start(bf16[1,512,256]{2,1,0:T(8,128)(2,1)} %broadcast_select_fusion.1), channel_id=1, source_target_pairs={{0,2},{1,3},{2,4},{3,5},{4,6},{5,7},{6,8},{7,9},{8,10},{9,11},{10,... | collective-permute-start | bytes 786440 | tf_op jit(solution)/shard_map/ppermute | solution.py:24
  12.7 77.9 %collective-permute-start.1 = (bf16[1,512,256]{2,1,0:T(8,128)(2,1)}, bf16[1,512,256]{2,1,0:T(8,128)(2,1)}, u32[]{:S(2)}, u32[]{:S(2)}) collective-permute-start(bf16[1,512,256]{2,1,0:T(8,128)(2,1)} %broadcast_select_fusion.1), channel_id=1, source_target_pairs={{0,1},{1,2},{2,3},{3,4},{4,5},{5,6},{6,7},{7,8},{8,9},{9,10},{10,1... | collective-permute-start | bytes 786440 | tf_op jit(solution)/shard_map/ppermute | solution.py:24
  17.7 75.9 %collective-permute-start.2 = (bf16[1,512,256]{2,1,0:T(8,128)(2,1)}, bf16[1,512,256]{2,1,0:T(8,128)(2,1)}, u32[]{:S(2)}, u32[]{:S(2)}) collective-permute-start(bf16[1,512,256]{2,1,0:T(8,128)(2,1)} %broadcast_select_fusion.1), channel_id=1, source_target_pairs={{1,0},{2,1},{3,2},{4,3},{5,4},{6,5},{7,6},{8,7},{9,8},{10,9},{11,1... | collective-permute-start | bytes 786440 | tf_op jit(solution)/shard_map/ppermute | solution.py:24
  19.6 76.2 %collective-permute-start.3 = (bf16[1,512,256]{2,1,0:T(8,128)(2,1)}, bf16[1,512,256]{2,1,0:T(8,128)(2,1)}, u32[]{:S(2)}, u32[]{:S(2)}) collective-permute-start(bf16[1,512,256]{2,1,0:T(8,128)(2,1)} %broadcast_select_fusion.1), channel_id=1, source_target_pairs={{2,0},{3,1},{4,2},{5,3},{6,4},{7,5},{8,6},{9,7},{10,8},{11,9},{12,... | collective-permute-start | bytes 786440 | tf_op jit(solution)/shard_map/ppermute | solution.py:24
  21.9 123.1 %collective-permute-start.8 = (bf16[1,512,256]{2,1,0:T(8,128)(2,1)S(1)}, bf16[1,512,256]{2,1,0:T(8,128)(2,1)}, u32[]{:S(2)}, u32[]{:S(2)}) collective-permute-start(bf16[1,512,256]{2,1,0:T(8,128)(2,1)S(1)} %broadcast_select_fusion), channel_id=1, source_target_pairs={{0,2},{1,3},{2,4},{3,5},{4,6},{5,7},{6,8},{7,9},{8,10},{9,11},{10,... | collective-permute-start | bytes 786440 | tf_op jit(solution)/shard_map/ppermute | solution.py:24
  85.2 64.4 %collective-permute-start.9 = (bf16[1,512,256]{2,1,0:T(8,128)(2,1)S(1)}, bf16[1,512,256]{2,1,0:T(8,128)(2,1)}, u32[]{:S(2)}, u32[]{:S(2)}) collective-permute-start(bf16[1,512,256]{2,1,0:T(8,128)(2,1)S(1)} %broadcast_select_fusion), channel_id=1, source_target_pairs={{0,1},{1,2},{2,3},{3,4},{4,5},{5,6},{6,7},{7,8},{8,9},{9,10},{10,1... | collective-permute-start | bytes 786440 | tf_op jit(solution)/shard_map/ppermute | solution.py:24
  90.6 61.9 %collective-permute-start.10 = (bf16[1,512,256]{2,1,0:T(8,128)(2,1)S(1)}, bf16[1,512,256]{2,1,0:T(8,128)(2,1)}, u32[]{:S(2)}, u32[]{:S(2)}) collective-permute-start(bf16[1,512,256]{2,1,0:T(8,128)(2,1)S(1)} %broadcast_select_fusion), channel_id=1, source_target_pairs={{1,0},{2,1},{3,2},{4,3},{5,4},{6,5},{7,6},{8,7},{9,8},{10,9},{11,1... | collective-permute-start | bytes 786440 | tf_op jit(solution)/shard_map/ppermute | solution.py:24
  93.6 61.2 %collective-permute-start.11 = (bf16[1,512,256]{2,1,0:T(8,128)(2,1)S(1)}, bf16[1,512,256]{2,1,0:T(8,128)(2,1)}, u32[]{:S(2)}, u32[]{:S(2)}) collective-permute-start(bf16[1,512,256]{2,1,0:T(8,128)(2,1)S(1)} %broadcast_select_fusion), channel_id=1, source_target_pairs={{2,0},{3,1},{4,2},{5,3},{6,4},{7,5},{8,6},{9,7},{10,8},{11,9},{12,... | collective-permute-start | bytes 786440 | tf_op jit(solution)/shard_map/ppermute | solution.py:24
  134.8 2.8 copy-start.3
  135.5 4.8 %copy-start = (bf16[1,512,6912]{2,1,0:T(8,128)(2,1)}, bf16[1,512,6912]{2,1,0:T(8,128)(2,1)S(1)}, u32[]{:S(2)}) copy-start(bf16[1,512,6912]{2,1,0:T(8,128)(2,1)S(1)} %constant_dynamic-update-slice_fusion.5) | copy-start | bytes 21233668
  137.6 14.9 %copy-start.10 = (bf16[1,512,256]{2,1,0:T(8,128)(2,1)S(1)}, bf16[1,512,256]{2,1,0:T(8,128)(2,1)}, u32[]{:S(2)}) copy-start(bf16[1,512,256]{2,1,0:T(8,128)(2,1)} %param.224) | copy-start | bytes 786436
  140.3 52.4 %collective-permute-start.4 = (bf16[1,512,256]{2,1,0:T(8,128)(2,1)S(1)}, bf16[1,512,256]{2,1,0:T(8,128)(2,1)}, u32[]{:S(2)}, u32[]{:S(2)}) collective-permute-start(bf16[1,512,256]{2,1,0:T(8,128)(2,1)S(1)} %bitcast.477), channel_id=1, source_target_pairs={{0,2},{1,3},{2,4},{3,5},{4,6},{5,7},{6,8},{7,9},{8,10},{9,11},{10,... | collective-permute-start | bytes 786440 | tf_op jit(solution)/shard_map/ppermute | solution.py:24
  145.0 52.6 %collective-permute-start.5 = (bf16[1,512,256]{2,1,0:T(8,128)(2,1)S(1)}, bf16[1,512,256]{2,1,0:T(8,128)(2,1)}, u32[]{:S(2)}, u32[]{:S(2)}) collective-permute-start(bf16[1,512,256]{2,1,0:T(8,128)(2,1)S(1)} %bitcast.478), channel_id=1, source_target_pairs={{0,1},{1,2},{2,3},{3,4},{4,5},{5,6},{6,7},{7,8},{8,9},{9,10},{10,1... | collective-permute-start | bytes 786440 | tf_op jit(solution)/shard_map/ppermute | solution.py:24
  149.5 52.4 %collective-permute-start.6 = (bf16[1,512,256]{2,1,0:T(8,128)(2,1)S(1)}, bf16[1,512,256]{2,1,0:T(8,128)(2,1)}, u32[]{:S(2)}, u32[]{:S(2)}) collective-permute-start(bf16[1,512,256]{2,1,0:T(8,128)(2,1)S(1)} %bitcast.479), channel_id=1, source_target_pairs={{1,0},{2,1},{3,2},{4,3},{5,4},{6,5},{7,6},{8,7},{9,8},{10,9},{11,1... | collective-permute-start | bytes 786440 | tf_op jit(solution)/shard_map/ppermute | solution.py:24
  152.5 50.4 %collective-permute-start.7 = (bf16[1,512,256]{2,1,0:T(8,128)(2,1)S(1)}, bf16[1,512,256]{2,1,0:T(8,128)(2,1)}, u32[]{:S(2)}, u32[]{:S(2)}) collective-permute-start(bf16[1,512,256]{2,1,0:T(8,128)(2,1)S(1)} %bitcast.480), channel_id=1, source_target_pairs={{2,0},{3,1},{4,2},{5,3},{6,4},{7,5},{8,6},{9,7},{10,8},{11,9},{12,... | collective-permute-start | bytes 786440 | tf_op jit(solution)/shard_map/ppermute | solution.py:24
  178.0 2.0 copy-start.6
  178.0 2.1 copy-start.12
  178.7 3.4 slice-start
  180.1 2.3 slice-start.1
  182.4 29.7 %copy-start.8 = (bf16[512,256]{1,0:T(8,128)(2,1)}, bf16[512,256]{1,0:T(8,128)(2,1)S(1)}, u32[]{:S(2)}) copy-start(bf16[512,256]{1,0:T(8,128)(2,1)S(1)} %fusion.24) | copy-start | bytes 786436
  187.3 13.2 %collective-permute-start.12 = (bf16[1,512,256]{2,1,0:T(8,128)(2,1)S(1)}, bf16[1,512,256]{2,1,0:T(8,128)(2,1)S(1)}, u32[]{:S(2)}, u32[]{:S(2)}) collective-permute-start(bf16[1,512,256]{2,1,0:T(8,128)(2,1)S(1)} %bitcast.364), channel_id=1, source_target_pairs={{0,2},{1,3},{2,4},{3,5},{4,6},{5,7},{6,8},{7,9},{8,10},{9,11},{10,... | collective-permute-start | bytes 786440 | tf_op jit(solution)/shard_map/ppermute | solution.py:24
  192.7 11.3 %collective-permute-start.13 = (bf16[1,512,256]{2,1,0:T(8,128)(2,1)S(1)}, bf16[1,512,256]{2,1,0:T(8,128)(2,1)S(1)}, u32[]{:S(2)}, u32[]{:S(2)}) collective-permute-start(bf16[1,512,256]{2,1,0:T(8,128)(2,1)S(1)} %bitcast.365), channel_id=1, source_target_pairs={{0,1},{1,2},{2,3},{3,4},{4,5},{5,6},{6,7},{7,8},{8,9},{9,10},{10,1... | collective-permute-start | bytes 786440 | tf_op jit(solution)/shard_map/ppermute | solution.py:24
  197.6 8.2 %collective-permute-start.14 = (bf16[1,512,256]{2,1,0:T(8,128)(2,1)S(1)}, bf16[1,512,256]{2,1,0:T(8,128)(2,1)S(1)}, u32[]{:S(2)}, u32[]{:S(2)}) collective-permute-start(bf16[1,512,256]{2,1,0:T(8,128)(2,1)S(1)} %bitcast.366), channel_id=1, source_target_pairs={{1,0},{2,1},{3,2},{4,3},{5,4},{6,5},{7,6},{8,7},{9,8},{10,9},{11,1... | collective-permute-start | bytes 786440 | tf_op jit(solution)/shard_map/ppermute | solution.py:24
  200.6 11.0 %collective-permute-start.15 = (bf16[1,512,256]{2,1,0:T(8,128)(2,1)S(1)}, bf16[1,512,256]{2,1,0:T(8,128)(2,1)S(1)}, u32[]{:S(2)}, u32[]{:S(2)}) collective-permute-start(bf16[1,512,256]{2,1,0:T(8,128)(2,1)S(1)} %bitcast.367), channel_id=1, source_target_pairs={{2,0},{3,1},{4,2},{5,3},{6,4},{7,5},{8,6},{9,7},{10,8},{11,9},{12,... | collective-permute-start | bytes 786440 | tf_op jit(solution)/shard_map/ppermute | solution.py:24
  248.6 2.9 copy-start.1
  256.4 2.0 copy-start.4
  284.3 2.4 copy-start.5
  284.3 3.8 slice-start.3
  284.8 6.1 %copy-start.7 = (bf16[27,256,256]{1,2,0:T(8,128)(2,1)S(1)}, bf16[27,256,256]{1,2,0:T(8,128)(2,1)}, u32[]{:S(2)}) copy-start(bf16[27,256,256]{1,2,0:T(8,128)(2,1)} %copy.12) | copy-start | bytes 10616836
  444.1 5.6 %copy-start.2 = (f32[6912,256]{1,0:T(8,128)S(1)}, f32[6912,256]{1,0:T(8,128)}, u32[]{:S(2)}) copy-start(f32[6912,256]{1,0:T(8,128)} %get-tuple-element.2445) | copy-start | bytes 21233668
  (2 other events, 2.5 us)
Sparse Core Ops, SparseCore 0:
  256.6 187.4 all-reduce.32
where the time goes:
time: 463 us; the launch traced here: 459 us
  waiting for transfers between devices  158 us (34%)
  other arithmetic  89.5 us (19%)
  local copies, waits for them, and re-layouts  81.1 us (18%)
  between operations  64.5 us (14%)
  starting transfers between devices  46.5 us (10%)
  matrix products  20 us (4%)
    psum x1, waiting for transfers between devices, on_device(): lax.psum((partial_one, partial_two), ('region', 'shard'))  151 us
    select_n x78, other arithmetic, framed(): pieces = jnp.where(present[position], pieces, jnp.zeros_like(pieces))  77.3 us
    ppermute x16, starting transfers between devices, shifted(): return lax.ppermute(array, axis, pairs)  46.4 us
    unnamed x154, local copies, waits for them, and re-layouts  32.6 us
    scatter x104, local copies, waits for them, and re-layouts, framed(): framed_grid = framed_grid.at[target_range(step_x), target_range(step_y),...  30.8 us
  transfers between devices with their start and end apart: 17, of which 3 were waited for; matrix products, arithmetic and copies ran while one was open for 28% of the time, Pallas kernels for 0%

commit v1 on v0

v1 whole, which is shorter than its diff:
```python
import jax
import jax.numpy as jnp
from jax import lax
from jax.experimental import pallas as pl
from jax.experimental.pallas import tpu as pltpu
from jax.sharding import PartitionSpec as P

AXES = ("region", "shard")
SIDES = (4, 4, 4, 2)
ROWS = 512
CH = 256
TAPS = 2304
FRAME_ROWS = 640
F32 = jnp.float32
BF16 = jnp.bfloat16
VMEM_LIMIT = 40 * 1024 * 1024
VMEM_SPEC = pl.BlockSpec(memory_space=pltpu.VMEM)
SMEM_SPEC = pl.BlockSpec(memory_space=pltpu.SMEM)
ANY_SPEC = pl.BlockSpec(memory_space=pl.ANY)


def coordinates(index):
    return {"x": index // 32, "z": (index // 8) % 4, "y": (index // 2) % 4, "core": index % 2}


def device_at(place):
    return place["x"] * 32 + place["z"] * 8 + place["y"] * 2 + place["core"]


def ring_send(array, axis_of_core, step):
    pairs = []
    for index in range(128):
        place = coordinates(index)
        axis = axis_of_core[place["core"]]
        place[axis] = (place[axis] + step) % 4
        pairs.append((index, device_at(place)))
    return lax.ppermute(array, AXES, pairs)


def swap(array):
    return lax.ppermute(array, AXES, [(index, index ^ 1) for index in range(128)])


def shifted(array, by):
    return lax.ppermute(array, AXES, [(i, i + by) for i in range(128) if 0 <= i + by < 128])


def build(stack, field, pick, out, first_row):
    z_of = lax.broadcasted_iota(jnp.int32, (10, 8, CH), 1)

    def plane(X, sx, xp):
        base = pl.multiple_of(xp * 64, 64)

        def column(sz):
            low = stack[field, pick(sx, 0, sz), pl.ds(base + 48, 16), :].astype(F32)[8:16]
            mid = stack[field, pick(sx, 1, sz), pl.ds(base, 64), :].astype(F32)
            high = stack[field, pick(sx, 2, sz), pl.ds(base, 16), :].astype(F32)[0:8]
            return jnp.concatenate([low, mid, high], axis=0).reshape(10, 8, CH)

        below, here, above = column(0), column(1), column(2)
        shifts = (
            pltpu.roll(jnp.where(z_of == 7, below, here), 1, 1),
            here,
            pltpu.roll(jnp.where(z_of == 0, above, here), 7, 1),
        )
        rows = pl.ds(pl.multiple_of(first_row + X * 64, 64), 64)
        for dz, grid in enumerate(shifts):
            even = grid.reshape(80, CH).astype(BF16)
            odd = grid[1:9].reshape(64, CH).astype(BF16)
            out[rows, (0 + dz) * CH : (1 + dz) * CH] = even[0:64]
            out[rows, (3 + dz) * CH : (4 + dz) * CH] = odd
            out[rows, (6 + dz) * CH : (7 + dz) * CH] = even[16:80]

    plane(0, 0, 7)

    @pl.loop(1, 9)
    def _(X):
        plane(X, 1, X - 1)

    plane(9, 2, 0)


def convolved(frame, weights):
    total = jnp.dot(frame[0:ROWS, :], weights[0], preferred_element_type=F32)
    total += jnp.dot(frame[64 : 64 + ROWS, :], weights[1], preferred_element_type=F32)
    total += jnp.dot(frame[128 : 128 + ROWS, :], weights[2], preferred_element_type=F32)
    return total


def load_stack(bricks, stack, sems):
    copies = [
        pltpu.make_async_copy(brick, stack.at[:, place], sems.at[place])
        for place, brick in enumerate(bricks)
    ]
    for copy in copies:
        copy.start()
    stack[:, 6] = jnp.zeros((2, ROWS, CH), BF16)
    for copy in copies:
        copy.wait()


def first_kernel(
    pick_ref, core_ref, own, before, after, mate, mate_before, mate_after, weight_one, turned_two,
    hidden_grad, frames, stack, spare, sems
):
    load_stack((own, before, after, mate, mate_before, mate_after), stack, sems)
    core = core_ref[0]

    def pick_of(which):
        return lambda sx, sy, sz: pick_ref[which, 9 * sx + 3 * sy + sz]

    build(stack, 1 - core, pick_of(0), frames, 0)
    build(stack, core, pick_of(0), spare, 0)
    build(stack, 1 - core, pick_of(1), frames, FRAME_ROWS)

    def finish(frame_in, frame_cot):
        pre_act = convolved(frame_in, weight_one)
        grad_hidden = convolved(frame_cot, turned_two)
        sig = 1.0 / (1.0 + jnp.exp(-pre_act))
        hidden_grad[0] = (pre_act * sig).astype(BF16)
        hidden_grad[1] = (grad_hidden * sig * (1.0 + pre_act * (1.0 - sig))).astype(BF16)

    @pl.when(core == 0)
    def _():
        finish(spare, frames)

    @pl.when(core != 0)
    def _():
        finish(frames, spare)


def second_kernel(
    pick_ref, own, before, after, mate, mate_before, mate_after, weight_two, turned_one,
    output, grad_input, stack, frame, sems
):
    load_stack((own, before, after, mate, mate_before, mate_after), stack, sems)

    def pick(sx, sy, sz):
        return pick_ref[0, 9 * sx + 3 * sy + sz]

    build(stack, 0, pick, frame, 0)
    output[...] = convolved(frame, weight_two).astype(BF16)
    build(stack, 1, pick, frame, 0)
    grad_input[...] = convolved(frame, turned_one).astype(BF16)


def gradient_kernel(place_ref, own, mate, frames, *rest):
    parts_a, parts_b, (turned, block) = rest[0:4], rest[4:8], rest[8:]
    core = place_ref[0]
    turned[0] = own[core].astype(F32).T.astype(BF16)
    turned[1] = mate[core].astype(F32).T.astype(BF16)

    def one(k, parts, axis_place, first):
        window = jnp.where(core == 0, 26 - k, k)
        row = pl.multiple_of((window // 9) * 64, 64)
        lane = pl.multiple_of((window % 9) * CH, CH)
        total = jnp.dot(turned[0], frames[pl.ds(row, ROWS), pl.ds(lane, CH)], preferred_element_type=F32)
        total += jnp.dot(
            turned[1], frames[pl.ds(FRAME_ROWS + row, ROWS), pl.ds(lane, CH)], preferred_element_type=F32
        )

        @pl.when(core == 0)
        def _():
            block[...] = total

        @pl.when(core != 0)
        def _():
            block[...] = total.T

        for step in range(4):
            chunk = pl.multiple_of(((axis_place + step) % 4) * 64, 64)
            parts[step][k - first] = block[pl.ds(chunk, 64), :].astype(BF16)

    @pl.loop(0, 18)
    def _(k):
        one(k, parts_a, place_ref[1], 0)

    @pl.loop(18, 27)
    def _(k):
        one(k, parts_b, place_ref[2], 18)


def scatter_kernel(place_ref, *refs):
    ins_a, ins_b, outs = refs[0:4], refs[4:8], refs[8:12]
    for step in range(4):
        rows = pl.ds(pl.multiple_of(((place_ref[3] + step) % 4) * 16, 16), 16)
        for ins, first, count in ((ins_a, 0, 18), (ins_b, 18, 9)):
            total = (ins[0][:, rows, :].astype(F32) + ins[2][:, rows, :].astype(F32)) + (
                ins[1][:, rows, :].astype(F32) + ins[3][:, rows, :].astype(F32)
            )
            outs[step][first : first + count] = total.astype(BF16)


def gather_kernel(place_ref, part0, part1, part2, part3, out_a, out_b):
    for step, part in enumerate((part0, part1, part2, part3)):
        rows = pl.ds(pl.multiple_of(((place_ref[3] + 4 - step) % 4) * 16, 16), 16)
        out_a[:, rows, :] = part[0:18]
        out_b[:, rows, :] = part[18:27]


def final_kernel(place_ref, *refs):
    own_a, own_b, mate_a, mate_b = refs[0:4], refs[4:8], refs[8:12], refs[12:16]
    grad_one, grad_two, sems = refs[16:]
    core = place_ref[0]

    def copies(dst, parts_a, parts_b, place_a, place_b, sem):
        made = []
        for step in range(4):
            rows_a = pl.ds(pl.multiple_of(((place_a + 4 - step) % 4) * 64, 64), 64)
            rows_b = pl.ds(pl.multiple_of(((place_b + 4 - step) % 4) * 64, 64), 64)
            made.append(pltpu.make_async_copy(parts_a[step], dst.at[0:18, rows_a, :], sem.at[step]))
            made.append(pltpu.make_async_copy(parts_b[step], dst.at[18:27, rows_b, :], sem.at[4 + step]))
        return made

    def run(one, two):
        made = copies(one[0], one[1], one[2], one[3], place_ref[2], sems.at[0])
        made += copies(two[0], two[1], two[2], two[3], place_ref[2], sems.at[1])
        for copy in made:
            copy.start()
        for copy in made:
            copy.wait()

    @pl.when(core == 0)
    def _():
        run((grad_two, own_a, own_b, place_ref[1]), (grad_one, mate_a, mate_b, place_ref[3]))

    @pl.when(core != 0)
    def _():
        run((grad_one, own_a, own_b, place_ref[1]), (grad_two, mate_a, mate_b, place_ref[3]))


def call(kernel, name, outs, in_specs, out_specs, scratch, flops, moved):
    return pl.pallas_call(
        kernel,
        name=name,
        out_shape=[jax.ShapeDtypeStruct(shape, BF16) for shape in outs],
        in_specs=in_specs,
        out_specs=out_specs,
        scratch_shapes=scratch,
        compiler_params=pltpu.CompilerParams(vmem_limit_bytes=VMEM_LIMIT),
        cost_estimate=pl.CostEstimate(flops=flops, bytes_accessed=moved, transcendentals=0),
    )


def on_device(
    features, cotangent, weight_one, weight_two, occupancy, neighbour_owner, neighbour_slot
):
    index = lax.axis_index(AXES)
    here = coordinates(index)
    core = here["core"]
    first_axis = jnp.where(core == 0, here["x"], here["z"])
    second_axis = jnp.where(core == 0, here["z"], here["x"])
    place = jnp.stack([core, first_axis, here["y"], second_axis]).astype(jnp.int32)

    graph = jnp.concatenate([occupancy.reshape(1, 1), neighbour_owner], axis=1)
    graph_mate = swap(graph)
    two = jnp.concatenate([graph, graph_mate], axis=0)
    first_brick = index - core - 2
    own_brick = jnp.stack([index, index ^ 1])[:, None]
    own_brick = jnp.where(two[:, 0:1] > 0, own_brick, -1)
    owners = jnp.concatenate([two[:, 1:14], own_brick, two[:, 14:27]], axis=1)
    rel = owners - first_brick
    same = (rel % 2) == core
    kind = jnp.where(rel // 2 == 1, 0, jnp.where(rel // 2 == 0, 1, 2))
    picks = jnp.where(owners >= 0, jnp.where(same, kind, kind + 3), 6).astype(jnp.int32)

    one = weight_one.reshape(3, TAPS, CH)
    two_w = weight_two.reshape(3, TAPS, CH)
    turned_one = jnp.transpose(weight_one[::-1], (0, 2, 1)).reshape(3, TAPS, CH)
    turned_two = jnp.transpose(weight_two[::-1], (0, 2, 1)).reshape(3, TAPS, CH)

    def halo(field):
        before, after = shifted(field, 2), shifted(field, -2)
        return field, before, after, swap(field), swap(before), swap(after)

    stack = pltpu.VMEM((2, 7, ROWS, CH), BF16)
    sems = pltpu.SemaphoreType.DMA((6,))
    fields = jnp.concatenate([features, cotangent], axis=0)
    hidden_grad, frames = call(
        first_kernel, "first_convs",
        [(2, ROWS, CH), (2 * FRAME_ROWS, TAPS)],
        [SMEM_SPEC, SMEM_SPEC] + [ANY_SPEC] * 6 + [VMEM_SPEC] * 2, [VMEM_SPEC] * 2,
        [stack, pltpu.VMEM((FRAME_ROWS, TAPS), BF16), sems],
        4 * ROWS * TAPS * 3 * CH, 16_000_000,
    )(picks, place, *halo(fields), one, turned_two)

    hidden_grad_mate = swap(hidden_grad)
    parts = call(
        gradient_kernel, "weight_grads",
        [(18, 64, CH)] * 4 + [(9, 64, CH)] * 4,
        [SMEM_SPEC] + [VMEM_SPEC] * 3, [VMEM_SPEC] * 8,
        [pltpu.VMEM((2, CH, ROWS), BF16), pltpu.VMEM((CH, CH), F32)],
        4 * ROWS * TAPS * 3 * CH, 10_000_000,
    )(place, hidden_grad, hidden_grad_mate, frames)
    parts_a, parts_b = parts[0:4], parts[4:8]

    axis_a, axis_b, axis_c = ("x", "z"), ("y", "y"), ("z", "x")
    sent_a = [parts_a[0]] + [ring_send(parts_a[d], axis_a, d) for d in (1, 2, 3)]
    sent_b = [parts_b[0]] + [ring_send(parts_b[d], axis_b, d) for d in (1, 2, 3)]
    quarter = call(
        scatter_kernel, "sum_and_split", [(27, 16, CH)] * 4,
        [SMEM_SPEC] + [VMEM_SPEC] * 8, [VMEM_SPEC] * 4, [], 4_000_000, 4_500_000,
    )(place, *sent_a, *sent_b)
    sent = [quarter[0]] + [ring_send(quarter[d], axis_c, d) for d in (1, 2, 3)]

    def added(arrays):
        wide = [array.astype(F32) for array in arrays]
        return (wide[0] + wide[2]) + (wide[1] + wide[3])

    small = added(sent).astype(BF16)
    small_a, small_b = small[0:18], small[18:27]
    all_a = added([small_a] + [ring_send(small_a, axis_b, d) for d in (1, 2, 3)])
    all_b = added([small_b] + [ring_send(small_b, axis_a, d) for d in (1, 2, 3)])
    scale = float(128 * ROWS) ** (-0.5)
    whole = (scale * jnp.concatenate([all_a, all_b], axis=0)).astype(BF16)

    back = [whole] + [ring_send(whole, axis_c, d) for d in (1, 2, 3)]
    wide_a, wide_b = call(
        gather_kernel, "gather_rows", [(18, 64, CH), (9, 64, CH)],
        [SMEM_SPEC] + [VMEM_SPEC] * 4, [VMEM_SPEC] * 2, [], 1000, 1_800_000,
    )(place, *back)
    final_a = [wide_a] + [ring_send(wide_a, axis_a, d) for d in (1, 2, 3)]
    final_b = [wide_b] + [ring_send(wide_b, axis_b, d) for d in (1, 2, 3)]
    mate_a = [swap(array) for array in final_a]
    mate_b = [swap(array) for array in final_b]
    grad_one, grad_two = call(
        final_kernel, "place_rows", [(27, CH, CH)] * 2,
        [SMEM_SPEC] + [VMEM_SPEC] * 16, [ANY_SPEC] * 2,
        [pltpu.SemaphoreType.DMA((2, 8))], 1000, 14_000_000,
    )(place, *final_a, *final_b, *mate_a, *mate_b)

    before, after = shifted(hidden_grad, 2), shifted(hidden_grad, -2)
    output, grad_input = call(
        second_kernel, "second_convs",
        [(ROWS, CH)] * 2,
        [SMEM_SPEC] + [ANY_SPEC] * 6 + [VMEM_SPEC] * 2, [VMEM_SPEC] * 2,
        [stack, pltpu.VMEM((FRAME_ROWS, TAPS), BF16), sems],
        4 * ROWS * TAPS * 3 * CH, 12_000_000,
    )(picks, hidden_grad, before, after, hidden_grad_mate, swap(before), swap(after), two_w, turned_one)

    return output[None], grad_input[None], grad_one, grad_two


def solution(mesh):
    by_brick = P(AXES, None, None)
    in_specs = (by_brick, by_brick, P(), P(), P(AXES), P(AXES, None), P(AXES, None))
    out_specs = (by_brick, by_brick, P(), P())
    return jax.shard_map(
        on_device, mesh=mesh, in_specs=in_specs, out_specs=out_specs, check_vma=False
    )
```

time: 463 us -> 192 us (0.41)
  waiting for transfers between devices: 158 us -> 33.2 us
  other arithmetic: 89.5 us -> 1.83 us
  between operations: 64.5 us -> 1.76 us
  local copies, waits for them, and re-layouts: 81.1 us -> 37.9 us
  Pallas kernels: 0 us -> 40.4 us
  starting transfers between devices: 46.5 us -> 75.7 us
  matrix products: 20 us -> 0 us
    psum x1 -> x0, waiting for transfers between devices: 151 us -> none  [on_device(): lax.psum((partial_one, partial_two), ('region', 'shard'))]
    select_n x81 -> x2, other arithmetic: 80.6 us -> 0.09 us  [the longest x1 0.09 us: on_device(): jnp.where(owners >= 0, jnp.where(same, kind, kind + 3), 6).astype(jnp.int32)]
    pallas_call x0 -> x6, Pallas kernels: none -> 40.4 us  [the longest x1 13.3 us: on_device(): call(gradient_kernel, 'weight_grads', [(18, 64, CH)] * 4 + [(9, 64, CH)]...]
    scatter x108 -> x0, local copies, waits for them, and re-layouts: 33.3 us -> none  [the longest x104 30.8 us: framed(): framed_grid = framed_grid.at[target_range(step_x), target_range(step_y),...]
    ppermute x16 -> x43, starting transfers between devices: 46.4 us -> 75.7 us  [the longest x24 48.9 us: ring_send(): return lax.ppermute(array, AXES, pairs)]
    ppermute x16 -> x43, waiting for transfers between devices: 6.98 us -> 33.2 us  [the longest x24 27.2 us: ring_send(): return lax.ppermute(array, AXES, pairs)]
    dot_general x6 -> x0, matrix products: 20 us -> none  [the longest x1 4.9 us: on_device(): lax.dot_general(columns(grid_hidden, every_offset), masked_cot.reshape(sl...]
    transpose x0 -> x4, local copies, waits for them, and re-layouts: none -> 18.1 us  [the longest x2 10 us: on_device(): turned_two = jnp.transpose(weight_two[::-1], (0, 2, 1)).reshape(3, TAPS, CH)]
  transfers between devices with their start and end apart: 17 -> 43, of which waited for: 3 -> 13; matrix products, arithmetic and copies ran while one was open for 28% -> 11% of each run, Pallas kernels for 0% -> 6%
where the time goes in v1:
time: 192 us; the launch traced here: 191 us
  starting transfers between devices  75.7 us (39%)
  Pallas kernels  40.4 us (21%)
  local copies, waits for them, and re-layouts  37.9 us (20%)
  waiting for transfers between devices  33.2 us (17%)
    ppermute x24, starting transfers between devices, ring_send(): return lax.ppermute(array, AXES, pairs)  48.9 us
    ppermute x24, waiting for transfers between devices, ring_send(): return lax.ppermute(array, AXES, pairs)  27.2 us
    unnamed x53, local copies, waits for them, and re-layouts  18 us
    ppermute x15, starting transfers between devices, swap(): lax.ppermute(array, AXES, [(index, index ^ 1) for index in range(128)])  17.9 us
    pallas_call x1, Pallas kernels, on_device(): call(gradient_kernel, 'weight_grads', [(18, 64, CH)] * 4 + [(9, 64, CH)]...  13.3 us
    transpose x2, local copies, waits for them, and re-layouts, on_device(): turned_two = jnp.transpose(weight_two[::-1], (0, 2, 1)).reshape(3, TAPS, CH)  10 us
    pallas_call x1, Pallas kernels, on_device(): call(second_kernel, 'second_convs', [(ROWS, CH)] * 2, [SMEM_SPEC] + [ANY_...  9.64 us
    pallas_call x1, Pallas kernels, on_device(): call(first_kernel, 'first_convs', [(2, ROWS, CH), (2 * FRAME_ROWS, TAPS)]...  9.52 us
  transfers between devices with their start and end apart: 43, of which 13 were waited for; matrix products, arithmetic and copies ran while one was open for 11% of the time, Pallas kernels for 6%

profile of v1, /device:TPU:1, one launch (start us, length us, event | category | flops | bytes accessed | tf_op | source)
XLA Modules:
  0.0 190.8 jit_solution(1218206783725862289)
XLA Ops:
  2.3 1.7 constant_dynamic-update-slice_fusion.own
  4.0 4.8 %collective-permute-start.1 = (bf16[2,512,256]{2,1,0:T(8,128)(2,1)}, bf16[2,512,256]{2,1,0:T(8,128)(2,1)}, u32[]{:S(2)}, u32[]{:S(2)}) collective-permute-start(bf16[2,512,256]{2,1,0:T(8,128)(2,1)} %constant_dynamic-update-slice_fusion.own), channel_id=1, source_target_pairs={{0,2},{1,3},{2,4},{3,5},{4,6},{5,7},{6,8},{7,9},{8,10},{9,11},{10,... | collective-permute-start | bytes 1572872 | tf_op jit(solution)/shard_map/ppermute | solution.py:45
  13.2 4.2 %reverse_bitcast_fusion.1 = bf16[27,256,256]{1,2,0:T(8,128)(2,1)} fusion(bf16[27,256,256]{2,1,0:T(8,128)(2,1)} %param.10), kind=kLoop, calls=%fused_computation.1 | loop fusion | bytes 7077888 | tf_op jit(solution)/shard_map/transpose | solution.py:270
  17.4 5.9 %copy.11 = bf16[27,256,256]{2,1,0:T(8,128)(2,1)} copy(bf16[27,256,256]{1,2,0:T(8,128)(2,1)} %reverse_bitcast_fusion.1) | data formatting | bytes 7077888 | tf_op jit(solution)/shard_map/transpose | solution.py:270
  27.1 2.0 %copy-done.2 = bf16[27,256,256]{2,1,0:T(8,128)(2,1)S(1)} copy-done((bf16[27,256,256]{2,1,0:T(8,128)(2,1)S(1)}, bf16[27,256,256]{2,1,0:T(8,128)(2,1)}, u32[]{:S(2)}) %copy-start.2) | copy-done | bytes 3538968
  29.1 9.5 %first_convs.1 = (bf16[2,512,256]{2,1,0:T(8,128)(2,1)S(1)}, bf16[1280,2304]{1,0:T(8,128)(2,1)}) custom-call(s32[2,27]{1,0:T(2,128)S(1)} %compare_select_fusion.3.pick_ref, s32[4]{0:T(128)S(1)} %pad_add_fusion.3.core_ref.place_ref, bf16[2,512,256]{2,1,0:T(8,128)(2,1)} %constant_dynamic-update-slice_fusion.own, ...), custom_call_target="tpu_custom_call" | custom-call | flops 3623878656 | bytes 16000000 | tf_op jit(solution)/shard_map/first_convs/pallas_call | solution.py:279
  40.6 2.9 %copy-done.24 = bf16[1280,2304]{1,0:T(8,128)(2,1)S(1)} copy-done((bf16[1280,2304]{1,0:T(8,128)(2,1)S(1)}, bf16[1280,2304]{1,0:T(8,128)(2,1)}, u32[]{:S(2)}) %copy-start.24) | copy-done | bytes 5898264
  43.5 13.3 %weight_grads.1 = (bf16[18,64,256]{2,1,0:T(8,128)(2,1)S(1)}, bf16[18,64,256]{2,1,0:T(8,128)(2,1)S(1)}, bf16[18,64,256]{2,1,0:T(8,128)(2,1)S(1)}, bf16[18,64,256]...) custom-call(s32[4]{0:T(128)S(1)} %pad_add_fusion.3.core_ref.place_re, ...), custom_call_target="tpu_custom_call" | custom-call | flops 3623878656 | bytes 10000000 | tf_op jit(solution)/shard_map/weight_grads/pallas_call | solution.py:288
  56.8 1.8 collective-permute-start.14
  58.6 1.8 collective-permute-start.11
  60.3 3.3 %collective-permute-start.12 = (bf16[18,64,256]{2,1,0:T(8,128)(2,1)S(1)}, bf16[18,64,256]{2,1,0:T(8,128)(2,1)S(1)}, u32[]{:S(2)}, u32[]{:S(2)}) collective-permute-start(bf16[18,64,256]{2,1,0:T(8,128)(2,1)S(1)} %get-tuple-element.30), channel_id=1, source_target_pairs={{0,64},{1,17},{2,66},{3,19},{4,68},{5,21},{6,70},{7,23},{8,72},{9,... | collective-permute-start | bytes 1769480 | tf_op jit(solution)/shard_map/ppermute | solution.py:37
  64.3 3.6 %collective-permute-start.15 = (bf16[9,64,256]{2,1,0:T(8,128)(2,1)S(1)}, bf16[9,64,256]{2,1,0:T(8,128)(2,1)S(1)}, u32[]{:S(2)}, u32[]{:S(2)}) collective-permute-start(bf16[9,64,256]{2,1,0:T(8,128)(2,1)S(1)} %get-tuple-element.34), channel_id=1, source_target_pairs={{0,4},{1,5},{2,6},{3,7},{4,0},{5,1},{6,2},{7,3},{8,12},{9,13},{10,... | collective-permute-start | bytes 884744 | tf_op jit(solution)/shard_map/ppermute | solution.py:37
  67.9 6.8 %collective-permute-done.15.refs_6_ = bf16[9,64,256]{2,1,0:T(8,128)(2,1)S(1)} collective-permute-done((bf16[9,64,256]{2,1,0:T(8,128)(2,1)S(1)}, bf16[9,64,256]{2,1,0:T(8,128)(2,1)S(1)}, u32[]{:S(2)}, u32[]{:S(2)}) %collective-permute-start.15) | collective-permute-done | bytes 294944 | tf_op jit(solution)/shard_map/ppermute | solution.py:37
  74.7 6.5 %collective-permute-done.16.refs_7_ = bf16[9,64,256]{2,1,0:T(8,128)(2,1)S(1)} collective-permute-done((bf16[9,64,256]{2,1,0:T(8,128)(2,1)S(1)}, bf16[9,64,256]{2,1,0:T(8,128)(2,1)S(1)}, u32[]{:S(2)}, u32[]{:S(2)}) %collective-permute-start.16) | collective-permute-done | bytes 294944 | tf_op jit(solution)/shard_map/ppermute | solution.py:37
  82.2 2.5 %collective-permute-start.19 = (bf16[27,16,256]{2,1,0:T(8,128)(2,1)S(1)}, bf16[27,16,256]{2,1,0:T(8,128)(2,1)S(1)}, u32[]{:S(2)}, u32[]{:S(2)}) collective-permute-start(bf16[27,16,256]{2,1,0:T(8,128)(2,1)S(1)} %get-tuple-element.39), channel_id=1, source_target_pairs={{0,24},{1,97},{2,26},{3,99},{4,28},{5,101},{6,30},{7,103},{8,0},{9... | collective-permute-start | bytes 663560 | tf_op jit(solution)/shard_map/ppermute | solution.py:37
  88.8 4.3 %collective-permute-done.18 = bf16[27,16,256]{2,1,0:T(8,128)(2,1)S(1)} collective-permute-done((bf16[27,16,256]{2,1,0:T(8,128)(2,1)S(1)}, bf16[27,16,256]{2,1,0:T(8,128)(2,1)S(1)}, u32[]{:S(2)}, u32[]{:S(2)}) %collective-permute-start.18) | collective-permute-done | bytes 221216 | tf_op jit(solution)/shard_map/ppermute | solution.py:37
  97.6 7.6 %collective-permute-start.9 = (bf16[2,512,256]{2,1,0:T(8,128)(2,1)S(1)}, bf16[2,512,256]{2,1,0:T(8,128)(2,1)S(1)}, u32[]{:S(2)}, u32[]{:S(2)}) collective-permute-start(bf16[2,512,256]{2,1,0:T(8,128)(2,1)S(1)} %collective-permute-done.6.before), channel_id=1, source_target_pairs={{0,1},{1,0},{2,3},{3,2},{4,5},{5,4},{6,7},{7,6},{8,9},{9,8},{10,11... | collective-permute-start | bytes 1572872 | tf_op jit(solution)/shard_map/ppermute | solution.py:41
  105.4 2.2 %collective-permute-start.22 = (bf16[18,16,256]{2,1,0:T(8,128)(2,1)S(1)}, bf16[18,16,256]{2,1,0:T(8,128)(2,1)S(1)}, u32[]{:S(2)}, u32[]{:S(2)}) collective-permute-start(bf16[18,16,256]{2,1,0:T(8,128)(2,1)S(1)} %slice.20), channel_id=1, source_target_pairs={{0,6},{1,7},{2,0},{3,1},{4,2},{5,3},{6,4},{7,5},{8,14},{9,15},{10,... | collective-permute-start | bytes 442376 | tf_op jit(solution)/shard_map/ppermute | solution.py:37
  110.1 2.9 %collective-permute-done.21 = bf16[18,16,256]{2,1,0:T(8,128)(2,1)S(1)} collective-permute-done((bf16[18,16,256]{2,1,0:T(8,128)(2,1)S(1)}, bf16[18,16,256]{2,1,0:T(8,128)(2,1)S(1)}, u32[]{:S(2)}, u32[]{:S(2)}) %collective-permute-start.21) | collective-permute-done | bytes 147488 | tf_op jit(solution)/shard_map/ppermute | solution.py:37
  114.8 4.2 %collective-permute-start.26 = (bf16[27,16,256]{2,1,0:T(8,128)(2,1)S(1)}, bf16[27,16,256]{2,1,0:T(8,128)(2,1)S(1)}, u32[]{:S(2)}, u32[]{:S(2)}) collective-permute-start(bf16[27,16,256]{2,1,0:T(8,128)(2,1)S(1)} %fusion.part0), channel_id=1, source_target_pairs={{0,8},{1,33},{2,10},{3,35},{4,12},{5,37},{6,14},{7,39},{8,16},{9,4... | collective-permute-start | bytes 663560 | tf_op jit(solution)/shard_map/ppermute | solution.py:37
  119.2 2.2 %collective-permute-start.28 = (bf16[27,16,256]{2,1,0:T(8,128)(2,1)S(1)}, bf16[27,16,256]{2,1,0:T(8,128)(2,1)S(1)}, u32[]{:S(2)}, u32[]{:S(2)}) collective-permute-start(bf16[27,16,256]{2,1,0:T(8,128)(2,1)S(1)} %fusion.part0), channel_id=1, source_target_pairs={{0,24},{1,97},{2,26},{3,99},{4,28},{5,101},{6,30},{7,103},{8,0},{9... | collective-permute-start | bytes 663560 | tf_op jit(solution)/shard_map/ppermute | solution.py:37
  121.8 3.4 %collective-permute-done.27.part2 = bf16[27,16,256]{2,1,0:T(8,128)(2,1)S(1)} collective-permute-done((bf16[27,16,256]{2,1,0:T(8,128)(2,1)S(1)}, bf16[27,16,256]{2,1,0:T(8,128)(2,1)S(1)}, u32[]{:S(2)}, u32[]{:S(2)}) %collective-permute-start.27) | collective-permute-done | bytes 221216 | tf_op jit(solution)/shard_map/ppermute | solution.py:37
  126.7 2.3 %collective-permute-start.33 = (bf16[9,64,256]{2,1,0:T(8,128)(2,1)S(1)}, bf16[9,64,256]{2,1,0:T(8,128)(2,1)S(1)}, u32[]{:S(2)}, u32[]{:S(2)}) collective-permute-start(bf16[9,64,256]{2,1,0:T(8,128)(2,1)S(1)} %get-tuple-element.41.refs_4_), channel_id=1, source_target_pairs={{0,4},{1,5},{2,6},{3,7},{4,0},{5,1},{6,2},{7,3},{8,12},{9,13},{10,... | collective-permute-start | bytes 884744 | tf_op jit(solution)/shard_map/ppermute | solution.py:37
  133.1 7.2 %collective-permute-start.30 = (bf16[18,64,256]{2,1,0:T(8,128)(2,1)}, bf16[18,64,256]{2,1,0:T(8,128)(2,1)}, u32[]{:S(2)}, u32[]{:S(2)}) collective-permute-start(bf16[18,64,256]{2,1,0:T(8,128)(2,1)} %get-tuple-element.40.refs_0_), channel_id=1, source_target_pairs={{0,64},{1,17},{2,66},{3,19},{4,68},{5,21},{6,70},{7,23},{8,72},{9,... | collective-permute-start | bytes 1769480 | tf_op jit(solution)/shard_map/ppermute | solution.py:37
  140.3 9.3 %collective-permute-start.31 = (bf16[18,64,256]{2,1,0:T(8,128)(2,1)}, bf16[18,64,256]{2,1,0:T(8,128)(2,1)}, u32[]{:S(2)}, u32[]{:S(2)}) collective-permute-start(bf16[18,64,256]{2,1,0:T(8,128)(2,1)} %get-tuple-element.40.refs_0_), channel_id=1, source_target_pairs={{0,96},{1,25},{2,98},{3,27},{4,100},{5,29},{6,102},{7,31},{8,104},... | collective-permute-start | bytes 1769480 | tf_op jit(solution)/shard_map/ppermute | solution.py:37
  152.9 3.8 %collective-permute-start.36 = (bf16[18,64,256]{2,1,0:T(8,128)(2,1)}, bf16[18,64,256]{2,1,0:T(8,128)(2,1)}, u32[]{:S(2)}, u32[]{:S(2)}) collective-permute-start(bf16[18,64,256]{2,1,0:T(8,128)(2,1)} %collective-permute-done.29.refs_1_), channel_id=1, source_target_pairs={{0,1},{1,0},{2,3},{3,2},{4,5},{5,4},{6,7},{7,6},{8,9},{9,8},{10,11... | collective-permute-start | bytes 1769480 | tf_op jit(solution)/shard_map/ppermute | solution.py:41
  156.7 1.7 collective-permute-start.38
  158.5 2.2 %reverse_bitcast_fusion = bf16[27,256,256]{1,2,0:T(8,128)(2,1)} fusion(bf16[27,256,256]{2,1,0:T(8,128)(2,1)S(1)} %copy-done), kind=kLoop, calls=%fused_computation | loop fusion | bytes 7077888 | tf_op jit(solution)/shard_map/transpose | solution.py:269
  160.7 5.9 %copy.12 = bf16[27,256,256]{2,1,0:T(8,128)(2,1)} copy(bf16[27,256,256]{1,2,0:T(8,128)(2,1)} %reverse_bitcast_fusion) | data formatting | bytes 7077888 | tf_op jit(solution)/shard_map/transpose | solution.py:269
  167.0 2.0 %copy-done.3 = bf16[27,256,256]{2,1,0:T(8,128)(2,1)S(1)} copy-done((bf16[27,256,256]{2,1,0:T(8,128)(2,1)S(1)}, bf16[27,256,256]{2,1,0:T(8,128)(2,1)}, u32[]{:S(2)}) %copy-start.3) | copy-done | bytes 3538968
  175.3 9.6 %second_convs.1 = (bf16[512,256]{1,0:T(8,128)(2,1)}, bf16[512,256]{1,0:T(8,128)(2,1)}) custom-call(s32[2,27]{1,0:T(2,128)S(1)} %compare_select_fusion.3.pick_ref, bf16[2,512,256]{2,1,0:T(8,128)(2,1)S(1)} %copy-done.13, bf16[2,512,256]{2,1,0:T(8,128)(2,1)S(1)} %copy-done.17, bf16[2,512,256]{2,1,0:T(8,128)(2,1)S(1)} %copy-done.19, ...), custom_call_target="tpu_custom_call" | custom-call | flops 3623878656 | bytes 12000000 | tf_op jit(solution)/shard_map/second_convs/pallas_call | solution.py:333
  185.0 5.5 %place_rows.1 = (bf16[27,256,256]{2,1,0:T(8,128)(2,1)}, bf16[27,256,256]{2,1,0:T(8,128)(2,1)}) custom-call(s32[4]{0:T(128)S(1)} %pad_add_fusion.3.core_ref.place_ref, bf16[18,64,256]{2,1,0:T(8,128)(2,1)} %get-tuple-element.40.refs_0_, bf16[18,64,256]{2,1,0:T(8,128)(2,1)} %collective-permute-done.29.refs_1_, ...), custom_call_target="tpu_custom_call" | custom-call | flops 1000 | bytes 14000000 | tf_op jit(solution)/shard_map/place_rows/pallas_call | solution.py:326
  (132 shorter events, 42.2 us)
Async XLA Ops:
  4.0 19.4 %collective-permute-start.1 = (bf16[2,512,256]{2,1,0:T(8,128)(2,1)}, bf16[2,512,256]{2,1,0:T(8,128)(2,1)}, u32[]{:S(2)}, u32[]{:S(2)}) collective-permute-start(bf16[2,512,256]{2,1,0:T(8,128)(2,1)} %constant_dynamic-update-slice_fusion.own), channel_id=1, source_target_pairs={{0,2},{1,3},{2,4},{3,5},{4,6},{5,7},{6,8},{7,9},{8,10},{9,11},{10,... | collective-permute-start | bytes 1572872 | tf_op jit(solution)/shard_map/ppermute | solution.py:45
  8.8 15.1 %collective-permute-start.2 = (bf16[2,512,256]{2,1,0:T(8,128)(2,1)}, bf16[2,512,256]{2,1,0:T(8,128)(2,1)}, u32[]{:S(2)}, u32[]{:S(2)}) collective-permute-start(bf16[2,512,256]{2,1,0:T(8,128)(2,1)} %constant_dynamic-update-slice_fusion.own), channel_id=1, source_target_pairs={{2,0},{3,1},{4,2},{5,3},{6,4},{7,5},{8,6},{9,7},{10,8},{11,9},{12,... | collective-permute-start | bytes 1572872 | tf_op jit(solution)/shard_map/ppermute | solution.py:45
  10.1 15.4 %collective-permute-start.3 = (bf16[2,512,256]{2,1,0:T(8,128)(2,1)}, bf16[2,512,256]{2,1,0:T(8,128)(2,1)}, u32[]{:S(2)}, u32[]{:S(2)}) collective-permute-start(bf16[2,512,256]{2,1,0:T(8,128)(2,1)} %constant_dynamic-update-slice_fusion.own), channel_id=1, source_target_pairs={{0,1},{1,0},{2,3},{3,2},{4,5},{5,4},{6,7},{7,6},{8,9},{9,8},{10,11... | collective-permute-start | bytes 1572872 | tf_op jit(solution)/shard_map/ppermute | solution.py:41
  13.0 10.3 %collective-permute-start = (s32[1,27]{1,0:T(1,128)}, s32[1,27]{1,0:T(1,128)S(1)}, u32[]{:S(2)}, u32[]{:S(2)}) collective-permute-start(s32[1,27]{1,0:T(1,128)} %pad_add_fusion.2), channel_id=1, source_target_pairs={{0,1},{1,0},{2,3},{3,2},{4,5},{5,4},{6,7},{7,6},{8,9},{9,8},{10,11... | collective-permute-start | bytes 332 | tf_op jit(solution)/shard_map/ppermute | solution.py:41
  56.8 11.2 %collective-permute-start.14 = (bf16[9,64,256]{2,1,0:T(8,128)(2,1)S(1)}, bf16[9,64,256]{2,1,0:T(8,128)(2,1)S(1)}, u32[]{:S(2)}, u32[]{:S(2)}) collective-permute-start(bf16[9,64,256]{2,1,0:T(8,128)(2,1)S(1)} %get-tuple-element.33), channel_id=1, source_target_pairs={{0,2},{1,3},{2,4},{3,5},{4,6},{5,7},{6,0},{7,1},{8,10},{9,11},{10,... | collective-permute-start | bytes 884744 | tf_op jit(solution)/shard_map/ppermute | solution.py:37
  58.6 22.7 %collective-permute-start.11 = (bf16[18,64,256]{2,1,0:T(8,128)(2,1)S(1)}, bf16[18,64,256]{2,1,0:T(8,128)(2,1)S(1)}, u32[]{:S(2)}, u32[]{:S(2)}) collective-permute-start(bf16[18,64,256]{2,1,0:T(8,128)(2,1)S(1)} %get-tuple-element.29), channel_id=1, source_target_pairs={{0,32},{1,9},{2,34},{3,11},{4,36},{5,13},{6,38},{7,15},{8,40},{9,1... | collective-permute-start | bytes 1769480 | tf_op jit(solution)/shard_map/ppermute | solution.py:37
  60.3 20.9 %collective-permute-start.12 = (bf16[18,64,256]{2,1,0:T(8,128)(2,1)S(1)}, bf16[18,64,256]{2,1,0:T(8,128)(2,1)S(1)}, u32[]{:S(2)}, u32[]{:S(2)}) collective-permute-start(bf16[18,64,256]{2,1,0:T(8,128)(2,1)S(1)} %get-tuple-element.30), channel_id=1, source_target_pairs={{0,64},{1,17},{2,66},{3,19},{4,68},{5,21},{6,70},{7,23},{8,72},{9,... | collective-permute-start | bytes 1769480 | tf_op jit(solution)/shard_map/ppermute | solution.py:37
  63.6 17.6 %collective-permute-start.13 = (bf16[18,64,256]{2,1,0:T(8,128)(2,1)S(1)}, bf16[18,64,256]{2,1,0:T(8,128)(2,1)S(1)}, u32[]{:S(2)}, u32[]{:S(2)}) collective-permute-start(bf16[18,64,256]{2,1,0:T(8,128)(2,1)S(1)} %get-tuple-element.31), channel_id=1, source_target_pairs={{0,96},{1,25},{2,98},{3,27},{4,100},{5,29},{6,102},{7,31},{8,104},... | collective-permute-start | bytes 1769480 | tf_op jit(solution)/shard_map/ppermute | solution.py:37
  64.3 10.4 %collective-permute-start.15 = (bf16[9,64,256]{2,1,0:T(8,128)(2,1)S(1)}, bf16[9,64,256]{2,1,0:T(8,128)(2,1)S(1)}, u32[]{:S(2)}, u32[]{:S(2)}) collective-permute-start(bf16[9,64,256]{2,1,0:T(8,128)(2,1)S(1)} %get-tuple-element.34), channel_id=1, source_target_pairs={{0,4},{1,5},{2,6},{3,7},{4,0},{5,1},{6,2},{7,3},{8,12},{9,13},{10,... | collective-permute-start | bytes 884744 | tf_op jit(solution)/shard_map/ppermute | solution.py:37
  67.9 13.3 %collective-permute-start.16 = (bf16[9,64,256]{2,1,0:T(8,128)(2,1)S(1)}, bf16[9,64,256]{2,1,0:T(8,128)(2,1)S(1)}, u32[]{:S(2)}, u32[]{:S(2)}) collective-permute-start(bf16[9,64,256]{2,1,0:T(8,128)(2,1)S(1)} %get-tuple-element.35), channel_id=1, source_target_pairs={{0,6},{1,7},{2,0},{3,1},{4,2},{5,3},{6,4},{7,5},{8,14},{9,15},{10,... | collective-permute-start | bytes 884744 | tf_op jit(solution)/shard_map/ppermute | solution.py:37
  84.7 8.4 %collective-permute-start.18 = (bf16[27,16,256]{2,1,0:T(8,128)(2,1)S(1)}, bf16[27,16,256]{2,1,0:T(8,128)(2,1)S(1)}, u32[]{:S(2)}, u32[]{:S(2)}) collective-permute-start(bf16[27,16,256]{2,1,0:T(8,128)(2,1)S(1)} %get-tuple-element.38), channel_id=1, source_target_pairs={{0,8},{1,33},{2,10},{3,35},{4,12},{5,37},{6,14},{7,39},{8,16},{9,4... | collective-permute-start | bytes 663560 | tf_op jit(solution)/shard_map/ppermute | solution.py:37
  84.8 8.4 %collective-permute-start.17 = (bf16[27,16,256]{2,1,0:T(8,128)(2,1)S(1)}, bf16[27,16,256]{2,1,0:T(8,128)(2,1)S(1)}, u32[]{:S(2)}, u32[]{:S(2)}) collective-permute-start(bf16[27,16,256]{2,1,0:T(8,128)(2,1)S(1)} %get-tuple-element.37), channel_id=1, source_target_pairs={{0,16},{1,65},{2,18},{3,67},{4,20},{5,69},{6,22},{7,71},{8,24},{9,... | collective-permute-start | bytes 663560 | tf_op jit(solution)/shard_map/ppermute | solution.py:37
  86.0 11.6 %collective-permute-start.6 = (bf16[2,512,256]{2,1,0:T(8,128)(2,1)S(1)}, bf16[2,512,256]{2,1,0:T(8,128)(2,1)S(1)}, u32[]{:S(2)}, u32[]{:S(2)}) collective-permute-start(bf16[2,512,256]{2,1,0:T(8,128)(2,1)S(1)} %get-tuple-element.24.own), channel_id=1, source_target_pairs={{0,2},{1,3},{2,4},{3,5},{4,6},{5,7},{6,8},{7,9},{8,10},{9,11},{10,... | collective-permute-start | bytes 1572872 | tf_op jit(solution)/shard_map/ppermute | solution.py:45
  87.3 17.9 %collective-permute-start.7 = (bf16[2,512,256]{2,1,0:T(8,128)(2,1)S(1)}, bf16[2,512,256]{2,1,0:T(8,128)(2,1)S(1)}, u32[]{:S(2)}, u32[]{:S(2)}) collective-permute-start(bf16[2,512,256]{2,1,0:T(8,128)(2,1)S(1)} %get-tuple-element.24.own), channel_id=1, source_target_pairs={{2,0},{3,1},{4,2},{5,3},{6,4},{7,5},{8,6},{9,7},{10,8},{11,9},{12,... | collective-permute-start | bytes 1572872 | tf_op jit(solution)/shard_map/ppermute | solution.py:45
  93.3 12.1 %collective-permute-start.25 = (bf16[9,16,256]{2,1,0:T(8,128)(2,1)S(1)}, bf16[9,16,256]{2,1,0:T(8,128)(2,1)S(1)}, u32[]{:S(2)}, u32[]{:S(2)}) collective-permute-start(bf16[9,16,256]{2,1,0:T(8,128)(2,1)S(1)} %slice.21), channel_id=1, source_target_pairs={{0,96},{1,25},{2,98},{3,27},{4,100},{5,29},{6,102},{7,31},{8,104},... | collective-permute-start | bytes 221192 | tf_op jit(solution)/shard_map/ppermute | solution.py:37
  94.7 12.9 %collective-permute-start.24 = (bf16[9,16,256]{2,1,0:T(8,128)(2,1)S(1)}, bf16[9,16,256]{2,1,0:T(8,128)(2,1)S(1)}, u32[]{:S(2)}, u32[]{:S(2)}) collective-permute-start(bf16[9,16,256]{2,1,0:T(8,128)(2,1)S(1)} %slice.21), channel_id=1, source_target_pairs={{0,32},{1,9},{2,34},{3,11},{4,36},{5,13},{6,38},{7,15},{8,40},{9,1... | collective-permute-start | bytes 221192 | tf_op jit(solution)/shard_map/ppermute | solution.py:37
  94.8 12.8 %collective-permute-start.23 = (bf16[9,16,256]{2,1,0:T(8,128)(2,1)S(1)}, bf16[9,16,256]{2,1,0:T(8,128)(2,1)S(1)}, u32[]{:S(2)}, u32[]{:S(2)}) collective-permute-start(bf16[9,16,256]{2,1,0:T(8,128)(2,1)S(1)} %slice.21), channel_id=1, source_target_pairs={{0,64},{1,17},{2,66},{3,19},{4,68},{5,21},{6,70},{7,23},{8,72},{9,... | collective-permute-start | bytes 221192 | tf_op jit(solution)/shard_map/ppermute | solution.py:37
  97.6 32.5 %collective-permute-start.9 = (bf16[2,512,256]{2,1,0:T(8,128)(2,1)S(1)}, bf16[2,512,256]{2,1,0:T(8,128)(2,1)S(1)}, u32[]{:S(2)}, u32[]{:S(2)}) collective-permute-start(bf16[2,512,256]{2,1,0:T(8,128)(2,1)S(1)} %collective-permute-done.6.before), channel_id=1, source_target_pairs={{0,1},{1,0},{2,3},{3,2},{4,5},{5,4},{6,7},{7,6},{8,9},{9,8},{10,11... | collective-permute-start | bytes 1572872 | tf_op jit(solution)/shard_map/ppermute | solution.py:41
  105.2 27.0 %collective-permute-start.10 = (bf16[2,512,256]{2,1,0:T(8,128)(2,1)S(1)}, bf16[2,512,256]{2,1,0:T(8,128)(2,1)S(1)}, u32[]{:S(2)}, u32[]{:S(2)}) collective-permute-start(bf16[2,512,256]{2,1,0:T(8,128)(2,1)S(1)} %collective-permute-done.7.after), channel_id=1, source_target_pairs={{0,1},{1,0},{2,3},{3,2},{4,5},{5,4},{6,7},{7,6},{8,9},{9,8},{10,11... | collective-permute-start | bytes 1572872 | tf_op jit(solution)/shard_map/ppermute | solution.py:41
  126.7 13.6 %collective-permute-start.32 = (bf16[9,64,256]{2,1,0:T(8,128)(2,1)S(1)}, bf16[9,64,256]{2,1,0:T(8,128)(2,1)}, u32[]{:S(2)}, u32[]{:S(2)}) collective-permute-start(bf16[9,64,256]{2,1,0:T(8,128)(2,1)S(1)} %get-tuple-element.41.refs_4_), channel_id=1, source_target_pairs={{0,2},{1,3},{2,4},{3,5},{4,6},{5,7},{6,0},{7,1},{8,10},{9,11},{10,... | collective-permute-start | bytes 884744 | tf_op jit(solution)/shard_map/ppermute | solution.py:37
  126.7 22.9 %collective-permute-start.33 = (bf16[9,64,256]{2,1,0:T(8,128)(2,1)S(1)}, bf16[9,64,256]{2,1,0:T(8,128)(2,1)S(1)}, u32[]{:S(2)}, u32[]{:S(2)}) collective-permute-start(bf16[9,64,256]{2,1,0:T(8,128)(2,1)S(1)} %get-tuple-element.41.refs_4_), channel_id=1, source_target_pairs={{0,4},{1,5},{2,6},{3,7},{4,0},{5,1},{6,2},{7,3},{8,12},{9,13},{10,... | collective-permute-start | bytes 884744 | tf_op jit(solution)/shard_map/ppermute | solution.py:37
  128.9 20.6 %collective-permute-start.34 = (bf16[9,64,256]{2,1,0:T(8,128)(2,1)S(1)}, bf16[9,64,256]{2,1,0:T(8,128)(2,1)S(1)}, u32[]{:S(2)}, u32[]{:S(2)}) collective-permute-start(bf16[9,64,256]{2,1,0:T(8,128)(2,1)S(1)} %get-tuple-element.41.refs_4_), channel_id=1, source_target_pairs={{0,6},{1,7},{2,0},{3,1},{4,2},{5,3},{6,4},{7,5},{8,14},{9,15},{10,... | collective-permute-start | bytes 884744 | tf_op jit(solution)/shard_map/ppermute | solution.py:37
  130.9 21.9 %collective-permute-start.29 = (bf16[18,64,256]{2,1,0:T(8,128)(2,1)}, bf16[18,64,256]{2,1,0:T(8,128)(2,1)}, u32[]{:S(2)}, u32[]{:S(2)}) collective-permute-start(bf16[18,64,256]{2,1,0:T(8,128)(2,1)} %get-tuple-element.40.refs_0_), channel_id=1, source_target_pairs={{0,32},{1,9},{2,34},{3,11},{4,36},{5,13},{6,38},{7,15},{8,40},{9,1... | collective-permute-start | bytes 1769480 | tf_op jit(solution)/shard_map/ppermute | solution.py:37
  133.1 23.7 %collective-permute-start.30 = (bf16[18,64,256]{2,1,0:T(8,128)(2,1)}, bf16[18,64,256]{2,1,0:T(8,128)(2,1)}, u32[]{:S(2)}, u32[]{:S(2)}) collective-permute-start(bf16[18,64,256]{2,1,0:T(8,128)(2,1)} %get-tuple-element.40.refs_0_), channel_id=1, source_target_pairs={{0,64},{1,17},{2,66},{3,19},{4,68},{5,21},{6,70},{7,23},{8,72},{9,... | collective-permute-start | bytes 1769480 | tf_op jit(solution)/shard_map/ppermute | solution.py:37
  140.3 16.5 %collective-permute-start.31 = (bf16[18,64,256]{2,1,0:T(8,128)(2,1)}, bf16[18,64,256]{2,1,0:T(8,128)(2,1)}, u32[]{:S(2)}, u32[]{:S(2)}) collective-permute-start(bf16[18,64,256]{2,1,0:T(8,128)(2,1)} %get-tuple-element.40.refs_0_), channel_id=1, source_target_pairs={{0,96},{1,25},{2,98},{3,27},{4,100},{5,29},{6,102},{7,31},{8,104},... | collective-permute-start | bytes 1769480 | tf_op jit(solution)/shard_map/ppermute | solution.py:37
  149.6 16.9 %collective-permute-start.35 = (bf16[18,64,256]{2,1,0:T(8,128)(2,1)}, bf16[18,64,256]{2,1,0:T(8,128)(2,1)}, u32[]{:S(2)}, u32[]{:S(2)}) collective-permute-start(bf16[18,64,256]{2,1,0:T(8,128)(2,1)} %get-tuple-element.40.refs_0_), channel_id=1, source_target_pairs={{0,1},{1,0},{2,3},{3,2},{4,5},{5,4},{6,7},{7,6},{8,9},{9,8},{10,11... | collective-permute-start | bytes 1769480 | tf_op jit(solution)/shard_map/ppermute | solution.py:41
  152.7 13.8 %collective-permute-start.40 = (bf16[9,64,256]{2,1,0:T(8,128)(2,1)}, bf16[9,64,256]{2,1,0:T(8,128)(2,1)}, u32[]{:S(2)}, u32[]{:S(2)}) collective-permute-start(bf16[9,64,256]{2,1,0:T(8,128)(2,1)} %collective-permute-done.32.refs_5_), channel_id=1, source_target_pairs={{0,1},{1,0},{2,3},{3,2},{4,5},{5,4},{6,7},{7,6},{8,9},{9,8},{10,11... | collective-permute-start | bytes 884744 | tf_op jit(solution)/shard_map/ppermute | solution.py:41
  152.9 32.1 %collective-permute-start.36 = (bf16[18,64,256]{2,1,0:T(8,128)(2,1)}, bf16[18,64,256]{2,1,0:T(8,128)(2,1)}, u32[]{:S(2)}, u32[]{:S(2)}) collective-permute-start(bf16[18,64,256]{2,1,0:T(8,128)(2,1)} %collective-permute-done.29.refs_1_), channel_id=1, source_target_pairs={{0,1},{1,0},{2,3},{3,2},{4,5},{5,4},{6,7},{7,6},{8,9},{9,8},{10,11... | collective-permute-start | bytes 1769480 | tf_op jit(solution)/shard_map/ppermute | solution.py:41
  156.7 28.3 %collective-permute-start.37 = (bf16[18,64,256]{2,1,0:T(8,128)(2,1)}, bf16[18,64,256]{2,1,0:T(8,128)(2,1)}, u32[]{:S(2)}, u32[]{:S(2)}) collective-permute-start(bf16[18,64,256]{2,1,0:T(8,128)(2,1)} %collective-permute-done.30.refs_2_), channel_id=1, source_target_pairs={{0,1},{1,0},{2,3},{3,2},{4,5},{5,4},{6,7},{7,6},{8,9},{9,8},{10,11... | collective-permute-start | bytes 1769480 | tf_op jit(solution)/shard_map/ppermute | solution.py:41
  156.7 28.3 %collective-permute-start.38 = (bf16[18,64,256]{2,1,0:T(8,128)(2,1)}, bf16[18,64,256]{2,1,0:T(8,128)(2,1)}, u32[]{:S(2)}, u32[]{:S(2)}) collective-permute-start(bf16[18,64,256]{2,1,0:T(8,128)(2,1)} %collective-permute-done.31.refs_3_), channel_id=1, source_target_pairs={{0,1},{1,0},{2,3},{3,2},{4,5},{5,4},{6,7},{7,6},{8,9},{9,8},{10,11... | collective-permute-start | bytes 1769480 | tf_op jit(solution)/shard_map/ppermute | solution.py:41
  166.5 18.4 %collective-permute-start.41 = (bf16[9,64,256]{2,1,0:T(8,128)(2,1)}, bf16[9,64,256]{2,1,0:T(8,128)(2,1)S(1)}, u32[]{:S(2)}, u32[]{:S(2)}) collective-permute-start(bf16[9,64,256]{2,1,0:T(8,128)(2,1)} %copy-done.6), channel_id=1, source_target_pairs={{0,1},{1,0},{2,3},{3,2},{4,5},{5,4},{6,7},{7,6},{8,9},{9,8},{10,11... | collective-permute-start | bytes 884744 | tf_op jit(solution)/shard_map/ppermute | solution.py:41
  166.5 18.4 %collective-permute-start.42 = (bf16[9,64,256]{2,1,0:T(8,128)(2,1)}, bf16[9,64,256]{2,1,0:T(8,128)(2,1)S(1)}, u32[]{:S(2)}, u32[]{:S(2)}) collective-permute-start(bf16[9,64,256]{2,1,0:T(8,128)(2,1)} %copy-done.8), channel_id=1, source_target_pairs={{0,1},{1,0},{2,3},{3,2},{4,5},{5,4},{6,7},{7,6},{8,9},{9,8},{10,11... | collective-permute-start | bytes 884744 | tf_op jit(solution)/shard_map/ppermute | solution.py:41
  (37 other events, 314.7 us)

commit v2 on v1

v2 whole, which is shorter than its diff:
```python
import jax
import jax.numpy as jnp
from jax import lax
from jax.experimental import pallas as pl
from jax.experimental.pallas import tpu as pltpu
from jax.sharding import PartitionSpec as P

AXES = ("region", "shard")
SIDES = (4, 4, 4, 2)
ROWS = 512
CH = 256
TAPS = 2304
FRAME_ROWS = 640
F32 = jnp.float32
BF16 = jnp.bfloat16
VMEM_SPEC = pl.BlockSpec(memory_space=pltpu.VMEM)
SMEM_SPEC = pl.BlockSpec(memory_space=pltpu.SMEM)
ANY_SPEC = pl.BlockSpec(memory_space=pl.ANY)
HBM_SPEC = pl.BlockSpec(memory_space=pltpu.HBM)


def coordinates(index):
    return {"x": index // 32, "z": (index // 8) % 4, "y": (index // 2) % 4, "core": index % 2}


def device_at(place):
    return place["x"] * 32 + place["z"] * 8 + place["y"] * 2 + place["core"]


def ring_send(array, axis_of_core, step):
    pairs = []
    for index in range(128):
        place = coordinates(index)
        axis = axis_of_core[place["core"]]
        place[axis] = (place[axis] + step) % 4
        pairs.append((index, device_at(place)))
    return lax.ppermute(array, AXES, pairs)


def swap(array):
    return lax.ppermute(array, AXES, [(index, index ^ 1) for index in range(128)])


def shifted(array, by):
    return lax.ppermute(array, AXES, [(i, i + by) for i in range(128) if 0 <= i + by < 128])


def build(stack, field, pick, out, first_row):
    z_of = lax.broadcasted_iota(jnp.int32, (10, 8, CH), 1)

    def plane(X, sx, xp):
        base = pl.multiple_of(xp * 64, 64)

        def column(sz):
            low = stack[field, pick(sx, 0, sz), pl.ds(base + 48, 16), :].astype(F32)[8:16]
            mid = stack[field, pick(sx, 1, sz), pl.ds(base, 64), :].astype(F32)
            high = stack[field, pick(sx, 2, sz), pl.ds(base, 16), :].astype(F32)[0:8]
            return jnp.concatenate([low, mid, high], axis=0).reshape(10, 8, CH)

        below, here, above = column(0), column(1), column(2)
        shifts = (
            pltpu.roll(jnp.where(z_of == 7, below, here), 1, 1),
            here,
            pltpu.roll(jnp.where(z_of == 0, above, here), 7, 1),
        )
        rows = pl.ds(pl.multiple_of(first_row + X * 64, 64), 64)
        for dz, grid in enumerate(shifts):
            even = grid.reshape(80, CH).astype(BF16)
            odd = grid[1:9].reshape(64, CH).astype(BF16)
            out[rows, (0 + dz) * CH : (1 + dz) * CH] = even[0:64]
            out[rows, (3 + dz) * CH : (4 + dz) * CH] = odd
            out[rows, (6 + dz) * CH : (7 + dz) * CH] = even[16:80]

    plane(0, 0, 7)

    @pl.loop(1, 9)
    def _(X):
        plane(X, 1, X - 1)

    plane(9, 2, 0)


def convolved(frame, weights):
    total = None
    for plane in range(3):
        term = jnp.dot(
            frame[64 * plane : 64 * plane + ROWS, :],
            weights[9 * plane : 9 * plane + 9].reshape(TAPS, CH),
            preferred_element_type=F32,
        )
        total = term if total is None else total + term
    return total


def convolved_turned(frame, weights):
    total = None
    for k in range(27):
        window = frame[64 * (k // 9) : 64 * (k // 9) + ROWS, (k % 9) * CH : (k % 9 + 1) * CH]
        term = lax.dot_general(
            window, weights[26 - k], (((1,), (1,)), ((), ())), preferred_element_type=F32
        )
        total = term if total is None else total + term
    return total


def picker(pick_ref, which):
    return lambda sx, sy, sz: pick_ref[which, 9 * sx + 3 * sy + sz]


def loaded(bricks, weights, stack, held, sems):
    copies = [
        pltpu.make_async_copy(brick, stack.at[:, place], sems.at[place])
        for place, brick in enumerate(bricks)
    ]
    loads = [
        pltpu.make_async_copy(weight, held.at[place], sems.at[6 + place])
        for place, weight in enumerate(weights)
    ]
    for copy in copies + loads:
        copy.start()
    stack[:, 6] = jnp.zeros((2, ROWS, CH), BF16)
    for copy in copies:
        copy.wait()
    return loads


def order_kernel(passed, waited_for, passed_out):
    pass


def pack_kernel(features, cotangent, out, sems):
    copies = [
        pltpu.make_async_copy(field.at[0], out.at[place], sems.at[place])
        for place, field in enumerate((features, cotangent))
    ]
    for copy in copies:
        copy.start()
    for copy in copies:
        copy.wait()


def frames_kernel(
    pick_ref, place_ref, own, before, after, mate, mate_before, mate_after, frames, spare, stack, sems
):
    loaded((own, before, after, mate, mate_before, mate_after), (), stack, None, sems)
    core = place_ref[0]
    build(stack, 1 - core, picker(pick_ref, 0), frames, 0)
    build(stack, core, picker(pick_ref, 0), spare, 0)
    build(stack, 1 - core, picker(pick_ref, 1), frames, FRAME_ROWS)


def hidden_kernel(place_ref, frames, spare, weight_one, pre_act):
    @pl.when(place_ref[0] == 0)
    def _():
        pre_act[...] = convolved(spare, weight_one)

    @pl.when(place_ref[0] != 0)
    def _():
        pre_act[...] = convolved(frames, weight_one)


def grad_kernel(place_ref, frames, spare, weight_two, pre_act_ref, both):
    def finish(frame):
        grad_hidden = convolved_turned(frame, weight_two)
        pre_act = pre_act_ref[...]
        sig = 1.0 / (1.0 + jnp.exp(-pre_act))
        both[0] = (pre_act / (1.0 + jnp.exp(-pre_act))).astype(BF16)
        both[1] = (grad_hidden * sig * (1.0 + pre_act * (1.0 - sig))).astype(BF16)

    @pl.when(place_ref[0] == 0)
    def _():
        finish(frames)

    @pl.when(place_ref[0] != 0)
    def _():
        finish(spare)


def outer_kernel(
    pick_ref, own, before, after, mate, mate_before, mate_after, weight_two, weight_one, passed,
    output, grad_input, passed_out, frame, stack, held, sems
):
    bricks = (own, before, after, mate, mate_before, mate_after)
    loads = loaded(bricks, (weight_two, weight_one), stack, held, sems)
    build(stack, 0, picker(pick_ref, 0), frame, 0)
    loads[0].wait()
    output[0] = convolved(frame, held.at[0]).astype(BF16)
    build(stack, 1, picker(pick_ref, 0), frame, 0)
    loads[1].wait()
    grad_input[0] = convolved_turned(frame, held.at[1]).astype(BF16)


def gradient_kernel(place_ref, both, both_mate, frames, passed, *rest):
    parts, (turned, blocks) = rest[0:4], rest[5:]
    core = place_ref[0]
    turned[0] = both[core].T
    turned[1] = both_mate[core].T

    def run(core):
        for plane in range(3):
            for third in range(3):
                lanes = slice(third * 3 * CH, (third + 1) * 3 * CH)
                row = 64 * plane
                total = jnp.dot(turned[0], frames[row : row + ROWS, lanes], preferred_element_type=F32)
                row += FRAME_ROWS
                total += jnp.dot(turned[1], frames[row : row + ROWS, lanes], preferred_element_type=F32)
                for tap in range(3):
                    k = 9 * plane + 3 * third + tap
                    block = total[:, tap * CH : (tap + 1) * CH].astype(BF16)
                    if core == 0:
                        blocks[26 - k] = block
                    else:
                        blocks[k] = block.T

    @pl.when(core == 0)
    def _():
        run(0)

    @pl.when(core != 0)
    def _():
        run(1)

    for step in range(4):
        rows = pl.ds(pl.multiple_of(((place_ref[1] + step) % 4) * 64, 64), 64)
        parts[step][...] = blocks[:, rows, :]


def scatter_kernel(place_ref, *refs):
    ins, outs = refs[0:4], refs[4:8]
    for step in range(4):
        rows = pl.ds(pl.multiple_of(((place_ref[3] + step) % 4) * 16, 16), 16)
        total = (ins[0][:, rows, :].astype(F32) + ins[2][:, rows, :].astype(F32)) + (
            ins[1][:, rows, :].astype(F32) + ins[3][:, rows, :].astype(F32)
        )
        outs[step][...] = total.astype(BF16)


def gather_kernel(place_ref, part0, part1, part2, part3, passed, wide, again, passed_out):
    for step, part in enumerate((part0, part1, part2, part3)):
        rows = pl.ds(pl.multiple_of(((place_ref[3] + 4 - step) % 4) * 16, 16), 16)
        wide[:, rows, :] = part[...]
        again[:, rows, :] = part[...]


def final_kernel(place_ref, *refs):
    own, mate = refs[0:4], refs[4:8]
    grad_one, grad_two, sems = refs[8:]

    def copies(dst, parts, place, sem):
        return [
            pltpu.make_async_copy(
                parts[step],
                dst.at[:, pl.ds(pl.multiple_of(((place + 4 - step) % 4) * 64, 64), 64), :],
                sem.at[step],
            )
            for step in range(4)
        ]

    def run(own_dst, mate_dst):
        made = copies(own_dst, own, place_ref[1], sems.at[0])
        made += copies(mate_dst, mate, place_ref[2], sems.at[1])
        for copy in made:
            copy.start()
        for copy in made:
            copy.wait()

    @pl.when(place_ref[0] == 0)
    def _():
        run(grad_two, grad_one)

    @pl.when(place_ref[0] != 0)
    def _():
        run(grad_one, grad_two)


def call(kernel, name, outs, in_specs, out_specs, scratch, flops, moved, mib, aliases=None):
    return pl.pallas_call(
        kernel,
        name=name,
        out_shape=[
            jax.ShapeDtypeStruct(*out) if isinstance(out[0], tuple) else jax.ShapeDtypeStruct(out, BF16)
            for out in outs
        ],
        in_specs=in_specs,
        out_specs=out_specs,
        scratch_shapes=scratch,
        input_output_aliases=aliases or {},
        compiler_params=pltpu.CompilerParams(vmem_limit_bytes=mib * 1024 * 1024),
        cost_estimate=pl.CostEstimate(flops=flops, bytes_accessed=moved, transcendentals=0),
    )


def on_device(
    features, cotangent, weight_one, weight_two, occupancy, neighbour_owner, neighbour_slot
):
    index = lax.axis_index(AXES)
    here = coordinates(index)
    core = here["core"]
    first, second, third = ("x", "z"), ("z", "y"), ("y", "x")

    def along(axis, which):
        return jnp.where(which == 0, here[axis[0]], here[axis[1]])

    place = jnp.stack([core, along(first, core), along(first, 1 - core), along(second, core)])
    place = place.astype(jnp.int32)

    graph = jnp.concatenate([occupancy.reshape(1, 1), neighbour_owner], axis=1)
    graph_mate = swap(graph)
    two = jnp.concatenate([graph, graph_mate], axis=0)
    first_brick = index - core - 2
    own_brick = jnp.stack([index, index ^ 1])[:, None]
    own_brick = jnp.where(two[:, 0:1] > 0, own_brick, -1)
    owners = jnp.concatenate([two[:, 1:14], own_brick, two[:, 14:27]], axis=1)
    rel = owners - first_brick
    same = (rel % 2) == core
    kind = jnp.where(rel // 2 == 1, 0, jnp.where(rel // 2 == 0, 1, 2))
    picks = jnp.where(owners >= 0, jnp.where(same, kind, kind + 3), 6).astype(jnp.int32)

    def sent_halo(field):
        return shifted(field, 2), shifted(field, -2)

    flops = 2 * ROWS * TAPS * 3 * CH
    stack = pltpu.VMEM((2, 7, ROWS, CH), BF16)
    frame = pltpu.VMEM((FRAME_ROWS, TAPS), BF16)
    held = pltpu.VMEM((2, 27, CH, CH), BF16)
    sems = pltpu.SemaphoreType.DMA((8,))
    pair = (2, ROWS, CH)
    rows64, rows16 = (27, 64, CH), (27, 16, CH)

    (fields,) = call(
        pack_kernel, "pack_fields", [pair], [HBM_SPEC] * 2, [VMEM_SPEC],
        [pltpu.SemaphoreType.DMA((2,))], 1000, 1_000_000, 60,
    )(features, cotangent)
    before, after = sent_halo(fields)
    frames, spare = call(
        frames_kernel, "build_frames", [(2 * FRAME_ROWS, TAPS), (FRAME_ROWS, TAPS)],
        [SMEM_SPEC] * 2 + [ANY_SPEC] * 6, [VMEM_SPEC] * 2, [stack, sems], 1_000_000, 12_000_000, 14,
    )(picks, place, fields, before, after, swap(fields), swap(before), swap(after))
    (pre_act,) = call(
        hidden_kernel, "first_conv", [((ROWS, CH), F32)], [SMEM_SPEC] + [VMEM_SPEC] * 3, [VMEM_SPEC], [],
        flops, 4_000_000, 14,
    )(place, frames, spare, weight_one)
    (both,) = call(
        grad_kernel, "grad_conv", [pair], [SMEM_SPEC] + [VMEM_SPEC] * 4, [VMEM_SPEC], [],
        flops, 4_000_000, 14,
    )(place, frames, spare, weight_two, pre_act)
    both_mate = swap(both)

    *parts, both = call(
        gradient_kernel, "weight_grads", [rows64] * 4 + [pair],
        [SMEM_SPEC] + [VMEM_SPEC] * 3 + [ANY_SPEC], [VMEM_SPEC] * 4 + [ANY_SPEC],
        [pltpu.VMEM((2, CH, ROWS), BF16), pltpu.VMEM((27, CH, CH), BF16)],
        2 * flops, 10_000_000, 18, {4: 4},
    )(place, both, both_mate, frames, both)

    def rounds(arrays, axis):
        return [arrays[0]] + [ring_send(arrays[d], axis, d) for d in (1, 2, 3)]

    arrived = rounds(parts, first)
    quarter = call(
        scatter_kernel, "sum_and_split", [rows16] * 4, [SMEM_SPEC] + [VMEM_SPEC] * 4, [VMEM_SPEC] * 4,
        [], 4_000_000, 4_500_000, 12,
    )(place, *arrived)

    (both,) = call(
        order_kernel, "after_first_arrival", [pair], [ANY_SPEC] * 2, [ANY_SPEC], [], 1000, 1000, 8, {0: 0},
    )(both, quarter[0])
    before, after = sent_halo(both)
    mate_before, mate_after = swap(before), swap(after)
    def added(arrays):
        wide = [array.astype(F32) for array in arrays]
        return (wide[0] + wide[2]) + (wide[1] + wide[3])

    small = added(rounds(quarter, second)).astype(BF16)
    scale = float(128 * ROWS) ** (-0.5)
    whole = (scale * added(rounds([small] * 4, third))).astype(BF16)

    wide, again, both = call(
        gather_kernel, "gather_rows", [rows64] * 2 + [pair],
        [SMEM_SPEC] + [VMEM_SPEC] * 4 + [ANY_SPEC], [VMEM_SPEC] * 2 + [ANY_SPEC], [],
        1000, 2_700_000, 12, {5: 2},
    )(place, *rounds([whole] * 4, second), both)
    chunks = rounds([wide] * 4, first)
    output, grad_input, again = call(
        outer_kernel, "outer_convs", [(1, ROWS, CH)] * 2 + [rows64],
        [SMEM_SPEC] + [ANY_SPEC] * 6 + [HBM_SPEC] * 2 + [ANY_SPEC], [VMEM_SPEC] * 2 + [ANY_SPEC],
        [frame, stack, held, sems],
        2 * flops, 12_000_000, 18, {9: 2},
    )(picks, both, before, after, both_mate, mate_before, mate_after, weight_two, weight_one, again)
    mates = [swap(again)] + [swap(chunk) for chunk in chunks[1:]]
    grad_one, grad_two = call(
        final_kernel, "place_rows", [(27, CH, CH)] * 2,
        [SMEM_SPEC] + [VMEM_SPEC] * 8, [ANY_SPEC] * 2,
        [pltpu.SemaphoreType.DMA((2, 4))], 1000, 14_000_000, 12,
    )(place, *chunks, *mates)
    return output, grad_input, grad_one, grad_two


def solution(mesh):
    by_brick = P(AXES, None, None)
    in_specs = (by_brick, by_brick, P(), P(), P(AXES), P(AXES, None), P(AXES, None))
    out_specs = (by_brick, by_brick, P(), P())
    return jax.shard_map(
        on_device, mesh=mesh, in_specs=in_specs, out_specs=out_specs, check_vma=False
    )
```

time: 192 us -> 150 us (0.78)
  local copies, waits for them, and re-layouts: 37.9 us -> 1.25 us
  waiting for transfers between devices: 33.2 us -> 54.5 us
  starting transfers between devices: 75.7 us -> 59.2 us
  Pallas kernels: 40.4 us -> 30.8 us
    ppermute x24 -> x15, starting transfers between devices: 48.9 us -> 27.6 us  [ring_send(): return lax.ppermute(array, AXES, pairs)]
    transpose x4 -> x0, local copies, waits for them, and re-layouts: 18.1 us -> none  [the longest x2 10 us: on_device(): turned_two = jnp.transpose(weight_two[::-1], (0, 2, 1)).reshape(3, TAPS, CH)]
    unnamed x53 -> x7, local copies, waits for them, and re-layouts: 18 us -> 1.09 us
    ppermute x4, waiting for transfers between devices: 1.66 us -> 11.3 us  [shifted(): lax.ppermute(array, AXES, [(i, i + by) for i in range(128) if 0 <= i + by...]
    ppermute x24 -> x15, waiting for transfers between devices: 27.2 us -> 34.9 us  [ring_send(): return lax.ppermute(array, AXES, pairs)]
    pallas_call x5 -> x9, Pallas kernels: 34.9 us -> 27.3 us  [the longest x1 10.5 us: on_device(): call(outer_kernel, 'outer_convs', [(1, ROWS, CH)] * 2 + [rows64], [SMEM_S...]
    ppermute x15 -> x11, waiting for transfers between devices: 4.31 us -> 8.25 us  [swap(): lax.ppermute(array, AXES, [(index, index ^ 1) for index in range(128)])]
    ppermute x4, starting transfers between devices: 8.88 us -> 12.1 us  [shifted(): lax.ppermute(array, AXES, [(i, i + by) for i in range(128) if 0 <= i + by...]
  transfers between devices with their start and end apart: 43 -> 30, of which waited for: 13 -> 16; matrix products, arithmetic and copies ran while one was open for 11% -> 1% of each run, Pallas kernels for 6% -> 7%
where the time goes in v2:
time: 150 us; the launch traced here: 149 us
  starting transfers between devices  59.2 us (39%)
  waiting for transfers between devices  54.5 us (36%)
  Pallas kernels  30.8 us (21%)
  other arithmetic  1.95 us (1%)
  between operations  1.67 us (1%)
    ppermute x15, waiting for transfers between devices, ring_send(): return lax.ppermute(array, AXES, pairs)  34.9 us
    ppermute x15, starting transfers between devices, ring_send(): return lax.ppermute(array, AXES, pairs)  27.6 us
    ppermute x11, starting transfers between devices, swap(): lax.ppermute(array, AXES, [(index, index ^ 1) for index in range(128)])  19.6 us
    ppermute x4, starting transfers between devices, shifted(): lax.ppermute(array, AXES, [(i, i + by) for i in range(128) if 0 <= i + by...  12.1 us
    ppermute x4, waiting for transfers between devices, shifted(): lax.ppermute(array, AXES, [(i, i + by) for i in range(128) if 0 <= i + by...  11.3 us
    pallas_call x1, Pallas kernels, on_device(): call(outer_kernel, 'outer_convs', [(1, ROWS, CH)] * 2 + [rows64], [SMEM_S...  10.5 us
    ppermute x11, waiting for transfers between devices, swap(): lax.ppermute(array, AXES, [(index, index ^ 1) for index in range(128)])  8.25 us
    pallas_call x1, Pallas kernels, on_device(): call(gradient_kernel, 'weight_grads', [rows64] * 4 + [pair], [SMEM_SPEC]...  5.05 us
  transfers between devices with their start and end apart: 30, of which 16 were waited for; matrix products, arithmetic and copies ran while one was open for 1% of the time, Pallas kernels for 7%

profile of v2, /device:TPU:1, one launch (start us, length us, event | category | flops | bytes accessed | tf_op | source)
XLA Modules:
  0.0 149.4 jit_solution(17279205883168836537)
XLA Ops:
  0.6 2.0 %pack_fields.1.own = bf16[2,512,256]{2,1,0:T(8,128)(2,1)} custom-call(bf16[1,512,256]{2,1,0:T(8,128)(2,1)} %features.1, bf16[1,512,256]{2,1,0:T(8,128)(2,1)} %cotangent.1), custom_call_target="tpu_custom_call" | custom-call | flops 1000 | bytes 1000000 | tf_op jit(solution)/shard_map/pack_fields/pallas_call | solution.py:330
  3.9 5.5 %collective-permute-start.1 = (bf16[2,512,256]{2,1,0:T(8,128)(2,1)}, bf16[2,512,256]{2,1,0:T(8,128)(2,1)}, u32[]{:S(2)}, u32[]{:S(2)}) collective-permute-start(bf16[2,512,256]{2,1,0:T(8,128)(2,1)} %pack_fields.1.own), channel_id=1, source_target_pairs={{0,2},{1,3},{2,4},{3,5},{4,6},{5,7},{6,8},{7,9},{8,10},{9,11},{10,... | collective-permute-start | bytes 1572872 | tf_op jit(solution)/shard_map/ppermute | solution.py:45
  9.4 1.3 collective-permute-start.3
  13.9 4.3 %collective-permute-done.2.after = bf16[2,512,256]{2,1,0:T(8,128)(2,1)} collective-permute-done((bf16[2,512,256]{2,1,0:T(8,128)(2,1)}, bf16[2,512,256]{2,1,0:T(8,128)(2,1)}, u32[]{:S(2)}, u32[]{:S(2)}) %collective-permute-start.2) | collective-permute-done | bytes 524320 | tf_op jit(solution)/shard_map/ppermute | solution.py:45
  18.2 1.6 %collective-permute-start.5 = (bf16[2,512,256]{2,1,0:T(8,128)(2,1)}, bf16[2,512,256]{2,1,0:T(8,128)(2,1)S(1)}, u32[]{:S(2)}, u32[]{:S(2)}) collective-permute-start(bf16[2,512,256]{2,1,0:T(8,128)(2,1)} %collective-permute-done.2.after), channel_id=1, source_target_pairs={{0,1},{1,0},{2,3},{3,2},{4,5},{5,4},{6,7},{7,6},{8,9},{9,8},{10,11... | collective-permute-start | bytes 1572872 | tf_op jit(solution)/shard_map/ppermute | solution.py:41
  23.8 2.9 %build_frames.1 = (bf16[1280,2304]{1,0:T(8,128)(2,1)S(1)}, bf16[640,2304]{1,0:T(8,128)(2,1)S(1)}) custom-call(s32[2,27]{1,0:T(2,128)S(1)} %compare_select_fusion.3.pick_ref, s32[4]{0:T(128)S(1)} %pad_add_fusion.3.place_ref, bf16[2,512,256]{2,1,0:T(8,128)(2,1)S(1)} %copy-done.2, bf16[2,512,256]{2,1,0:T(8,128)(2,1)} %collective-permute-done.1.before, ...), custom_call_target="tpu_custom_call" | custom-call | flops 1000000 | bytes 12000000 | tf_op jit(solution)/shard_map/build_frames/pallas_call | solution.py:335
  26.8 2.5 %first_conv.1.pre_act_ref = f32[512,256]{1,0:T(8,128)S(1)} custom-call(s32[4]{0:T(128)S(1)} %pad_add_fusion.3.place_ref, bf16[1280,2304]{1,0:T(8,128)(2,1)S(1)} %get-tuple-element.23.frames, bf16[640,2304]{1,0:T(8,128)(2,1)S(1)} %get-tuple-element.24.spare, bf16[27,256,256]{2,1,0:T(8,128)(2,1)S(1)} %copy-done), custom_call_target="tpu_custom_call" | custom-call | flops 1811939328 | bytes 4000000 | tf_op jit(solution)/shard_map/first_conv/pallas_call | solution.py:339
  29.4 2.6 %grad_conv.1.both = bf16[2,512,256]{2,1,0:T(8,128)(2,1)S(1)} custom-call(s32[4]{0:T(128)S(1)} %pad_add_fusion.3.place_ref, bf16[1280,2304]{1,0:T(8,128)(2,1)S(1)} %get-tuple-element.23.frames, bf16[640,2304]{1,0:T(8,128)(2,1)S(1)} %get-tuple-element.24.spare, bf16[27,256,256]{2,1,0:T(8,128)(2,1)S(1)} %copy-done.1, f32[512,256]{1,0:T(8,128)S(1)} %first_conv.1.pre_act_ref), custom_call_target="tpu_custom_call" | custom-call | flops 1811939328 | bytes 4000000 | tf_op jit(solution)/shard_map/grad_conv/pallas_call | solution.py:343
  32.5 1.5 %collective-permute-done.6.both_mate.mate = bf16[2,512,256]{2,1,0:T(8,128)(2,1)S(1)} collective-permute-done((bf16[2,512,256]{2,1,0:T(8,128)(2,1)S(1)}, bf16[2,512,256]{2,1,0:T(8,128)(2,1)S(1)}, u32[]{:S(2)}, u32[]{:S(2)}) %collective-permute-start.6) | collective-permute-done | bytes 524320 | tf_op jit(solution)/shard_map/ppermute | solution.py:41
  34.0 5.1 %weight_grads.1 = (bf16[27,64,256]{2,1,0:T(8,128)(2,1)S(1)}, bf16[27,64,256]{2,1,0:T(8,128)(2,1)S(1)}, bf16[27,64,256]{2,1,0:T(8,128)(2,1)S(1)}, bf16[27,64,256]...) custom-call(s32[4]{0:T(128)S(1)} %pad_add_fusion.3.place_ref, ...), custom_call_target="tpu_custom_call", output_to_operand_aliasing={{4}: (4, {})} | custom-call | flops 3623878656 | bytes 10000000 | tf_op jit(solution)/shard_map/weight_grads/pallas_call | solution.py:349
  39.0 7.0 %collective-permute-start.7 = (bf16[27,64,256]{2,1,0:T(8,128)(2,1)S(1)}, bf16[27,64,256]{2,1,0:T(8,128)(2,1)S(1)}, u32[]{:S(2)}, u32[]{:S(2)}) collective-permute-start(bf16[27,64,256]{2,1,0:T(8,128)(2,1)S(1)} %get-tuple-element.26), channel_id=1, source_target_pairs={{0,32},{1,9},{2,34},{3,11},{4,36},{5,13},{6,38},{7,15},{8,40},{9,1... | collective-permute-start | bytes 2654216 | tf_op jit(solution)/shard_map/ppermute | solution.py:37
  46.0 3.6 %collective-permute-start.8 = (bf16[27,64,256]{2,1,0:T(8,128)(2,1)S(1)}, bf16[27,64,256]{2,1,0:T(8,128)(2,1)S(1)}, u32[]{:S(2)}, u32[]{:S(2)}) collective-permute-start(bf16[27,64,256]{2,1,0:T(8,128)(2,1)S(1)} %get-tuple-element.27), channel_id=1, source_target_pairs={{0,64},{1,17},{2,66},{3,19},{4,68},{5,21},{6,70},{7,23},{8,72},{9,... | collective-permute-start | bytes 2654216 | tf_op jit(solution)/shard_map/ppermute | solution.py:37
  50.0 9.1 %collective-permute-done.7.refs_1_ = bf16[27,64,256]{2,1,0:T(8,128)(2,1)S(1)} collective-permute-done((bf16[27,64,256]{2,1,0:T(8,128)(2,1)S(1)}, bf16[27,64,256]{2,1,0:T(8,128)(2,1)S(1)}, u32[]{:S(2)}, u32[]{:S(2)}) %collective-permute-start.7) | collective-permute-done | bytes 884768 | tf_op jit(solution)/shard_map/ppermute | solution.py:37
  59.1 10.7 %collective-permute-done.8.refs_2_ = bf16[27,64,256]{2,1,0:T(8,128)(2,1)S(1)} collective-permute-done((bf16[27,64,256]{2,1,0:T(8,128)(2,1)S(1)}, bf16[27,64,256]{2,1,0:T(8,128)(2,1)S(1)}, u32[]{:S(2)}, u32[]{:S(2)}) %collective-permute-start.8) | collective-permute-done | bytes 884768 | tf_op jit(solution)/shard_map/ppermute | solution.py:37
  70.9 1.8 %collective-permute-start.11 = (bf16[27,16,256]{2,1,0:T(8,128)(2,1)S(1)}, bf16[27,16,256]{2,1,0:T(8,128)(2,1)S(1)}, u32[]{:S(2)}, u32[]{:S(2)}) collective-permute-start(bf16[27,16,256]{2,1,0:T(8,128)(2,1)S(1)} %get-tuple-element.31), channel_id=1, source_target_pairs={{0,8},{1,3},{2,10},{3,5},{4,12},{5,7},{6,14},{7,1},{8,16},{9,11},{... | collective-permute-start | bytes 663560 | tf_op jit(solution)/shard_map/ppermute | solution.py:37
  73.6 3.6 %collective-permute-done.10 = bf16[27,16,256]{2,1,0:T(8,128)(2,1)S(1)} collective-permute-done((bf16[27,16,256]{2,1,0:T(8,128)(2,1)S(1)}, bf16[27,16,256]{2,1,0:T(8,128)(2,1)S(1)}, u32[]{:S(2)}, u32[]{:S(2)}) %collective-permute-start.10) | collective-permute-done | bytes 221216 | tf_op jit(solution)/shard_map/ppermute | solution.py:37
  77.3 2.1 %collective-permute-done.11 = bf16[27,16,256]{2,1,0:T(8,128)(2,1)S(1)} collective-permute-done((bf16[27,16,256]{2,1,0:T(8,128)(2,1)S(1)}, bf16[27,16,256]{2,1,0:T(8,128)(2,1)S(1)}, u32[]{:S(2)}, u32[]{:S(2)}) %collective-permute-start.11) | collective-permute-done | bytes 221216 | tf_op jit(solution)/shard_map/ppermute | solution.py:37
  79.4 7.2 %collective-permute-start.15 = (bf16[27,16,256]{2,1,0:T(8,128)(2,1)S(1)}, bf16[27,16,256]{2,1,0:T(8,128)(2,1)S(1)}, u32[]{:S(2)}, u32[]{:S(2)}) collective-permute-start(bf16[27,16,256]{2,1,0:T(8,128)(2,1)S(1)} %add_convert_fusion), channel_id=1, source_target_pairs={{0,6},{1,97},{2,0},{3,99},{4,2},{5,101},{6,4},{7,103},{8,14},{9,10... | collective-permute-start | bytes 663560 | tf_op jit(solution)/shard_map/ppermute | solution.py:37
  86.6 1.4 collective-permute-start.13
  89.4 4.0 %collective-permute-start.19 = (bf16[2,512,256]{2,1,0:T(8,128)(2,1)S(1)}, bf16[2,512,256]{2,1,0:T(8,128)(2,1)S(1)}, u32[]{:S(2)}, u32[]{:S(2)}) collective-permute-start(bf16[2,512,256]{2,1,0:T(8,128)(2,1)S(1)} %after_first_arrival.1.passed), channel_id=1, source_target_pairs={{0,2},{1,3},{2,4},{3,5},{4,6},{5,7},{6,8},{7,9},{8,10},{9,11},{10,... | collective-permute-start | bytes 1572872 | tf_op jit(solution)/shard_map/ppermute | solution.py:45
  93.4 1.9 %collective-permute-done.14 = bf16[27,16,256]{2,1,0:T(8,128)(2,1)S(1)} collective-permute-done((bf16[27,16,256]{2,1,0:T(8,128)(2,1)S(1)}, bf16[27,16,256]{2,1,0:T(8,128)(2,1)S(1)}, u32[]{:S(2)}, u32[]{:S(2)}) %collective-permute-start.14) | collective-permute-done | bytes 221216 | tf_op jit(solution)/shard_map/ppermute | solution.py:37
  97.0 7.0 %collective-permute-done.20.after = bf16[2,512,256]{2,1,0:T(8,128)(2,1)S(1)} collective-permute-done((bf16[2,512,256]{2,1,0:T(8,128)(2,1)S(1)}, bf16[2,512,256]{2,1,0:T(8,128)(2,1)S(1)}, u32[]{:S(2)}, u32[]{:S(2)}) %collective-permute-start.20) | collective-permute-done | bytes 524320 | tf_op jit(solution)/shard_map/ppermute | solution.py:45
  104.0 6.1 %collective-permute-done.18.part3 = bf16[27,16,256]{2,1,0:T(8,128)(2,1)S(1)} collective-permute-done((bf16[27,16,256]{2,1,0:T(8,128)(2,1)S(1)}, bf16[27,16,256]{2,1,0:T(8,128)(2,1)S(1)}, u32[]{:S(2)}, u32[]{:S(2)}) %collective-permute-start.18) | collective-permute-done | bytes 221216 | tf_op jit(solution)/shard_map/ppermute | solution.py:37
  110.1 1.4 collective-permute-done.16.part1
  112.4 2.6 %collective-permute-start.24 = (bf16[27,64,256]{2,1,0:T(8,128)(2,1)S(1)}, bf16[27,64,256]{2,1,0:T(8,128)(2,1)S(1)}, u32[]{:S(2)}, u32[]{:S(2)}) collective-permute-start(bf16[27,64,256]{2,1,0:T(8,128)(2,1)S(1)} %get-tuple-element.38.refs_0_), channel_id=1, source_target_pairs={{0,64},{1,17},{2,66},{3,19},{4,68},{5,21},{6,70},{7,23},{8,72},{9,... | collective-permute-start | bytes 2654216 | tf_op jit(solution)/shard_map/ppermute | solution.py:37
  115.8 6.9 %collective-permute-start.22 = (bf16[2,512,256]{2,1,0:T(8,128)(2,1)S(1)}, bf16[2,512,256]{2,1,0:T(8,128)(2,1)S(1)}, u32[]{:S(2)}, u32[]{:S(2)}) collective-permute-start(bf16[2,512,256]{2,1,0:T(8,128)(2,1)S(1)} %collective-permute-done.20.after), channel_id=1, source_target_pairs={{0,1},{1,0},{2,3},{3,2},{4,5},{5,4},{6,7},{7,6},{8,9},{9,8},{10,11... | collective-permute-start | bytes 1572872 | tf_op jit(solution)/shard_map/ppermute | solution.py:41
  122.7 1.5 %collective-permute-done.22.mate_after = bf16[2,512,256]{2,1,0:T(8,128)(2,1)S(1)} collective-permute-done((bf16[2,512,256]{2,1,0:T(8,128)(2,1)S(1)}, bf16[2,512,256]{2,1,0:T(8,128)(2,1)S(1)}, u32[]{:S(2)}, u32[]{:S(2)}) %collective-permute-start.22) | collective-permute-done | bytes 524320 | tf_op jit(solution)/shard_map/ppermute | solution.py:41
  125.0 10.5 %outer_convs.1 = (bf16[1,512,256]{2,1,0:T(8,128)(2,1)}, bf16[1,512,256]{2,1,0:T(8,128)(2,1)}, bf16[27,64,256]{2,1,0:T(8,128)(2,1)S(1)}) custom-call(s32[2,27]{1,0:T(2,128)S(1)} %compare_select_fusion.3.pick_ref, bf16[2,512,256]{2,1,0:T(8,128)(2,1)S(1)} %get-tuple-element.34.own, ...), custom_call_target="tpu_custom_call", output_to_operand_aliasing={{2}: (9, {})} | custom-call | flops 3623878656 | bytes 12000000 | tf_op jit(solution)/shard_map/outer_convs/pallas_call | solution.py:384
  136.0 3.7 %collective-permute-start.29 = (bf16[27,64,256]{2,1,0:T(8,128)(2,1)S(1)}, bf16[27,64,256]{2,1,0:T(8,128)(2,1)S(1)}, u32[]{:S(2)}, u32[]{:S(2)}) collective-permute-start(bf16[27,64,256]{2,1,0:T(8,128)(2,1)S(1)} %collective-permute-done.25.refs_3_), channel_id=1, source_target_pairs={{0,1},{1,0},{2,3},{3,2},{4,5},{5,4},{6,7},{7,6},{8,9},{9,8},{10,11... | collective-permute-start | bytes 2654216 | tf_op jit(solution)/shard_map/ppermute | solution.py:41
  139.7 3.9 %collective-permute-start.27 = (bf16[27,64,256]{2,1,0:T(8,128)(2,1)S(1)}, bf16[27,64,256]{2,1,0:T(8,128)(2,1)S(1)}, u32[]{:S(2)}, u32[]{:S(2)}) collective-permute-start(bf16[27,64,256]{2,1,0:T(8,128)(2,1)S(1)} %collective-permute-done.23.refs_1_), channel_id=1, source_target_pairs={{0,1},{1,0},{2,3},{3,2},{4,5},{5,4},{6,7},{7,6},{8,9},{9,8},{10,11... | collective-permute-start | bytes 2654216 | tf_op jit(solution)/shard_map/ppermute | solution.py:41
  143.6 2.0 %collective-permute-done.27.refs_5_ = bf16[27,64,256]{2,1,0:T(8,128)(2,1)S(1)} collective-permute-done((bf16[27,64,256]{2,1,0:T(8,128)(2,1)S(1)}, bf16[27,64,256]{2,1,0:T(8,128)(2,1)S(1)}, u32[]{:S(2)}, u32[]{:S(2)}) %collective-permute-start.27) | collective-permute-done | bytes 884768 | tf_op jit(solution)/shard_map/ppermute | solution.py:41
  145.7 3.5 %place_rows.1 = (bf16[27,256,256]{2,1,0:T(8,128)(2,1)}, bf16[27,256,256]{2,1,0:T(8,128)(2,1)}) custom-call(s32[4]{0:T(128)S(1)} %pad_add_fusion.3.place_ref, bf16[27,64,256]{2,1,0:T(8,128)(2,1)S(1)} %get-tuple-element.38.refs_0_, bf16[27,64,256]{2,1,0:T(8,128)(2,1)S(1)} %collective-permute-done.23.refs_1_, ...), custom_call_target="tpu_custom_call" | custom-call | flops 1000 | bytes 14000000 | tf_op jit(solution)/shard_map/place_rows/pallas_call | solution.py:391
  (55 shorter events, 16.7 us)
Async XLA Ops:
  0.6 26.1 %copy-start = (bf16[27,256,256]{2,1,0:T(8,128)(2,1)S(1)}, bf16[27,256,256]{2,1,0:T(8,128)(2,1)}, u32[]{:S(2)}) copy-start(bf16[27,256,256]{2,1,0:T(8,128)(2,1)} %weight_one.3) | copy-start | bytes 10616836
  2.6 15.6 %collective-permute-start.2 = (bf16[2,512,256]{2,1,0:T(8,128)(2,1)}, bf16[2,512,256]{2,1,0:T(8,128)(2,1)}, u32[]{:S(2)}, u32[]{:S(2)}) collective-permute-start(bf16[2,512,256]{2,1,0:T(8,128)(2,1)} %pack_fields.1.own), channel_id=1, source_target_pairs={{2,0},{3,1},{4,2},{5,3},{6,4},{7,5},{8,6},{9,7},{10,8},{11,9},{12,... | collective-permute-start | bytes 1572872 | tf_op jit(solution)/shard_map/ppermute | solution.py:45
  3.9 15.9 %collective-permute-start.1 = (bf16[2,512,256]{2,1,0:T(8,128)(2,1)}, bf16[2,512,256]{2,1,0:T(8,128)(2,1)}, u32[]{:S(2)}, u32[]{:S(2)}) collective-permute-start(bf16[2,512,256]{2,1,0:T(8,128)(2,1)} %pack_fields.1.own), channel_id=1, source_target_pairs={{0,2},{1,3},{2,4},{3,5},{4,6},{5,7},{6,8},{7,9},{8,10},{9,11},{10,... | collective-permute-start | bytes 1572872 | tf_op jit(solution)/shard_map/ppermute | solution.py:45
  9.4 11.8 %collective-permute-start.3 = (bf16[2,512,256]{2,1,0:T(8,128)(2,1)}, bf16[2,512,256]{2,1,0:T(8,128)(2,1)}, u32[]{:S(2)}, u32[]{:S(2)}) collective-permute-start(bf16[2,512,256]{2,1,0:T(8,128)(2,1)} %pack_fields.1.own), channel_id=1, source_target_pairs={{0,1},{1,0},{2,3},{3,2},{4,5},{5,4},{6,7},{7,6},{8,9},{9,8},{10,11... | collective-permute-start | bytes 1572872 | tf_op jit(solution)/shard_map/ppermute | solution.py:41
  12.1 1.1 collective-permute-start
  18.2 3.4 %collective-permute-start.5 = (bf16[2,512,256]{2,1,0:T(8,128)(2,1)}, bf16[2,512,256]{2,1,0:T(8,128)(2,1)S(1)}, u32[]{:S(2)}, u32[]{:S(2)}) collective-permute-start(bf16[2,512,256]{2,1,0:T(8,128)(2,1)} %collective-permute-done.2.after), channel_id=1, source_target_pairs={{0,1},{1,0},{2,3},{3,2},{4,5},{5,4},{6,7},{7,6},{8,9},{9,8},{10,11... | collective-permute-start | bytes 1572872 | tf_op jit(solution)/shard_map/ppermute | solution.py:41
  19.9 2.9 %collective-permute-start.4 = (bf16[2,512,256]{2,1,0:T(8,128)(2,1)}, bf16[2,512,256]{2,1,0:T(8,128)(2,1)S(1)}, u32[]{:S(2)}, u32[]{:S(2)}) collective-permute-start(bf16[2,512,256]{2,1,0:T(8,128)(2,1)} %collective-permute-done.1.before), channel_id=1, source_target_pairs={{0,1},{1,0},{2,3},{3,2},{4,5},{5,4},{6,7},{7,6},{8,9},{9,8},{10,11... | collective-permute-start | bytes 1572872 | tf_op jit(solution)/shard_map/ppermute | solution.py:41
  26.8 2.6 %copy-start.1 = (bf16[27,256,256]{2,1,0:T(8,128)(2,1)S(1)}, bf16[27,256,256]{2,1,0:T(8,128)(2,1)}, u32[]{:S(2)}) copy-start(bf16[27,256,256]{2,1,0:T(8,128)(2,1)} %weight_two.3) | copy-start | bytes 10616836
  32.0 2.0 %collective-permute-start.6 = (bf16[2,512,256]{2,1,0:T(8,128)(2,1)S(1)}, bf16[2,512,256]{2,1,0:T(8,128)(2,1)S(1)}, u32[]{:S(2)}, u32[]{:S(2)}) collective-permute-start(bf16[2,512,256]{2,1,0:T(8,128)(2,1)S(1)} %grad_conv.1.both), channel_id=1, source_target_pairs={{0,1},{1,0},{2,3},{3,2},{4,5},{5,4},{6,7},{7,6},{8,9},{9,8},{10,11... | collective-permute-start | bytes 1572872 | tf_op jit(solution)/shard_map/ppermute | solution.py:41
  39.0 20.1 %collective-permute-start.7 = (bf16[27,64,256]{2,1,0:T(8,128)(2,1)S(1)}, bf16[27,64,256]{2,1,0:T(8,128)(2,1)S(1)}, u32[]{:S(2)}, u32[]{:S(2)}) collective-permute-start(bf16[27,64,256]{2,1,0:T(8,128)(2,1)S(1)} %get-tuple-element.26), channel_id=1, source_target_pairs={{0,32},{1,9},{2,34},{3,11},{4,36},{5,13},{6,38},{7,15},{8,40},{9,1... | collective-permute-start | bytes 2654216 | tf_op jit(solution)/shard_map/ppermute | solution.py:37
  46.0 23.8 %collective-permute-start.8 = (bf16[27,64,256]{2,1,0:T(8,128)(2,1)S(1)}, bf16[27,64,256]{2,1,0:T(8,128)(2,1)S(1)}, u32[]{:S(2)}, u32[]{:S(2)}) collective-permute-start(bf16[27,64,256]{2,1,0:T(8,128)(2,1)S(1)} %get-tuple-element.27), channel_id=1, source_target_pairs={{0,64},{1,17},{2,66},{3,19},{4,68},{5,21},{6,70},{7,23},{8,72},{9,... | collective-permute-start | bytes 2654216 | tf_op jit(solution)/shard_map/ppermute | solution.py:37
  49.6 20.2 %collective-permute-start.9 = (bf16[27,64,256]{2,1,0:T(8,128)(2,1)S(1)}, bf16[27,64,256]{2,1,0:T(8,128)(2,1)S(1)}, u32[]{:S(2)}, u32[]{:S(2)}) collective-permute-start(bf16[27,64,256]{2,1,0:T(8,128)(2,1)S(1)} %get-tuple-element.28), channel_id=1, source_target_pairs={{0,96},{1,25},{2,98},{3,27},{4,100},{5,29},{6,102},{7,31},{8,104},... | collective-permute-start | bytes 2654216 | tf_op jit(solution)/shard_map/ppermute | solution.py:37
  70.8 6.5 %collective-permute-start.10 = (bf16[27,16,256]{2,1,0:T(8,128)(2,1)S(1)}, bf16[27,16,256]{2,1,0:T(8,128)(2,1)S(1)}, u32[]{:S(2)}, u32[]{:S(2)}) collective-permute-start(bf16[27,16,256]{2,1,0:T(8,128)(2,1)S(1)} %get-tuple-element.30), channel_id=1, source_target_pairs={{0,16},{1,5},{2,18},{3,7},{4,20},{5,1},{6,22},{7,3},{8,24},{9,13},... | collective-permute-start | bytes 663560 | tf_op jit(solution)/shard_map/ppermute | solution.py:37
  70.9 8.4 %collective-permute-start.11 = (bf16[27,16,256]{2,1,0:T(8,128)(2,1)S(1)}, bf16[27,16,256]{2,1,0:T(8,128)(2,1)S(1)}, u32[]{:S(2)}, u32[]{:S(2)}) collective-permute-start(bf16[27,16,256]{2,1,0:T(8,128)(2,1)S(1)} %get-tuple-element.31), channel_id=1, source_target_pairs={{0,8},{1,3},{2,10},{3,5},{4,12},{5,7},{6,14},{7,1},{8,16},{9,11},{... | collective-permute-start | bytes 663560 | tf_op jit(solution)/shard_map/ppermute | solution.py:37
  72.7 6.6 %collective-permute-start.12 = (bf16[27,16,256]{2,1,0:T(8,128)(2,1)S(1)}, bf16[27,16,256]{2,1,0:T(8,128)(2,1)S(1)}, u32[]{:S(2)}, u32[]{:S(2)}) collective-permute-start(bf16[27,16,256]{2,1,0:T(8,128)(2,1)S(1)} %get-tuple-element.32), channel_id=1, source_target_pairs={{0,24},{1,7},{2,26},{3,1},{4,28},{5,3},{6,30},{7,5},{8,0},{9,15},{... | collective-permute-start | bytes 663560 | tf_op jit(solution)/shard_map/ppermute | solution.py:37
  79.4 14.0 %collective-permute-start.15 = (bf16[27,16,256]{2,1,0:T(8,128)(2,1)S(1)}, bf16[27,16,256]{2,1,0:T(8,128)(2,1)S(1)}, u32[]{:S(2)}, u32[]{:S(2)}) collective-permute-start(bf16[27,16,256]{2,1,0:T(8,128)(2,1)S(1)} %add_convert_fusion), channel_id=1, source_target_pairs={{0,6},{1,97},{2,0},{3,99},{4,2},{5,101},{6,4},{7,103},{8,14},{9,10... | collective-permute-start | bytes 663560 | tf_op jit(solution)/shard_map/ppermute | solution.py:37
  86.6 8.7 %collective-permute-start.14 = (bf16[27,16,256]{2,1,0:T(8,128)(2,1)S(1)}, bf16[27,16,256]{2,1,0:T(8,128)(2,1)S(1)}, u32[]{:S(2)}, u32[]{:S(2)}) collective-permute-start(bf16[27,16,256]{2,1,0:T(8,128)(2,1)S(1)} %add_convert_fusion), channel_id=1, source_target_pairs={{0,2},{1,33},{2,4},{3,35},{4,6},{5,37},{6,0},{7,39},{8,10},{9,41},... | collective-permute-start | bytes 663560 | tf_op jit(solution)/shard_map/ppermute | solution.py:37
  86.6 8.7 %collective-permute-start.13 = (bf16[27,16,256]{2,1,0:T(8,128)(2,1)S(1)}, bf16[27,16,256]{2,1,0:T(8,128)(2,1)S(1)}, u32[]{:S(2)}, u32[]{:S(2)}) collective-permute-start(bf16[27,16,256]{2,1,0:T(8,128)(2,1)S(1)} %add_convert_fusion), channel_id=1, source_target_pairs={{0,4},{1,65},{2,6},{3,67},{4,0},{5,69},{6,2},{7,71},{8,12},{9,73},... | collective-permute-start | bytes 663560 | tf_op jit(solution)/shard_map/ppermute | solution.py:37
  88.1 15.9 %collective-permute-start.20 = (bf16[2,512,256]{2,1,0:T(8,128)(2,1)S(1)}, bf16[2,512,256]{2,1,0:T(8,128)(2,1)S(1)}, u32[]{:S(2)}, u32[]{:S(2)}) collective-permute-start(bf16[2,512,256]{2,1,0:T(8,128)(2,1)S(1)} %after_first_arrival.1.passed), channel_id=1, source_target_pairs={{2,0},{3,1},{4,2},{5,3},{6,4},{7,5},{8,6},{9,7},{10,8},{11,9},{12,... | collective-permute-start | bytes 1572872 | tf_op jit(solution)/shard_map/ppermute | solution.py:45
  89.4 14.6 %collective-permute-start.19 = (bf16[2,512,256]{2,1,0:T(8,128)(2,1)S(1)}, bf16[2,512,256]{2,1,0:T(8,128)(2,1)S(1)}, u32[]{:S(2)}, u32[]{:S(2)}) collective-permute-start(bf16[2,512,256]{2,1,0:T(8,128)(2,1)S(1)} %after_first_arrival.1.passed), channel_id=1, source_target_pairs={{0,2},{1,3},{2,4},{3,5},{4,6},{5,7},{6,8},{7,9},{8,10},{9,11},{10,... | collective-permute-start | bytes 1572872 | tf_op jit(solution)/shard_map/ppermute | solution.py:45
  95.4 14.7 %collective-permute-start.18 = (bf16[27,16,256]{2,1,0:T(8,128)(2,1)S(1)}, bf16[27,16,256]{2,1,0:T(8,128)(2,1)S(1)}, u32[]{:S(2)}, u32[]{:S(2)}) collective-permute-start(bf16[27,16,256]{2,1,0:T(8,128)(2,1)S(1)} %multiply_convert_fusion.part0), channel_id=1, source_target_pairs={{0,24},{1,7},{2,26},{3,1},{4,28},{5,3},{6,30},{7,5},{8,0},{9,15},{... | collective-permute-start | bytes 663560 | tf_op jit(solution)/shard_map/ppermute | solution.py:37
  96.0 14.1 %collective-permute-start.17 = (bf16[27,16,256]{2,1,0:T(8,128)(2,1)S(1)}, bf16[27,16,256]{2,1,0:T(8,128)(2,1)S(1)}, u32[]{:S(2)}, u32[]{:S(2)}) collective-permute-start(bf16[27,16,256]{2,1,0:T(8,128)(2,1)S(1)} %multiply_convert_fusion.part0), channel_id=1, source_target_pairs={{0,16},{1,5},{2,18},{3,7},{4,20},{5,1},{6,22},{7,3},{8,24},{9,13},... | collective-permute-start | bytes 663560 | tf_op jit(solution)/shard_map/ppermute | solution.py:37
  96.0 15.6 %collective-permute-start.16 = (bf16[27,16,256]{2,1,0:T(8,128)(2,1)S(1)}, bf16[27,16,256]{2,1,0:T(8,128)(2,1)S(1)}, u32[]{:S(2)}, u32[]{:S(2)}) collective-permute-start(bf16[27,16,256]{2,1,0:T(8,128)(2,1)S(1)} %multiply_convert_fusion.part0), channel_id=1, source_target_pairs={{0,8},{1,3},{2,10},{3,5},{4,12},{5,7},{6,14},{7,1},{8,16},{9,11},{... | collective-permute-start | bytes 663560 | tf_op jit(solution)/shard_map/ppermute | solution.py:37
  112.2 23.8 %collective-permute-start.25 = (bf16[27,64,256]{2,1,0:T(8,128)(2,1)S(1)}, bf16[27,64,256]{2,1,0:T(8,128)(2,1)S(1)}, u32[]{:S(2)}, u32[]{:S(2)}) collective-permute-start(bf16[27,64,256]{2,1,0:T(8,128)(2,1)S(1)} %get-tuple-element.38.refs_0_), channel_id=1, source_target_pairs={{0,96},{1,25},{2,98},{3,27},{4,100},{5,29},{6,102},{7,31},{8,104},... | collective-permute-start | bytes 2654216 | tf_op jit(solution)/shard_map/ppermute | solution.py:37
  112.4 27.3 %collective-permute-start.24 = (bf16[27,64,256]{2,1,0:T(8,128)(2,1)S(1)}, bf16[27,64,256]{2,1,0:T(8,128)(2,1)S(1)}, u32[]{:S(2)}, u32[]{:S(2)}) collective-permute-start(bf16[27,64,256]{2,1,0:T(8,128)(2,1)S(1)} %get-tuple-element.38.refs_0_), channel_id=1, source_target_pairs={{0,64},{1,17},{2,66},{3,19},{4,68},{5,21},{6,70},{7,23},{8,72},{9,... | collective-permute-start | bytes 2654216 | tf_op jit(solution)/shard_map/ppermute | solution.py:37
  115.0 24.7 %collective-permute-start.23 = (bf16[27,64,256]{2,1,0:T(8,128)(2,1)S(1)}, bf16[27,64,256]{2,1,0:T(8,128)(2,1)S(1)}, u32[]{:S(2)}, u32[]{:S(2)}) collective-permute-start(bf16[27,64,256]{2,1,0:T(8,128)(2,1)S(1)} %get-tuple-element.38.refs_0_), channel_id=1, source_target_pairs={{0,32},{1,9},{2,34},{3,11},{4,36},{5,13},{6,38},{7,15},{8,40},{9,1... | collective-permute-start | bytes 2654216 | tf_op jit(solution)/shard_map/ppermute | solution.py:37
  115.8 8.5 %collective-permute-start.22 = (bf16[2,512,256]{2,1,0:T(8,128)(2,1)S(1)}, bf16[2,512,256]{2,1,0:T(8,128)(2,1)S(1)}, u32[]{:S(2)}, u32[]{:S(2)}) collective-permute-start(bf16[2,512,256]{2,1,0:T(8,128)(2,1)S(1)} %collective-permute-done.20.after), channel_id=1, source_target_pairs={{0,1},{1,0},{2,3},{3,2},{4,5},{5,4},{6,7},{7,6},{8,9},{9,8},{10,11... | collective-permute-start | bytes 1572872 | tf_op jit(solution)/shard_map/ppermute | solution.py:41
  122.7 2.3 %collective-permute-start.21 = (bf16[2,512,256]{2,1,0:T(8,128)(2,1)S(1)}, bf16[2,512,256]{2,1,0:T(8,128)(2,1)S(1)}, u32[]{:S(2)}, u32[]{:S(2)}) collective-permute-start(bf16[2,512,256]{2,1,0:T(8,128)(2,1)S(1)} %collective-permute-done.19.before), channel_id=1, source_target_pairs={{0,1},{1,0},{2,3},{3,2},{4,5},{5,4},{6,7},{7,6},{8,9},{9,8},{10,11... | collective-permute-start | bytes 1572872 | tf_op jit(solution)/shard_map/ppermute | solution.py:41
  135.5 8.1 %collective-permute-start.26 = (bf16[27,64,256]{2,1,0:T(8,128)(2,1)S(1)}, bf16[27,64,256]{2,1,0:T(8,128)(2,1)S(1)}, u32[]{:S(2)}, u32[]{:S(2)}) collective-permute-start(bf16[27,64,256]{2,1,0:T(8,128)(2,1)S(1)} %get-tuple-element.39), channel_id=1, source_target_pairs={{0,1},{1,0},{2,3},{3,2},{4,5},{5,4},{6,7},{7,6},{8,9},{9,8},{10,11... | collective-permute-start | bytes 2654216 | tf_op jit(solution)/shard_map/ppermute | solution.py:41
  136.0 7.6 %collective-permute-start.29 = (bf16[27,64,256]{2,1,0:T(8,128)(2,1)S(1)}, bf16[27,64,256]{2,1,0:T(8,128)(2,1)S(1)}, u32[]{:S(2)}, u32[]{:S(2)}) collective-permute-start(bf16[27,64,256]{2,1,0:T(8,128)(2,1)S(1)} %collective-permute-done.25.refs_3_), channel_id=1, source_target_pairs={{0,1},{1,0},{2,3},{3,2},{4,5},{5,4},{6,7},{7,6},{8,9},{9,8},{10,11... | collective-permute-start | bytes 2654216 | tf_op jit(solution)/shard_map/ppermute | solution.py:41
  139.6 4.0 %collective-permute-start.28 = (bf16[27,64,256]{2,1,0:T(8,128)(2,1)S(1)}, bf16[27,64,256]{2,1,0:T(8,128)(2,1)S(1)}, u32[]{:S(2)}, u32[]{:S(2)}) collective-permute-start(bf16[27,64,256]{2,1,0:T(8,128)(2,1)S(1)} %collective-permute-done.24.refs_2_), channel_id=1, source_target_pairs={{0,1},{1,0},{2,3},{3,2},{4,5},{5,4},{6,7},{7,6},{8,9},{9,8},{10,11... | collective-permute-start | bytes 2654216 | tf_op jit(solution)/shard_map/ppermute | solution.py:41
  139.7 6.0 %collective-permute-start.27 = (bf16[27,64,256]{2,1,0:T(8,128)(2,1)S(1)}, bf16[27,64,256]{2,1,0:T(8,128)(2,1)S(1)}, u32[]{:S(2)}, u32[]{:S(2)}) collective-permute-start(bf16[27,64,256]{2,1,0:T(8,128)(2,1)S(1)} %collective-permute-done.23.refs_1_), channel_id=1, source_target_pairs={{0,1},{1,0},{2,3},{3,2},{4,5},{5,4},{6,7},{7,6},{8,9},{9,8},{10,11... | collective-permute-start | bytes 2654216 | tf_op jit(solution)/shard_map/ppermute | solution.py:41
  (1 other events, 1.0 us)

commit v3 on v2

v3 whole, which is shorter than its diff:
```python
from functools import partial

import jax
import jax.numpy as jnp
from jax import lax
from jax.experimental import pallas as pl
from jax.experimental.pallas import tpu as pltpu
from jax.sharding import PartitionSpec as P

AXES = ("region", "shard")
SIDES = (4, 4, 4, 2)
ROWS = 512
OUTER = 320
CH = 256
TAPS = 2304
FRAME_ROWS = 640
EVEN = (1, 0, 3, 2)
ODD = (3, 2, 1, 0)
F32 = jnp.float32
BF16 = jnp.bfloat16
VMEM_SPEC = pl.BlockSpec(memory_space=pltpu.VMEM)
SMEM_SPEC = pl.BlockSpec(memory_space=pltpu.SMEM)
ANY_SPEC = pl.BlockSpec(memory_space=pl.ANY)
HBM_SPEC = pl.BlockSpec(memory_space=pltpu.HBM)


def coordinates(index):
    return {"x": index // 32, "z": (index // 8) % 4, "y": (index // 2) % 4, "core": index % 2}


def device_at(place):
    return place["x"] * 32 + place["z"] * 8 + place["y"] * 2 + place["core"]


def ring_send(array, axis_of_core, step, pairing=(None, None)):
    pairs = []
    for index in range(128):
        place = coordinates(index)
        axis = axis_of_core[place["core"]]
        place[axis] = (place[axis] + step) % 4
        partner = pairing[place["core"]]
        place["y"] = partner[place["y"]] if partner else place["y"]
        pairs.append((index, device_at(place)))
    return lax.ppermute(array, AXES, pairs)


def swap(array):
    return lax.ppermute(array, AXES, [(index, index ^ 1) for index in range(128)])


def shifted(array, by):
    return lax.ppermute(array, AXES, [(i, i + by) for i in range(128) if 0 <= i + by < 128])


def pack(brick, packed, field):
    packed[field, 0:64] = brick[0:64]
    packed[field, 64:128] = brick[448:512]
    for x in range(1, 7):
        slab = brick[64 * x : 64 * x + 64].astype(F32).reshape(8, 8, CH)
        edges = jnp.concatenate([slab[0], slab[7], slab[:, 0, :], slab[:, 7, :]], axis=0)
        packed[field, 96 + 32 * x : 128 + 32 * x] = edges.astype(BF16)


def build(full, packed, field, pick, out, first_row):
    z_of = lax.broadcasted_iota(jnp.int32, (10, 8, CH), 1)
    centre = pick(1, 1, 1) // 3

    def outer(sx, sy, sz, first, count):
        return packed[field, pick(sx, sy, sz), pl.ds(first, count), :].astype(F32)

    def plane(X, columns):
        below, here, above = [
            jnp.concatenate([low[None], mid, high[None]], axis=0) for low, mid, high in columns
        ]
        shifts = (
            pltpu.roll(jnp.where(z_of == 7, below, here), 1, 1),
            here,
            pltpu.roll(jnp.where(z_of == 0, above, here), 7, 1),
        )
        rows = pl.ds(pl.multiple_of(first_row + X * 64, 64), 64)
        for dz, grid in enumerate(shifts):
            even = grid.reshape(80, CH).astype(BF16)
            odd = grid[1:9].reshape(64, CH).astype(BF16)
            out[rows, (0 + dz) * CH : (1 + dz) * CH] = even[0:64]
            out[rows, (3 + dz) * CH : (4 + dz) * CH] = odd
            out[rows, (6 + dz) * CH : (7 + dz) * CH] = even[16:80]

    def inside(xp):
        return full[field, centre, pl.ds(pl.multiple_of(xp * 64, 64), 64), :].astype(F32).reshape(8, 8, CH)

    for X, sx, face in ((0, 0, 64), (1, 1, 0), (8, 1, 64), (9, 2, 0)):
        columns = []
        for sz in range(3):
            if sx == 1 and sz == 1:
                mid = inside(X - 1)
            else:
                mid = outer(sx, 1, sz, face, 64).reshape(8, 8, CH)
            columns.append((outer(sx, 0, sz, face + 48, 16)[8:16], mid, outer(sx, 2, sz, face, 16)[0:8]))
        plane(X, columns)

    @pl.loop(2, 8)
    def _(X):
        first = pl.multiple_of(64 + 32 * X, 32)
        columns = []
        for sz in range(3):
            if sz == 1:
                mid = inside(X - 1)
            else:
                edge = outer(1, 1, sz, first + 16, 16)
                edge = edge[8:16] if sz == 0 else edge[0:8]
                mid = jnp.broadcast_to(edge[:, None, :], (8, 8, CH))
            columns.append((outer(1, 0, sz, first, 16)[8:16], mid, outer(1, 2, sz, first, 16)[0:8]))
        plane(X, columns)


def convolved(frame, weights):
    total = None
    for plane in range(3):
        term = jnp.dot(
            frame[64 * plane : 64 * plane + ROWS, :],
            weights[9 * plane : 9 * plane + 9].reshape(TAPS, CH),
            preferred_element_type=F32,
        )
        total = term if total is None else total + term
    return total


def convolved_turned(frame, weights):
    total = None
    for k in range(27):
        window = frame[64 * (k // 9) : 64 * (k // 9) + ROWS, (k % 9) * CH : (k % 9 + 1) * CH]
        term = lax.dot_general(
            window, weights[26 - k], (((1,), (1,)), ((), ())), preferred_element_type=F32
        )
        total = term if total is None else total + term
    return total


def picker(pick_ref, which):
    return lambda sx, sy, sz: pick_ref[which, 9 * sx + 3 * sy + sz]


def loaded(own, mate, outers, weights, full, packed, held, sems):
    copies = [
        pltpu.make_async_copy(brick, full.at[:, place], sems.at[place])
        for place, brick in enumerate((own, mate))
    ]
    copies += [
        pltpu.make_async_copy(brick, packed.at[:, place], sems.at[2 + place])
        for place, brick in enumerate(outers)
    ]
    loads = [
        pltpu.make_async_copy(weight, held.at[place], sems.at[8 + place])
        for place, weight in enumerate(weights)
    ]
    for copy in copies + loads:
        copy.start()
    full[:, 2] = jnp.zeros((2, ROWS, CH), BF16)
    packed[:, 6] = jnp.zeros((2, OUTER, CH), BF16)
    for copy in copies:
        copy.wait()
    return loads


def order_kernel(passed, waited_for, passed_out):
    pass


def pack_kernel(features, cotangent, out, packed):
    for place, field in enumerate((features, cotangent)):
        out[place] = field[0]
        pack(field.at[0], packed, place)


def pack_both_kernel(both, waited_for, packed):
    for place in range(2):
        pack(both.at[place], packed, place)


def frames_kernel(
    pick_ref, place_ref, own, mate, packed_own, before, after, packed_mate, mate_before, mate_after,
    frames, spare, full, packed, sems
):
    outers = (packed_own, before, after, packed_mate, mate_before, mate_after)
    loaded(own, mate, outers, (), full, packed, None, sems)
    core = place_ref[0]
    build(full, packed, 1 - core, picker(pick_ref, 0), frames, 0)
    build(full, packed, core, picker(pick_ref, 0), spare, 0)
    build(full, packed, 1 - core, picker(pick_ref, 1), frames, FRAME_ROWS)


def hidden_kernel(place_ref, frames, spare, weight_one, pre_act):
    @pl.when(place_ref[0] == 0)
    def _():
        pre_act[...] = convolved(spare, weight_one)

    @pl.when(place_ref[0] != 0)
    def _():
        pre_act[...] = convolved(frames, weight_one)


def grad_kernel(place_ref, frames, spare, weight_two, pre_act_ref, both):
    def finish(frame):
        grad_hidden = convolved_turned(frame, weight_two)
        pre_act = pre_act_ref[...]
        sig = 1.0 / (1.0 + jnp.exp(-pre_act))
        both[0] = (pre_act / (1.0 + jnp.exp(-pre_act))).astype(BF16)
        both[1] = (grad_hidden * sig * (1.0 + pre_act * (1.0 - sig))).astype(BF16)

    @pl.when(place_ref[0] == 0)
    def _():
        finish(frames)

    @pl.when(place_ref[0] != 0)
    def _():
        finish(spare)


def outer_kernel(
    pick_ref, own, mate, packed_own, before, after, packed_mate, mate_before, mate_after,
    weight_two, weight_one, passed, output, grad_input, passed_out, frame, full, packed, held, sems
):
    outers = (packed_own, before, after, packed_mate, mate_before, mate_after)
    loads = loaded(own, mate, outers, (weight_two, weight_one), full, packed, held, sems)
    build(full, packed, 0, picker(pick_ref, 0), frame, 0)
    loads[0].wait()
    output[0] = convolved(frame, held.at[0]).astype(BF16)
    build(full, packed, 1, picker(pick_ref, 0), frame, 0)
    loads[1].wait()
    grad_input[0] = convolved_turned(frame, held.at[1]).astype(BF16)


def gradient_kernel(place_ref, both, both_mate, frames, passed, *rest):
    parts, (turned, blocks) = rest[0:5], rest[6:]
    core = place_ref[0]
    turned[0] = both[core].T
    turned[1] = both_mate[core].T

    def run(core):
        for plane in range(3):
            for third in range(3):
                lanes = slice(third * 3 * CH, (third + 1) * 3 * CH)
                row = 64 * plane
                total = jnp.dot(turned[0], frames[row : row + ROWS, lanes], preferred_element_type=F32)
                row += FRAME_ROWS
                total += jnp.dot(turned[1], frames[row : row + ROWS, lanes], preferred_element_type=F32)
                for tap in range(3):
                    k = 9 * plane + 3 * third + tap
                    block = total[:, tap * CH : (tap + 1) * CH].astype(BF16)
                    if core == 0:
                        blocks[26 - k] = block
                    else:
                        blocks[k] = block.T

    @pl.when(core == 0)
    def _():
        run(0)

    @pl.when(core != 0)
    def _():
        run(1)

    for step, part in zip((0, 1, 3), parts[0:3]):
        part[...] = blocks[:, whole_rows(place_ref[1] + step), :]
    for other, part in enumerate(parts[3:5]):
        part[...] = blocks[:, half_rows(place_ref[1] + 2, place_ref[4] + other), :]


def whole_rows(along):
    return pl.ds(pl.multiple_of((along % 4) * 64, 64), 64)


def half_rows(along, bit):
    return pl.ds(pl.multiple_of((along % 4) * 64 + (bit % 2) * 32, 32), 32)


def scatter_kernel(place_ref, own, after, before, across, *outs):
    for step in range(4):
        quarter = (place_ref[3] + step) % 4
        rows = pl.ds(pl.multiple_of(quarter * 16, 16), 16)
        half = pl.ds(pl.multiple_of((quarter % 2) * 16, 16), 16)
        total = own[:, rows, :].astype(F32) + after[:, rows, :].astype(F32) + before[:, rows, :].astype(F32)
        two_on = across[:, half, :].astype(F32)
        total += jnp.where(quarter // 2 == place_ref[4], two_on, jnp.zeros_like(two_on))
        outs[step][...] = total.astype(BF16)


def gather_kernel(place_ref, part0, part1, part2, part3, passed, wide, again, half, passed_out):
    for step, part in enumerate((part0, part1, part2, part3)):
        quarter = (place_ref[3] + 4 - step) % 4
        rows = pl.ds(pl.multiple_of(quarter * 16, 16), 16)
        wide[:, rows, :] = part[...]
        again[:, rows, :] = part[...]

        @pl.when(quarter // 2 == place_ref[4])
        def _(part=part, quarter=quarter):
            half[:, pl.ds(pl.multiple_of((quarter % 2) * 16, 16), 16), :] = part[...]


def place_kernel(hows, place_ref, *refs):
    count = len(hows)
    own, mate = refs[0:count], refs[count : 2 * count]
    grad_one, grad_two, sems = refs[-3:]

    def run(own_dst, mate_dst):
        made = []
        for n, (how, other) in enumerate(hows):
            for side, (dst, part) in enumerate(((own_dst, own[n]), (mate_dst, mate[n]))):
                along, bit = place_ref[1 + side], place_ref[4 + side]
                rows = whole_rows(along + how) if how != 2 else half_rows(along + 2, bit + other)
                made.append(pltpu.make_async_copy(part, dst.at[:, rows, :], sems.at[side, n]))
        for copy in made:
            copy.start()
        for copy in made:
            copy.wait()

    @pl.when(place_ref[0] == 0)
    def _():
        run(grad_two, grad_one)

    @pl.when(place_ref[0] != 0)
    def _():
        run(grad_one, grad_two)


def call(kernel, name, outs, in_specs, out_specs, scratch, flops, moved, mib, aliases=None):
    return pl.pallas_call(
        kernel,
        name=name,
        out_shape=[
            jax.ShapeDtypeStruct(*out) if isinstance(out[0], tuple) else jax.ShapeDtypeStruct(out, BF16)
            for out in outs
        ],
        in_specs=in_specs,
        out_specs=out_specs,
        scratch_shapes=scratch,
        input_output_aliases=aliases or {},
        compiler_params=pltpu.CompilerParams(vmem_limit_bytes=mib * 1024 * 1024),
        cost_estimate=pl.CostEstimate(flops=flops, bytes_accessed=moved, transcendentals=0),
    )


def on_device(
    features, cotangent, weight_one, weight_two, occupancy, neighbour_owner, neighbour_slot
):
    index = lax.axis_index(AXES)
    here = coordinates(index)
    core = here["core"]
    first, second, third = ("x", "z"), ("z", "y"), ("y", "x")

    def along(axis, which):
        return jnp.where(which == 0, here[axis[0]], here[axis[1]])

    bits = jnp.stack([here["y"] % 2, here["y"] // 2])
    pairing = (EVEN, ODD)
    place = jnp.stack(
        [core, along(first, core), along(first, 1 - core), along(second, core), bits[core], bits[1 - core]]
    )
    place = place.astype(jnp.int32)

    graph = jnp.concatenate([occupancy.reshape(1, 1), neighbour_owner], axis=1)
    graph_mate = swap(graph)
    two = jnp.concatenate([graph, graph_mate], axis=0)
    first_brick = index - core - 2
    own_brick = jnp.stack([index, index ^ 1])[:, None]
    own_brick = jnp.where(two[:, 0:1] > 0, own_brick, -1)
    owners = jnp.concatenate([two[:, 1:14], own_brick, two[:, 14:27]], axis=1)
    rel = owners - first_brick
    same = (rel % 2) == core
    kind = jnp.where(rel // 2 == 1, 0, jnp.where(rel // 2 == 0, 1, 2))
    picks = jnp.where(owners >= 0, jnp.where(same, kind, kind + 3), 6).astype(jnp.int32)

    def sent_halo(field):
        return shifted(field, 2), shifted(field, -2)

    flops = 2 * ROWS * TAPS * 3 * CH
    full = pltpu.VMEM((2, 3, ROWS, CH), BF16)
    packed = pltpu.VMEM((2, 7, OUTER, CH), BF16)
    frame = pltpu.VMEM((FRAME_ROWS, TAPS), BF16)
    held = pltpu.VMEM((2, 27, CH, CH), BF16)
    sems = pltpu.SemaphoreType.DMA((10,))
    pair, skin = (2, ROWS, CH), (2, OUTER, CH)
    rows64, rows32, rows16 = (27, 64, CH), (27, 32, CH), (27, 16, CH)

    fields, skins = call(
        pack_kernel, "pack_fields", [pair, skin], [VMEM_SPEC] * 2, [VMEM_SPEC] * 2, [], 1000, 1_000_000, 60,
    )(features, cotangent)
    before, after = sent_halo(skins)
    frames, spare = call(
        frames_kernel, "build_frames", [(2 * FRAME_ROWS, TAPS), (FRAME_ROWS, TAPS)],
        [SMEM_SPEC] * 2 + [ANY_SPEC] * 8, [VMEM_SPEC] * 2, [full, packed, sems], 1_000_000, 12_000_000, 14,
    )(picks, place, fields, swap(fields), skins, before, after, swap(skins), swap(before), swap(after))
    (pre_act,) = call(
        hidden_kernel, "first_conv", [((ROWS, CH), F32)], [SMEM_SPEC] + [VMEM_SPEC] * 3, [VMEM_SPEC], [],
        flops, 4_000_000, 14,
    )(place, frames, spare, weight_one)
    (both,) = call(
        grad_kernel, "grad_conv", [pair], [SMEM_SPEC] + [VMEM_SPEC] * 4, [VMEM_SPEC], [],
        flops, 4_000_000, 14,
    )(place, frames, spare, weight_two, pre_act)
    both_mate = swap(both)

    *parts, both = call(
        gradient_kernel, "weight_grads", [rows64] * 3 + [rows32] * 2 + [pair],
        [SMEM_SPEC] + [VMEM_SPEC] * 3 + [ANY_SPEC], [VMEM_SPEC] * 5 + [ANY_SPEC],
        [pltpu.VMEM((2, CH, ROWS), BF16), pltpu.VMEM((27, CH, CH), BF16)],
        2 * flops, 10_000_000, 18, {4: 5},
    )(place, both, both_mate, frames, both)

    def rounds(arrays, axis):
        return [arrays[0]] + [ring_send(arrays[d], axis, d) for d in (1, 2, 3)]

    own, to_after, to_before, kept, given = parts
    across = kept.astype(F32) + ring_send(given, first, 0, pairing).astype(F32)
    arrived = [
        own,
        ring_send(to_after, first, 1),
        ring_send(to_before, first, 3),
        ring_send(across.astype(BF16), first, 2),
    ]
    quarter = call(
        scatter_kernel, "sum_and_split", [rows16] * 4, [SMEM_SPEC] + [VMEM_SPEC] * 4, [VMEM_SPEC] * 4,
        [], 4_000_000, 4_500_000, 12,
    )(place, *arrived)

    (skins,) = call(
        pack_both_kernel, "pack_both", [skin], [VMEM_SPEC, ANY_SPEC], [VMEM_SPEC], [], 1000, 1_000_000, 8,
    )(both, quarter[0])
    before, after = sent_halo(skins)
    mate_before, mate_after = swap(before), swap(after)
    skins_mate = swap(skins)
    def added(arrays):
        wide = [array.astype(F32) for array in arrays]
        return (wide[0] + wide[2]) + (wide[1] + wide[3])

    small = added(rounds(quarter, second)).astype(BF16)
    scale = float(128 * ROWS) ** (-0.5)
    whole = (scale * added(rounds([small] * 4, third))).astype(BF16)

    wide, again, half, both = call(
        gather_kernel, "gather_rows", [rows64] * 2 + [rows32, pair],
        [SMEM_SPEC] + [VMEM_SPEC] * 4 + [ANY_SPEC], [VMEM_SPEC] * 3 + [ANY_SPEC], [],
        1000, 2_700_000, 12, {5: 3},
    )(place, *rounds([whole] * 4, second), both)
    half = ring_send(half, first, 2)
    other_half = ring_send(half, first, 0, pairing)
    from_before, from_after = ring_send(wide, first, 1), ring_send(wide, first, 3)
    output, grad_input, again = call(
        outer_kernel, "outer_convs", [(1, ROWS, CH)] * 2 + [rows64],
        [SMEM_SPEC] + [ANY_SPEC] * 8 + [HBM_SPEC] * 2 + [ANY_SPEC], [VMEM_SPEC] * 2 + [ANY_SPEC],
        [frame, full, packed, held, sems], 2 * flops, 12_000_000, 18, {11: 2},
    )(picks, both, both_mate, skins, before, after, skins_mate, mate_before, mate_after, weight_two, weight_one, again)
    early = [(0, 0), (2, 0)]
    late = [(3, 0), (1, 0), (2, 1)]
    grad_one, grad_two = call(
        partial(place_kernel, early), "place_early", [(27, CH, CH)] * 2,
        [SMEM_SPEC] + [VMEM_SPEC] * 4, [ANY_SPEC] * 2,
        [pltpu.SemaphoreType.DMA((2, 2))], 1000, 5_000_000, 12,
    )(place, wide, half, swap(again), swap(half))
    chunks = [from_before, from_after, other_half]
    grad_one, grad_two = call(
        partial(place_kernel, late), "place_late", [(27, CH, CH)] * 2,
        [SMEM_SPEC] + [VMEM_SPEC] * 6 + [ANY_SPEC] * 2, [ANY_SPEC] * 2,
        [pltpu.SemaphoreType.DMA((2, 3))], 1000, 9_000_000, 12, {7: 0, 8: 1},
    )(place, *chunks, *[swap(chunk) for chunk in chunks], grad_one, grad_two)
    return output, grad_input, grad_one, grad_two


def solution(mesh):
    by_brick = P(AXES, None, None)
    in_specs = (by_brick, by_brick, P(), P(), P(AXES), P(AXES, None), P(AXES, None))
    out_specs = (by_brick, by_brick, P(), P())
    return jax.shard_map(
        on_device, mesh=mesh, in_specs=in_specs, out_specs=out_specs, check_vma=False
    )
```

time: 150 us -> 139 us (0.927)
  waiting for transfers between devices: 54.5 us -> 38 us
  local copies, waits for them, and re-layouts: 1.25 us -> 4.18 us
  Pallas kernels: 30.8 us -> 32.9 us
    ppermute x15 -> x17, starting transfers between devices: 27.6 us -> 38.7 us  [ring_send(): return lax.ppermute(array, AXES, pairs)]
    ppermute x11 -> x14, starting transfers between devices: 19.6 us -> 8.88 us  [swap(): lax.ppermute(array, AXES, [(index, index ^ 1) for index in range(128)])]
    ppermute x4, waiting for transfers between devices: 11.3 us -> 0.62 us  [shifted(): lax.ppermute(array, AXES, [(i, i + by) for i in range(128) if 0 <= i + by...]
    ppermute x11 -> x14, waiting for transfers between devices: 8.25 us -> 4.04 us  [swap(): lax.ppermute(array, AXES, [(index, index ^ 1) for index in range(128)])]
    ppermute x15 -> x17, waiting for transfers between devices: 34.9 us -> 33.3 us  [ring_send(): return lax.ppermute(array, AXES, pairs)]
    pallas_call x5 -> x6, Pallas kernels: 11.2 us -> 12.8 us  [the longest x1 5.06 us: on_device(): call(gradient_kernel, 'weight_grads', [rows64] * 3 + [rows32] * 2 + [pair...]
  transfers between devices with their start and end apart: 30 -> 35, of which waited for: 16 -> 14; matrix products, arithmetic and copies ran while one was open for 1% -> 3% of each run, Pallas kernels for 7% -> 10%
where the time goes in v3:
time: 139 us; the launch traced here: 138 us
  starting transfers between devices  59.4 us (43%)
  waiting for transfers between devices  38 us (27%)
  Pallas kernels  32.9 us (24%)
  local copies, waits for them, and re-layouts  4.18 us (3%)
  other arithmetic  2.1 us (2%)
  between operations  1.7 us (1%)
    ppermute x17, starting transfers between devices, ring_send(): return lax.ppermute(array, AXES, pairs)  38.7 us
    ppermute x17, waiting for transfers between devices, ring_send(): return lax.ppermute(array, AXES, pairs)  33.3 us
    ppermute x4, starting transfers between devices, shifted(): lax.ppermute(array, AXES, [(i, i + by) for i in range(128) if 0 <= i + by...  11.8 us
    pallas_call x1, Pallas kernels, on_device(): call(outer_kernel, 'outer_convs', [(1, ROWS, CH)] * 2 + [rows64], [SMEM_S...  10.8 us
    ppermute x14, starting transfers between devices, swap(): lax.ppermute(array, AXES, [(index, index ^ 1) for index in range(128)])  8.88 us
    pallas_call x1, Pallas kernels, on_device(): call(gradient_kernel, 'weight_grads', [rows64] * 3 + [rows32] * 2 + [pair...  5.06 us
    ppermute x14, waiting for transfers between devices, swap(): lax.ppermute(array, AXES, [(index, index ^ 1) for index in range(128)])  4.04 us
    pallas_call x1, Pallas kernels, on_device(): call(frames_kernel, 'build_frames', [(2 * FRAME_ROWS, TAPS), (FRAME_ROWS,...  3.08 us
  transfers between devices with their start and end apart: 35, of which 14 were waited for; matrix products, arithmetic and copies ran while one was open for 3% of the time, Pallas kernels for 10%

profile of v3, /device:TPU:1, one launch (start us, length us, event | category | flops | bytes accessed | tf_op | source)
XLA Modules:
  0.0 138.3 jit_solution(6485970201422178172)
XLA Ops:
  0.6 2.1 %pack_fields.1 = (bf16[2,512,256]{2,1,0:T(8,128)(2,1)}, bf16[2,320,256]{2,1,0:T(8,128)(2,1)}) custom-call(bf16[1,512,256]{2,1,0:T(8,128)(2,1)} %features.1, bf16[1,512,256]{2,1,0:T(8,128)(2,1)} %cotangent.1), custom_call_target="tpu_custom_call" | custom-call | flops 1000 | bytes 1000000 | tf_op jit(solution)/shard_map/pack_fields/pallas_call | solution.py:385
  2.8 1.4 %collective-permute-start.4 = (bf16[2,320,256]{2,1,0:T(8,128)(2,1)}, bf16[2,320,256]{2,1,0:T(8,128)(2,1)}, u32[]{:S(2)}, u32[]{:S(2)}) collective-permute-start(bf16[2,320,256]{2,1,0:T(8,128)(2,1)} %get-tuple-element.30.packed_own), channel_id=1, source_target_pairs={{0,1},{1,0},{2,3},{3,2},{4,5},{5,4},{6,7},{7,6},{8,9},{9,8},{10,11... | collective-permute-start | bytes 983048 | tf_op jit(solution)/shard_map/ppermute | solution.py:48
  5.5 4.7 %collective-permute-start.2 = (bf16[2,320,256]{2,1,0:T(8,128)(2,1)}, bf16[2,320,256]{2,1,0:T(8,128)(2,1)}, u32[]{:S(2)}, u32[]{:S(2)}) collective-permute-start(bf16[2,320,256]{2,1,0:T(8,128)(2,1)} %get-tuple-element.30.packed_own), channel_id=1, source_target_pairs={{0,2},{1,3},{2,4},{3,5},{4,6},{5,7},{6,8},{7,9},{8,10},{9,11},{10,... | collective-permute-start | bytes 983048 | tf_op jit(solution)/shard_map/ppermute | solution.py:52
  13.0 1.4 stack.43.place_ref
  21.2 3.1 %build_frames.1 = (bf16[1280,2304]{1,0:T(8,128)(2,1)S(1)}, bf16[640,2304]{1,0:T(8,128)(2,1)S(1)}) custom-call(s32[2,27]{1,0:T(2,128)S(1)} %compare_select_fusion.3.pick_ref, s32[6]{0:T(128)S(1)} %stack.43.place_ref, bf16[2,512,256]{2,1,0:T(8,128)(2,1)S(1)} %copy-done.2, bf16[2,512,256]{2,1,0:T(8,128)(2,1)} %collective-permute-done.1.mate, ...), custom_call_target="tpu_custom_call" | custom-call | flops 1000000 | bytes 12000000 | tf_op jit(solution)/shard_map/build_frames/pallas_call | solution.py:389
  24.3 2.6 %first_conv.1.pre_act_ref = f32[512,256]{1,0:T(8,128)S(1)} custom-call(s32[6]{0:T(128)S(1)} %stack.43.place_ref, bf16[1280,2304]{1,0:T(8,128)(2,1)S(1)} %get-tuple-element.31.frames, bf16[640,2304]{1,0:T(8,128)(2,1)S(1)} %get-tuple-element.32.spare, bf16[27,256,256]{2,1,0:T(8,128)(2,1)S(1)} %copy-done), custom_call_target="tpu_custom_call" | custom-call | flops 1811939328 | bytes 4000000 | tf_op jit(solution)/shard_map/first_conv/pallas_call | solution.py:393
  26.9 2.6 %grad_conv.1.both = bf16[2,512,256]{2,1,0:T(8,128)(2,1)S(1)} custom-call(s32[6]{0:T(128)S(1)} %stack.43.place_ref, bf16[1280,2304]{1,0:T(8,128)(2,1)S(1)} %get-tuple-element.31.frames, bf16[640,2304]{1,0:T(8,128)(2,1)S(1)} %get-tuple-element.32.spare, bf16[27,256,256]{2,1,0:T(8,128)(2,1)S(1)} %copy-done.1, f32[512,256]{1,0:T(8,128)S(1)} %first_conv.1.pre_act_ref), custom_call_target="tpu_custom_call" | custom-call | flops 1811939328 | bytes 4000000 | tf_op jit(solution)/shard_map/grad_conv/pallas_call | solution.py:397
  30.0 1.5 %collective-permute-done.7.both_mate.mate = bf16[2,512,256]{2,1,0:T(8,128)(2,1)S(1)} collective-permute-done((bf16[2,512,256]{2,1,0:T(8,128)(2,1)S(1)}, bf16[2,512,256]{2,1,0:T(8,128)(2,1)S(1)}, u32[]{:S(2)}, u32[]{:S(2)}) %collective-permute-start.7) | collective-permute-done | bytes 524320 | tf_op jit(solution)/shard_map/ppermute | solution.py:48
  31.5 5.1 %weight_grads.1 = (bf16[27,64,256]{2,1,0:T(8,128)(2,1)S(1)}, bf16[27,64,256]{2,1,0:T(8,128)(2,1)S(1)}, bf16[27,64,256]{2,1,0:T(8,128)(2,1)S(1)}, bf16[27,32,256]...) custom-call(s32[6]{0:T(128)S(1)} %stack.43.place_ref, ...), custom_call_target="tpu_custom_call", output_to_operand_aliasing={{5}: (4, {})} | custom-call | flops 3623878656 | bytes 10000000 | tf_op jit(solution)/shard_map/weight_grads/pallas_call | solution.py:403
  36.5 5.0 %collective-permute-start.10 = (bf16[27,32,256]{2,1,0:T(8,128)(2,1)S(1)}, bf16[27,32,256]{2,1,0:T(8,128)(2,1)S(1)}, u32[]{:S(2)}, u32[]{:S(2)}) collective-permute-start(bf16[27,32,256]{2,1,0:T(8,128)(2,1)S(1)} %get-tuple-element.37), channel_id=1, source_target_pairs={{0,2},{1,7},{2,0},{3,5},{4,6},{5,3},{6,4},{7,1},{8,10},{9,15},{10,... | collective-permute-start | bytes 1327112 | tf_op jit(solution)/shard_map/ppermute | solution.py:44
  41.5 2.0 %collective-permute-start.8 = (bf16[27,64,256]{2,1,0:T(8,128)(2,1)S(1)}, bf16[27,64,256]{2,1,0:T(8,128)(2,1)S(1)}, u32[]{:S(2)}, u32[]{:S(2)}) collective-permute-start(bf16[27,64,256]{2,1,0:T(8,128)(2,1)S(1)} %get-tuple-element.34), channel_id=1, source_target_pairs={{0,32},{1,9},{2,34},{3,11},{4,36},{5,13},{6,38},{7,15},{8,40},{9,1... | collective-permute-start | bytes 2654216 | tf_op jit(solution)/shard_map/ppermute | solution.py:44
  43.5 3.9 %collective-permute-start.9 = (bf16[27,64,256]{2,1,0:T(8,128)(2,1)S(1)}, bf16[27,64,256]{2,1,0:T(8,128)(2,1)S(1)}, u32[]{:S(2)}, u32[]{:S(2)}) collective-permute-start(bf16[27,64,256]{2,1,0:T(8,128)(2,1)S(1)} %get-tuple-element.35), channel_id=1, source_target_pairs={{0,96},{1,25},{2,98},{3,27},{4,100},{5,29},{6,102},{7,31},{8,104},... | collective-permute-start | bytes 2654216 | tf_op jit(solution)/shard_map/ppermute | solution.py:44
  47.6 6.7 %collective-permute-start.11 = (bf16[27,32,256]{2,1,0:T(8,128)(2,1)S(1)}, bf16[27,32,256]{2,1,0:T(8,128)(2,1)S(1)}, u32[]{:S(2)}, u32[]{:S(2)}) collective-permute-start(bf16[27,32,256]{2,1,0:T(8,128)(2,1)S(1)} %add_convert_fusion), channel_id=1, source_target_pairs={{0,64},{1,17},{2,66},{3,19},{4,68},{5,21},{6,70},{7,23},{8,72},{9,... | collective-permute-start | bytes 1327112 | tf_op jit(solution)/shard_map/ppermute | solution.py:44
  54.3 9.7 %collective-permute-done.11.across = bf16[27,32,256]{2,1,0:T(8,128)(2,1)S(1)} collective-permute-done((bf16[27,32,256]{2,1,0:T(8,128)(2,1)S(1)}, bf16[27,32,256]{2,1,0:T(8,128)(2,1)S(1)}, u32[]{:S(2)}, u32[]{:S(2)}) %collective-permute-start.11) | collective-permute-done | bytes 442400 | tf_op jit(solution)/shard_map/ppermute | solution.py:44
  65.2 1.4 %collective-permute-start.13 = (bf16[27,16,256]{2,1,0:T(8,128)(2,1)S(1)}, bf16[27,16,256]{2,1,0:T(8,128)(2,1)S(1)}, u32[]{:S(2)}, u32[]{:S(2)}) collective-permute-start(bf16[27,16,256]{2,1,0:T(8,128)(2,1)S(1)} %get-tuple-element.40), channel_id=1, source_target_pairs={{0,8},{1,3},{2,10},{3,5},{4,12},{5,7},{6,14},{7,1},{8,16},{9,11},{... | collective-permute-start | bytes 663560 | tf_op jit(solution)/shard_map/ppermute | solution.py:44
  66.6 1.3 collective-permute-start.14
  68.0 3.6 %collective-permute-done.12 = bf16[27,16,256]{2,1,0:T(8,128)(2,1)S(1)} collective-permute-done((bf16[27,16,256]{2,1,0:T(8,128)(2,1)S(1)}, bf16[27,16,256]{2,1,0:T(8,128)(2,1)S(1)}, u32[]{:S(2)}, u32[]{:S(2)}) %collective-permute-start.12) | collective-permute-done | bytes 221216 | tf_op jit(solution)/shard_map/ppermute | solution.py:44
  71.6 2.1 %collective-permute-done.13 = bf16[27,16,256]{2,1,0:T(8,128)(2,1)S(1)} collective-permute-done((bf16[27,16,256]{2,1,0:T(8,128)(2,1)S(1)}, bf16[27,16,256]{2,1,0:T(8,128)(2,1)S(1)}, u32[]{:S(2)}, u32[]{:S(2)}) %collective-permute-start.13) | collective-permute-done | bytes 221216 | tf_op jit(solution)/shard_map/ppermute | solution.py:44
  73.8 8.1 %collective-permute-start.17 = (bf16[27,16,256]{2,1,0:T(8,128)(2,1)S(1)}, bf16[27,16,256]{2,1,0:T(8,128)(2,1)S(1)}, u32[]{:S(2)}, u32[]{:S(2)}) collective-permute-start(bf16[27,16,256]{2,1,0:T(8,128)(2,1)S(1)} %add_convert_fusion.1), channel_id=1, source_target_pairs={{0,6},{1,97},{2,0},{3,99},{4,2},{5,101},{6,4},{7,103},{8,14},{9,10... | collective-permute-start | bytes 663560 | tf_op jit(solution)/shard_map/ppermute | solution.py:44
  81.9 2.5 %collective-permute-start.15 = (bf16[27,16,256]{2,1,0:T(8,128)(2,1)S(1)}, bf16[27,16,256]{2,1,0:T(8,128)(2,1)S(1)}, u32[]{:S(2)}, u32[]{:S(2)}) collective-permute-start(bf16[27,16,256]{2,1,0:T(8,128)(2,1)S(1)} %add_convert_fusion.1), channel_id=1, source_target_pairs={{0,4},{1,65},{2,6},{3,67},{4,0},{5,69},{6,2},{7,71},{8,12},{9,73},... | collective-permute-start | bytes 663560 | tf_op jit(solution)/shard_map/ppermute | solution.py:44
  84.8 5.5 %collective-permute-done.16 = bf16[27,16,256]{2,1,0:T(8,128)(2,1)S(1)} collective-permute-done((bf16[27,16,256]{2,1,0:T(8,128)(2,1)S(1)}, bf16[27,16,256]{2,1,0:T(8,128)(2,1)S(1)}, u32[]{:S(2)}, u32[]{:S(2)}) %collective-permute-start.16) | collective-permute-done | bytes 221216 | tf_op jit(solution)/shard_map/ppermute | solution.py:44
  90.4 3.3 %collective-permute-start.20 = (bf16[27,16,256]{2,1,0:T(8,128)(2,1)S(1)}, bf16[27,16,256]{2,1,0:T(8,128)(2,1)S(1)}, u32[]{:S(2)}, u32[]{:S(2)}) collective-permute-start(bf16[27,16,256]{2,1,0:T(8,128)(2,1)S(1)} %multiply_convert_fusion.part0), channel_id=1, source_target_pairs={{0,24},{1,7},{2,26},{3,1},{4,28},{5,3},{6,30},{7,5},{8,0},{9,15},{... | collective-permute-start | bytes 663560 | tf_op jit(solution)/shard_map/ppermute | solution.py:44
  94.4 1.3 collective-permute-start.22
  95.7 4.5 %collective-permute-start.21 = (bf16[2,320,256]{2,1,0:T(8,128)(2,1)S(1)}, bf16[2,320,256]{2,1,0:T(8,128)(2,1)S(1)}, u32[]{:S(2)}, u32[]{:S(2)}) collective-permute-start(bf16[2,320,256]{2,1,0:T(8,128)(2,1)S(1)} %pack_both.1.packed_own), channel_id=1, source_target_pairs={{0,2},{1,3},{2,4},{3,5},{4,6},{5,7},{6,8},{7,9},{8,10},{9,11},{10,... | collective-permute-start | bytes 983048 | tf_op jit(solution)/shard_map/ppermute | solution.py:52
  100.3 5.6 %collective-permute-done.20.part3 = bf16[27,16,256]{2,1,0:T(8,128)(2,1)S(1)} collective-permute-done((bf16[27,16,256]{2,1,0:T(8,128)(2,1)S(1)}, bf16[27,16,256]{2,1,0:T(8,128)(2,1)S(1)}, u32[]{:S(2)}, u32[]{:S(2)}) %collective-permute-start.20) | collective-permute-done | bytes 221216 | tf_op jit(solution)/shard_map/ppermute | solution.py:44
  106.7 1.5 %collective-permute-start.26 = (bf16[27,64,256]{2,1,0:T(8,128)(2,1)S(1)}, bf16[27,64,256]{2,1,0:T(8,128)(2,1)S(1)}, u32[]{:S(2)}, u32[]{:S(2)}) collective-permute-start(bf16[27,64,256]{2,1,0:T(8,128)(2,1)S(1)} %get-tuple-element.47.refs_0_), channel_id=1, source_target_pairs={{0,32},{1,9},{2,34},{3,11},{4,36},{5,13},{6,38},{7,15},{8,40},{9,1... | collective-permute-start | bytes 2654216 | tf_op jit(solution)/shard_map/ppermute | solution.py:44
  110.8 10.8 %outer_convs.1 = (bf16[1,512,256]{2,1,0:T(8,128)(2,1)}, bf16[1,512,256]{2,1,0:T(8,128)(2,1)}, bf16[27,64,256]{2,1,0:T(8,128)(2,1)S(1)}) custom-call(s32[2,27]{1,0:T(2,128)S(1)} %compare_select_fusion.3.pick_ref, bf16[2,512,256]{2,1,0:T(8,128)(2,1)S(1)} %get-tuple-element.43.own, ...), custom_call_target="tpu_custom_call", output_to_operand_aliasing={{2}: (11, {})} | custom-call | flops 3623878656 | bytes 12000000 | tf_op jit(solution)/shard_map/outer_convs/pallas_call | solution.py:448
  121.6 3.3 %collective-permute-start.33 = (bf16[27,64,256]{2,1,0:T(8,128)(2,1)S(1)}, bf16[27,64,256]{2,1,0:T(8,128)(2,1)S(1)}, u32[]{:S(2)}, u32[]{:S(2)}) collective-permute-start(bf16[27,64,256]{2,1,0:T(8,128)(2,1)S(1)} %get-tuple-element.49), channel_id=1, source_target_pairs={{0,1},{1,0},{2,3},{3,2},{4,5},{5,4},{6,7},{7,6},{8,9},{9,8},{10,11... | collective-permute-start | bytes 2654216 | tf_op jit(solution)/shard_map/ppermute | solution.py:48
  124.9 1.4 %collective-permute-start.29 = (bf16[27,32,256]{2,1,0:T(8,128)(2,1)S(1)}, bf16[27,32,256]{2,1,0:T(8,128)(2,1)S(1)}, u32[]{:S(2)}, u32[]{:S(2)}) collective-permute-start(bf16[27,32,256]{2,1,0:T(8,128)(2,1)S(1)} %collective-permute-done.28.refs_1_), channel_id=1, source_target_pairs={{0,2},{1,7},{2,0},{3,5},{4,6},{5,3},{6,4},{7,1},{8,10},{9,15},{10,... | collective-permute-start | bytes 1327112 | tf_op jit(solution)/shard_map/ppermute | solution.py:44
  126.9 6.3 %collective-permute-done.29.refs_2_ = bf16[27,32,256]{2,1,0:T(8,128)(2,1)S(1)} collective-permute-done((bf16[27,32,256]{2,1,0:T(8,128)(2,1)S(1)}, bf16[27,32,256]{2,1,0:T(8,128)(2,1)S(1)}, u32[]{:S(2)}, u32[]{:S(2)}) %collective-permute-start.29) | collective-permute-done | bytes 442400 | tf_op jit(solution)/shard_map/ppermute | solution.py:44
  133.3 2.1 %place_early.1 = (bf16[27,256,256]{2,1,0:T(8,128)(2,1)}, bf16[27,256,256]{2,1,0:T(8,128)(2,1)}) custom-call(s32[6]{0:T(128)S(1)} %stack.43.place_ref, bf16[27,64,256]{2,1,0:T(8,128)(2,1)S(1)} %get-tuple-element.47.refs_0_, bf16[27,32,256]{2,1,0:T(8,128)(2,1)S(1)} %collective-permute-done.28.refs_1_, ...), custom_call_target="tpu_custom_call" | custom-call | flops 1000 | bytes 5000000 | tf_op jit(solution)/shard_map/place_early/pallas_call | solution.py:455
  135.5 2.7 %place_late.1 = (bf16[27,256,256]{2,1,0:T(8,128)(2,1)}, bf16[27,256,256]{2,1,0:T(8,128)(2,1)}) custom-call(s32[6]{0:T(128)S(1)} %stack.43.place_ref, bf16[27,64,256]{2,1,0:T(8,128)(2,1)S(1)} %collective-permute-done.26.refs_0_, bf16[27,64,256]{2,1,0:T(8,128)(2,1)S(1)} %collective-permute-done.27.refs_1_, ...), custom_call_target="tpu_custom_call", output_to_operand_aliasing={{0}: (7, {}), {1}: (8, {})} | custom-call | flops 1000 | bytes 9000000 | tf_op jit(solution)/shard_map/place_late/pallas_call | solution.py:461
  (71 shorter events, 17.5 us)
Async XLA Ops:
  2.8 15.0 %collective-permute-start.4 = (bf16[2,320,256]{2,1,0:T(8,128)(2,1)}, bf16[2,320,256]{2,1,0:T(8,128)(2,1)}, u32[]{:S(2)}, u32[]{:S(2)}) collective-permute-start(bf16[2,320,256]{2,1,0:T(8,128)(2,1)} %get-tuple-element.30.packed_own), channel_id=1, source_target_pairs={{0,1},{1,0},{2,3},{3,2},{4,5},{5,4},{6,7},{7,6},{8,9},{9,8},{10,11... | collective-permute-start | bytes 983048 | tf_op jit(solution)/shard_map/ppermute | solution.py:48
  4.2 11.5 %collective-permute-start.3 = (bf16[2,320,256]{2,1,0:T(8,128)(2,1)}, bf16[2,320,256]{2,1,0:T(8,128)(2,1)}, u32[]{:S(2)}, u32[]{:S(2)}) collective-permute-start(bf16[2,320,256]{2,1,0:T(8,128)(2,1)} %get-tuple-element.30.packed_own), channel_id=1, source_target_pairs={{2,0},{3,1},{4,2},{5,3},{6,4},{7,5},{8,6},{9,7},{10,8},{11,9},{12,... | collective-permute-start | bytes 983048 | tf_op jit(solution)/shard_map/ppermute | solution.py:52
  5.5 11.1 %collective-permute-start.2 = (bf16[2,320,256]{2,1,0:T(8,128)(2,1)}, bf16[2,320,256]{2,1,0:T(8,128)(2,1)}, u32[]{:S(2)}, u32[]{:S(2)}) collective-permute-start(bf16[2,320,256]{2,1,0:T(8,128)(2,1)} %get-tuple-element.30.packed_own), channel_id=1, source_target_pairs={{0,2},{1,3},{2,4},{3,5},{4,6},{5,7},{6,8},{7,9},{8,10},{9,11},{10,... | collective-permute-start | bytes 983048 | tf_op jit(solution)/shard_map/ppermute | solution.py:52
  11.6 2.8 %collective-permute-start = (s32[1,27]{1,0:T(1,128)S(1)}, s32[1,27]{1,0:T(1,128)S(1)}, u32[]{:S(2)}, u32[]{:S(2)}) collective-permute-start(s32[1,27]{1,0:T(1,128)S(1)} %pad_add_fusion.2), channel_id=1, source_target_pairs={{0,1},{1,0},{2,3},{3,2},{4,5},{5,4},{6,7},{7,6},{8,9},{9,8},{10,11... | collective-permute-start | bytes 332 | tf_op jit(solution)/shard_map/ppermute | solution.py:48
  12.2 5.6 %collective-permute-start.1 = (bf16[2,512,256]{2,1,0:T(8,128)(2,1)}, bf16[2,512,256]{2,1,0:T(8,128)(2,1)}, u32[]{:S(2)}, u32[]{:S(2)}) collective-permute-start(bf16[2,512,256]{2,1,0:T(8,128)(2,1)} %get-tuple-element.29.own), channel_id=1, source_target_pairs={{0,1},{1,0},{2,3},{3,2},{4,5},{5,4},{6,7},{7,6},{8,9},{9,8},{10,11... | collective-permute-start | bytes 1572872 | tf_op jit(solution)/shard_map/ppermute | solution.py:48
  15.7 2.3 %collective-permute-start.6 = (bf16[2,320,256]{2,1,0:T(8,128)(2,1)}, bf16[2,320,256]{2,1,0:T(8,128)(2,1)S(1)}, u32[]{:S(2)}, u32[]{:S(2)}) collective-permute-start(bf16[2,320,256]{2,1,0:T(8,128)(2,1)} %collective-permute-done.3.after), channel_id=1, source_target_pairs={{0,1},{1,0},{2,3},{3,2},{4,5},{5,4},{6,7},{7,6},{8,9},{9,8},{10,11... | collective-permute-start | bytes 983048 | tf_op jit(solution)/shard_map/ppermute | solution.py:48
  16.6 2.6 %collective-permute-start.5 = (bf16[2,320,256]{2,1,0:T(8,128)(2,1)}, bf16[2,320,256]{2,1,0:T(8,128)(2,1)S(1)}, u32[]{:S(2)}, u32[]{:S(2)}) collective-permute-start(bf16[2,320,256]{2,1,0:T(8,128)(2,1)} %collective-permute-done.2.before), channel_id=1, source_target_pairs={{0,1},{1,0},{2,3},{3,2},{4,5},{5,4},{6,7},{7,6},{8,9},{9,8},{10,11... | collective-permute-start | bytes 983048 | tf_op jit(solution)/shard_map/ppermute | solution.py:48
  36.5 10.9 %collective-permute-start.10 = (bf16[27,32,256]{2,1,0:T(8,128)(2,1)S(1)}, bf16[27,32,256]{2,1,0:T(8,128)(2,1)S(1)}, u32[]{:S(2)}, u32[]{:S(2)}) collective-permute-start(bf16[27,32,256]{2,1,0:T(8,128)(2,1)S(1)} %get-tuple-element.37), channel_id=1, source_target_pairs={{0,2},{1,7},{2,0},{3,5},{4,6},{5,3},{6,4},{7,1},{8,10},{9,15},{10,... | collective-permute-start | bytes 1327112 | tf_op jit(solution)/shard_map/ppermute | solution.py:44
  41.5 22.5 %collective-permute-start.8 = (bf16[27,64,256]{2,1,0:T(8,128)(2,1)S(1)}, bf16[27,64,256]{2,1,0:T(8,128)(2,1)S(1)}, u32[]{:S(2)}, u32[]{:S(2)}) collective-permute-start(bf16[27,64,256]{2,1,0:T(8,128)(2,1)S(1)} %get-tuple-element.34), channel_id=1, source_target_pairs={{0,32},{1,9},{2,34},{3,11},{4,36},{5,13},{6,38},{7,15},{8,40},{9,1... | collective-permute-start | bytes 2654216 | tf_op jit(solution)/shard_map/ppermute | solution.py:44
  43.5 20.5 %collective-permute-start.9 = (bf16[27,64,256]{2,1,0:T(8,128)(2,1)S(1)}, bf16[27,64,256]{2,1,0:T(8,128)(2,1)S(1)}, u32[]{:S(2)}, u32[]{:S(2)}) collective-permute-start(bf16[27,64,256]{2,1,0:T(8,128)(2,1)S(1)} %get-tuple-element.35), channel_id=1, source_target_pairs={{0,96},{1,25},{2,98},{3,27},{4,100},{5,29},{6,102},{7,31},{8,104},... | collective-permute-start | bytes 2654216 | tf_op jit(solution)/shard_map/ppermute | solution.py:44
  47.6 16.5 %collective-permute-start.11 = (bf16[27,32,256]{2,1,0:T(8,128)(2,1)S(1)}, bf16[27,32,256]{2,1,0:T(8,128)(2,1)S(1)}, u32[]{:S(2)}, u32[]{:S(2)}) collective-permute-start(bf16[27,32,256]{2,1,0:T(8,128)(2,1)S(1)} %add_convert_fusion), channel_id=1, source_target_pairs={{0,64},{1,17},{2,66},{3,19},{4,68},{5,21},{6,70},{7,23},{8,72},{9,... | collective-permute-start | bytes 1327112 | tf_op jit(solution)/shard_map/ppermute | solution.py:44
  65.1 6.5 %collective-permute-start.12 = (bf16[27,16,256]{2,1,0:T(8,128)(2,1)S(1)}, bf16[27,16,256]{2,1,0:T(8,128)(2,1)S(1)}, u32[]{:S(2)}, u32[]{:S(2)}) collective-permute-start(bf16[27,16,256]{2,1,0:T(8,128)(2,1)S(1)} %get-tuple-element.39), channel_id=1, source_target_pairs={{0,16},{1,5},{2,18},{3,7},{4,20},{5,1},{6,22},{7,3},{8,24},{9,13},... | collective-permute-start | bytes 663560 | tf_op jit(solution)/shard_map/ppermute | solution.py:44
  65.2 8.4 %collective-permute-start.13 = (bf16[27,16,256]{2,1,0:T(8,128)(2,1)S(1)}, bf16[27,16,256]{2,1,0:T(8,128)(2,1)S(1)}, u32[]{:S(2)}, u32[]{:S(2)}) collective-permute-start(bf16[27,16,256]{2,1,0:T(8,128)(2,1)S(1)} %get-tuple-element.40), channel_id=1, source_target_pairs={{0,8},{1,3},{2,10},{3,5},{4,12},{5,7},{6,14},{7,1},{8,16},{9,11},{... | collective-permute-start | bytes 663560 | tf_op jit(solution)/shard_map/ppermute | solution.py:44
  66.6 7.0 %collective-permute-start.14 = (bf16[27,16,256]{2,1,0:T(8,128)(2,1)S(1)}, bf16[27,16,256]{2,1,0:T(8,128)(2,1)S(1)}, u32[]{:S(2)}, u32[]{:S(2)}) collective-permute-start(bf16[27,16,256]{2,1,0:T(8,128)(2,1)S(1)} %get-tuple-element.41), channel_id=1, source_target_pairs={{0,24},{1,7},{2,26},{3,1},{4,28},{5,3},{6,30},{7,5},{8,0},{9,15},{... | collective-permute-start | bytes 663560 | tf_op jit(solution)/shard_map/ppermute | solution.py:44
  73.8 11.0 %collective-permute-start.17 = (bf16[27,16,256]{2,1,0:T(8,128)(2,1)S(1)}, bf16[27,16,256]{2,1,0:T(8,128)(2,1)S(1)}, u32[]{:S(2)}, u32[]{:S(2)}) collective-permute-start(bf16[27,16,256]{2,1,0:T(8,128)(2,1)S(1)} %add_convert_fusion.1), channel_id=1, source_target_pairs={{0,6},{1,97},{2,0},{3,99},{4,2},{5,101},{6,4},{7,103},{8,14},{9,10... | collective-permute-start | bytes 663560 | tf_op jit(solution)/shard_map/ppermute | solution.py:44
  81.9 8.4 %collective-permute-start.16 = (bf16[27,16,256]{2,1,0:T(8,128)(2,1)S(1)}, bf16[27,16,256]{2,1,0:T(8,128)(2,1)S(1)}, u32[]{:S(2)}, u32[]{:S(2)}) collective-permute-start(bf16[27,16,256]{2,1,0:T(8,128)(2,1)S(1)} %add_convert_fusion.1), channel_id=1, source_target_pairs={{0,2},{1,33},{2,4},{3,35},{4,6},{5,37},{6,0},{7,39},{8,10},{9,41},... | collective-permute-start | bytes 663560 | tf_op jit(solution)/shard_map/ppermute | solution.py:44
  81.9 8.4 %collective-permute-start.15 = (bf16[27,16,256]{2,1,0:T(8,128)(2,1)S(1)}, bf16[27,16,256]{2,1,0:T(8,128)(2,1)S(1)}, u32[]{:S(2)}, u32[]{:S(2)}) collective-permute-start(bf16[27,16,256]{2,1,0:T(8,128)(2,1)S(1)} %add_convert_fusion.1), channel_id=1, source_target_pairs={{0,4},{1,65},{2,6},{3,67},{4,0},{5,69},{6,2},{7,71},{8,12},{9,73},... | collective-permute-start | bytes 663560 | tf_op jit(solution)/shard_map/ppermute | solution.py:44
  90.4 15.5 %collective-permute-start.20 = (bf16[27,16,256]{2,1,0:T(8,128)(2,1)S(1)}, bf16[27,16,256]{2,1,0:T(8,128)(2,1)S(1)}, u32[]{:S(2)}, u32[]{:S(2)}) collective-permute-start(bf16[27,16,256]{2,1,0:T(8,128)(2,1)S(1)} %multiply_convert_fusion.part0), channel_id=1, source_target_pairs={{0,24},{1,7},{2,26},{3,1},{4,28},{5,3},{6,30},{7,5},{8,0},{9,15},{... | collective-permute-start | bytes 663560 | tf_op jit(solution)/shard_map/ppermute | solution.py:44
  93.6 12.3 %collective-permute-start.19 = (bf16[27,16,256]{2,1,0:T(8,128)(2,1)S(1)}, bf16[27,16,256]{2,1,0:T(8,128)(2,1)S(1)}, u32[]{:S(2)}, u32[]{:S(2)}) collective-permute-start(bf16[27,16,256]{2,1,0:T(8,128)(2,1)S(1)} %multiply_convert_fusion.part0), channel_id=1, source_target_pairs={{0,16},{1,5},{2,18},{3,7},{4,20},{5,1},{6,22},{7,3},{8,24},{9,13},... | collective-permute-start | bytes 663560 | tf_op jit(solution)/shard_map/ppermute | solution.py:44
  93.6 12.3 %collective-permute-start.18 = (bf16[27,16,256]{2,1,0:T(8,128)(2,1)S(1)}, bf16[27,16,256]{2,1,0:T(8,128)(2,1)S(1)}, u32[]{:S(2)}, u32[]{:S(2)}) collective-permute-start(bf16[27,16,256]{2,1,0:T(8,128)(2,1)S(1)} %multiply_convert_fusion.part0), channel_id=1, source_target_pairs={{0,8},{1,3},{2,10},{3,5},{4,12},{5,7},{6,14},{7,1},{8,16},{9,11},{... | collective-permute-start | bytes 663560 | tf_op jit(solution)/shard_map/ppermute | solution.py:44
  94.4 13.8 %collective-permute-start.22 = (bf16[2,320,256]{2,1,0:T(8,128)(2,1)S(1)}, bf16[2,320,256]{2,1,0:T(8,128)(2,1)S(1)}, u32[]{:S(2)}, u32[]{:S(2)}) collective-permute-start(bf16[2,320,256]{2,1,0:T(8,128)(2,1)S(1)} %pack_both.1.packed_own), channel_id=1, source_target_pairs={{2,0},{3,1},{4,2},{5,3},{6,4},{7,5},{8,6},{9,7},{10,8},{11,9},{12,... | collective-permute-start | bytes 983048 | tf_op jit(solution)/shard_map/ppermute | solution.py:52
  95.7 13.0 %collective-permute-start.21 = (bf16[2,320,256]{2,1,0:T(8,128)(2,1)S(1)}, bf16[2,320,256]{2,1,0:T(8,128)(2,1)S(1)}, u32[]{:S(2)}, u32[]{:S(2)}) collective-permute-start(bf16[2,320,256]{2,1,0:T(8,128)(2,1)S(1)} %pack_both.1.packed_own), channel_id=1, source_target_pairs={{0,2},{1,3},{2,4},{3,5},{4,6},{5,7},{6,8},{7,9},{8,10},{9,11},{10,... | collective-permute-start | bytes 983048 | tf_op jit(solution)/shard_map/ppermute | solution.py:52
  106.7 19.7 %collective-permute-start.27 = (bf16[27,64,256]{2,1,0:T(8,128)(2,1)S(1)}, bf16[27,64,256]{2,1,0:T(8,128)(2,1)S(1)}, u32[]{:S(2)}, u32[]{:S(2)}) collective-permute-start(bf16[27,64,256]{2,1,0:T(8,128)(2,1)S(1)} %get-tuple-element.47.refs_0_), channel_id=1, source_target_pairs={{0,96},{1,25},{2,98},{3,27},{4,100},{5,29},{6,102},{7,31},{8,104},... | collective-permute-start | bytes 2654216 | tf_op jit(solution)/shard_map/ppermute | solution.py:44
  106.7 19.6 %collective-permute-start.26 = (bf16[27,64,256]{2,1,0:T(8,128)(2,1)S(1)}, bf16[27,64,256]{2,1,0:T(8,128)(2,1)S(1)}, u32[]{:S(2)}, u32[]{:S(2)}) collective-permute-start(bf16[27,64,256]{2,1,0:T(8,128)(2,1)S(1)} %get-tuple-element.47.refs_0_), channel_id=1, source_target_pairs={{0,32},{1,9},{2,34},{3,11},{4,36},{5,13},{6,38},{7,15},{8,40},{9,1... | collective-permute-start | bytes 2654216 | tf_op jit(solution)/shard_map/ppermute | solution.py:44
  108.2 2.4 %collective-permute-start.25 = (bf16[2,320,256]{2,1,0:T(8,128)(2,1)S(1)}, bf16[2,320,256]{2,1,0:T(8,128)(2,1)S(1)}, u32[]{:S(2)}, u32[]{:S(2)}) collective-permute-start(bf16[2,320,256]{2,1,0:T(8,128)(2,1)S(1)} %collective-permute-done.22.after), channel_id=1, source_target_pairs={{0,1},{1,0},{2,3},{3,2},{4,5},{5,4},{6,7},{7,6},{8,9},{9,8},{10,11... | collective-permute-start | bytes 983048 | tf_op jit(solution)/shard_map/ppermute | solution.py:48
  109.8 15.1 %collective-permute-start.28 = (bf16[27,32,256]{2,1,0:T(8,128)(2,1)S(1)}, bf16[27,32,256]{2,1,0:T(8,128)(2,1)S(1)}, u32[]{:S(2)}, u32[]{:S(2)}) collective-permute-start(bf16[27,32,256]{2,1,0:T(8,128)(2,1)S(1)} %get-tuple-element.48), channel_id=1, source_target_pairs={{0,64},{1,17},{2,66},{3,19},{4,68},{5,21},{6,70},{7,23},{8,72},{9,... | collective-permute-start | bytes 1327112 | tf_op jit(solution)/shard_map/ppermute | solution.py:44
  121.6 11.7 %collective-permute-start.33 = (bf16[27,64,256]{2,1,0:T(8,128)(2,1)S(1)}, bf16[27,64,256]{2,1,0:T(8,128)(2,1)S(1)}, u32[]{:S(2)}, u32[]{:S(2)}) collective-permute-start(bf16[27,64,256]{2,1,0:T(8,128)(2,1)S(1)} %get-tuple-element.49), channel_id=1, source_target_pairs={{0,1},{1,0},{2,3},{3,2},{4,5},{5,4},{6,7},{7,6},{8,9},{9,8},{10,11... | collective-permute-start | bytes 2654216 | tf_op jit(solution)/shard_map/ppermute | solution.py:48
  124.9 8.4 %collective-permute-start.29 = (bf16[27,32,256]{2,1,0:T(8,128)(2,1)S(1)}, bf16[27,32,256]{2,1,0:T(8,128)(2,1)S(1)}, u32[]{:S(2)}, u32[]{:S(2)}) collective-permute-start(bf16[27,32,256]{2,1,0:T(8,128)(2,1)S(1)} %collective-permute-done.28.refs_1_), channel_id=1, source_target_pairs={{0,2},{1,7},{2,0},{3,5},{4,6},{5,3},{6,4},{7,1},{8,10},{9,15},{10,... | collective-permute-start | bytes 1327112 | tf_op jit(solution)/shard_map/ppermute | solution.py:44
  126.3 9.1 %collective-permute-start.31 = (bf16[27,64,256]{2,1,0:T(8,128)(2,1)S(1)}, bf16[27,64,256]{2,1,0:T(8,128)(2,1)S(1)}, u32[]{:S(2)}, u32[]{:S(2)}) collective-permute-start(bf16[27,64,256]{2,1,0:T(8,128)(2,1)S(1)} %collective-permute-done.27.refs_1_), channel_id=1, source_target_pairs={{0,1},{1,0},{2,3},{3,2},{4,5},{5,4},{6,7},{7,6},{8,9},{9,8},{10,11... | collective-permute-start | bytes 2654216 | tf_op jit(solution)/shard_map/ppermute | solution.py:48
  126.3 9.1 %collective-permute-start.30 = (bf16[27,64,256]{2,1,0:T(8,128)(2,1)S(1)}, bf16[27,64,256]{2,1,0:T(8,128)(2,1)S(1)}, u32[]{:S(2)}, u32[]{:S(2)}) collective-permute-start(bf16[27,64,256]{2,1,0:T(8,128)(2,1)S(1)} %collective-permute-done.26.refs_0_), channel_id=1, source_target_pairs={{0,1},{1,0},{2,3},{3,2},{4,5},{5,4},{6,7},{7,6},{8,9},{9,8},{10,11... | collective-permute-start | bytes 2654216 | tf_op jit(solution)/shard_map/ppermute | solution.py:48
  126.9 6.5 %collective-permute-start.34 = (bf16[27,32,256]{2,1,0:T(8,128)(2,1)S(1)}, bf16[27,32,256]{2,1,0:T(8,128)(2,1)S(1)}, u32[]{:S(2)}, u32[]{:S(2)}) collective-permute-start(bf16[27,32,256]{2,1,0:T(8,128)(2,1)S(1)} %collective-permute-done.28.refs_1_), channel_id=1, source_target_pairs={{0,1},{1,0},{2,3},{3,2},{4,5},{5,4},{6,7},{7,6},{8,9},{9,8},{10,11... | collective-permute-start | bytes 1327112 | tf_op jit(solution)/shard_map/ppermute | solution.py:48
  133.3 2.2 %collective-permute-start.32 = (bf16[27,32,256]{2,1,0:T(8,128)(2,1)S(1)}, bf16[27,32,256]{2,1,0:T(8,128)(2,1)S(1)}, u32[]{:S(2)}, u32[]{:S(2)}) collective-permute-start(bf16[27,32,256]{2,1,0:T(8,128)(2,1)S(1)} %collective-permute-done.29.refs_2_), channel_id=1, source_target_pairs={{0,1},{1,0},{2,3},{3,2},{4,5},{5,4},{6,7},{7,6},{8,9},{9,8},{10,11... | collective-permute-start | bytes 1327112 | tf_op jit(solution)/shard_map/ppermute | solution.py:48
  (7 other events, 33.9 us)

commit v4 on v3

--- a/solution.py
+++ b/solution.py
@@ -177,6 +177,11 @@
         pack(both.at[place], packed, place)
 
 
+def pack_mate_kernel(mate, packed):
+    for place in range(2):
+        pack(mate.at[place], packed, place)
+
+
 def frames_kernel(
     pick_ref, place_ref, own, mate, packed_own, before, after, packed_mate, mate_before, mate_after,
     frames, spare, full, packed, sems
@@ -216,18 +221,22 @@
         finish(spare)
 
 
-def outer_kernel(
-    pick_ref, own, mate, packed_own, before, after, packed_mate, mate_before, mate_after,
-    weight_two, weight_one, passed, output, grad_input, passed_out, frame, full, packed, held, sems
+def outer_frames_kernel(
+    pick_ref, own, mate, packed_own, before, after, packed_mate, mate_before, mate_after, waited_for,
+    frame_hidden, frame_grad, full, packed, sems
 ):
     outers = (packed_own, before, after, packed_mate, mate_before, mate_after)
-    loads = loaded(own, mate, outers, (weight_two, weight_one), full, packed, held, sems)
-    build(full, packed, 0, picker(pick_ref, 0), frame, 0)
-    loads[0].wait()
-    output[0] = convolved(frame, held.at[0]).astype(BF16)
-    build(full, packed, 1, picker(pick_ref, 0), frame, 0)
-    loads[1].wait()
-    grad_input[0] = convolved_turned(frame, held.at[1]).astype(BF16)
+    loaded(own, mate, outers, (), full, packed, None, sems)
+    build(full, packed, 0, picker(pick_ref, 0), frame_hidden, 0)
+    build(full, packed, 1, picker(pick_ref, 0), frame_grad, 0)
+
+
+def output_kernel(frame, weight_two, passed, output, passed_out):
+    output[0] = convolved(frame, weight_two).astype(BF16)
+
+
+def grad_input_kernel(frame, weight_one, passed, grad_input, passed_out):
+    grad_input[0] = convolved_turned(frame, weight_one).astype(BF16)
 
 
 def gradient_kernel(place_ref, both, both_mate, frames, passed, *rest):
@@ -386,10 +395,17 @@
         pack_kernel, "pack_fields", [pair, skin], [VMEM_SPEC] * 2, [VMEM_SPEC] * 2, [], 1000, 1_000_000, 60,
     )(features, cotangent)
     before, after = sent_halo(skins)
+
+    def packed_mate(mate):
+        return call(
+            pack_mate_kernel, "pack_mate", [skin], [VMEM_SPEC], [VMEM_SPEC], [], 1000, 1_000_000, 8
+        )(mate)[0]
+
+    mate = swap(fields)
     frames, spare = call(
         frames_kernel, "build_frames", [(2 * FRAME_ROWS, TAPS), (FRAME_ROWS, TAPS)],
         [SMEM_SPEC] * 2 + [ANY_SPEC] * 8, [VMEM_SPEC] * 2, [full, packed, sems], 1_000_000, 12_000_000, 14,
-    )(picks, place, fields, swap(fields), skins, before, after, swap(skins), swap(before), swap(after))
+    )(picks, place, fields, mate, skins, before, after, packed_mate(mate), swap(before), swap(after))
     (pre_act,) = call(
         hidden_kernel, "first_conv", [((ROWS, CH), F32)], [SMEM_SPEC] + [VMEM_SPEC] * 3, [VMEM_SPEC], [],
         flops, 4_000_000, 14,
@@ -428,7 +444,7 @@
     )(both, quarter[0])
     before, after = sent_halo(skins)
     mate_before, mate_after = swap(before), swap(after)
-    skins_mate = swap(skins)
+    skins_mate = packed_mate(both_mate)
     def added(arrays):
         wide = [array.astype(F32) for array in arrays]
         return (wide[0] + wide[2]) + (wide[1] + wide[3])
@@ -445,11 +461,18 @@
     half = ring_send(half, first, 2)
     other_half = ring_send(half, first, 0, pairing)
     from_before, from_after = ring_send(wide, first, 1), ring_send(wide, first, 3)
-    output, grad_input, again = call(
-        outer_kernel, "outer_convs", [(1, ROWS, CH)] * 2 + [rows64],
-        [SMEM_SPEC] + [ANY_SPEC] * 8 + [HBM_SPEC] * 2 + [ANY_SPEC], [VMEM_SPEC] * 2 + [ANY_SPEC],
-        [frame, full, packed, held, sems], 2 * flops, 12_000_000, 18, {11: 2},
-    )(picks, both, both_mate, skins, before, after, skins_mate, mate_before, mate_after, weight_two, weight_one, again)
+    frame_hidden, frame_grad = call(
+        outer_frames_kernel, "outer_frames", [(FRAME_ROWS, TAPS)] * 2, [SMEM_SPEC] + [ANY_SPEC] * 9,
+        [VMEM_SPEC] * 2, [full, packed, sems], 1_000_000, 8_000_000, 14,
+    )(picks, both, both_mate, skins, before, after, skins_mate, mate_before, mate_after, both)
+    output, again = call(
+        output_kernel, "output_conv", [(1, ROWS, CH), rows64], [VMEM_SPEC] * 2 + [ANY_SPEC],
+        [VMEM_SPEC, ANY_SPEC], [], flops, 4_000_000, 14, {2: 1},
+    )(frame_hidden, weight_two, again)
+    grad_input, again = call(
+        grad_input_kernel, "grad_input_conv", [(1, ROWS, CH), rows64], [VMEM_SPEC] * 2 + [ANY_SPEC],
+        [VMEM_SPEC, ANY_SPEC], [], flops, 4_000_000, 14, {2: 1},
+    )(frame_grad, weight_one, again)
     early = [(0, 0), (2, 0)]
     late = [(3, 0), (1, 0), (2, 1)]
     grad_one, grad_two = call(

time: 139 us -> 137 us (0.986)
  starting transfers between devices: 59.4 us -> 62.5 us
  waiting for transfers between devices: 38 us -> 35.3 us
  Pallas kernels: 32.9 us -> 30.6 us
    ppermute x17, starting transfers between devices: 38.7 us -> 41.9 us  [ring_send(): return lax.ppermute(array, AXES, pairs)]
    ppermute x14 -> x12, waiting for transfers between devices: 4.04 us -> 1.71 us  [swap(): lax.ppermute(array, AXES, [(index, index ^ 1) for index in range(128)])]
    pallas_call x1 -> x5, Pallas kernels: 10.8 us -> 8.55 us  [the longest x1 2.73 us: on_device(): call(grad_input_kernel, 'grad_input_conv', [(1, ROWS, CH), rows64], [VMEM...]
    ppermute x14 -> x12, starting transfers between devices: 8.88 us -> 8.09 us  [swap(): lax.ppermute(array, AXES, [(index, index ^ 1) for index in range(128)])]
  transfers between devices with their start and end apart: 35 -> 33, of which waited for: 14 -> 10; matrix products, arithmetic and copies ran while one was open for 3% -> 3% of each run, Pallas kernels for 10% -> 8%
where the time goes in v4:
time: 137 us; the launch traced here: 136 us
  starting transfers between devices  62.5 us (46%)
  waiting for transfers between devices  35.3 us (26%)
  Pallas kernels  30.6 us (22%)
  local copies, waits for them, and re-layouts  4.09 us (3%)
  other arithmetic  2.1 us (2%)
  between operations  1.72 us (1%)
    ppermute x17, starting transfers between devices, ring_send(): return lax.ppermute(array, AXES, pairs)  41.9 us
    ppermute x17, waiting for transfers between devices, ring_send(): return lax.ppermute(array, AXES, pairs)  33.6 us
    ppermute x4, starting transfers between devices, shifted(): lax.ppermute(array, AXES, [(i, i + by) for i in range(128) if 0 <= i + by...  12.5 us
    ppermute x12, starting transfers between devices, swap(): lax.ppermute(array, AXES, [(index, index ^ 1) for index in range(128)])  8.09 us
    pallas_call x1, Pallas kernels, on_device(): call(gradient_kernel, 'weight_grads', [rows64] * 3 + [rows32] * 2 + [pair...  5.06 us
    pallas_call x1, Pallas kernels, on_device(): call(frames_kernel, 'build_frames', [(2 * FRAME_ROWS, TAPS), (FRAME_ROWS,...  2.98 us
  transfers between devices with their start and end apart: 33, of which 10 were waited for; matrix products, arithmetic and copies ran while one was open for 3% of the time, Pallas kernels for 8%

profile of v4, /device:TPU:1, one launch (start us, length us, event | category | flops | bytes accessed | tf_op | source)
XLA Modules:
  0.0 136.3 jit_solution(5812620326368211808)
XLA Ops:
  0.6 2.1 %pack_fields.1 = (bf16[2,512,256]{2,1,0:T(8,128)(2,1)}, bf16[2,320,256]{2,1,0:T(8,128)(2,1)}) custom-call(bf16[1,512,256]{2,1,0:T(8,128)(2,1)} %features.1, bf16[1,512,256]{2,1,0:T(8,128)(2,1)} %cotangent.1), custom_call_target="tpu_custom_call" | custom-call | flops 1000 | bytes 1000000 | tf_op jit(solution)/shard_map/pack_fields/pallas_call | solution.py:394
  4.1 5.4 %collective-permute-start.2 = (bf16[2,320,256]{2,1,0:T(8,128)(2,1)}, bf16[2,320,256]{2,1,0:T(8,128)(2,1)}, u32[]{:S(2)}, u32[]{:S(2)}) collective-permute-start(bf16[2,320,256]{2,1,0:T(8,128)(2,1)} %get-tuple-element.33.packed_own), channel_id=1, source_target_pairs={{0,2},{1,3},{2,4},{3,5},{4,6},{5,7},{6,8},{7,9},{8,10},{9,11},{10,... | collective-permute-start | bytes 983048 | tf_op jit(solution)/shard_map/ppermute | solution.py:52
  20.4 3.0 %build_frames.1 = (bf16[1280,2304]{1,0:T(8,128)(2,1)S(1)}, bf16[640,2304]{1,0:T(8,128)(2,1)S(1)}) custom-call(s32[2,27]{1,0:T(2,128)S(1)} %compare_select_fusion.3.pick_ref, s32[6]{0:T(128)S(1)} %stack.43.place_ref, bf16[2,512,256]{2,1,0:T(8,128)(2,1)S(1)} %copy-done.2, bf16[2,512,256]{2,1,0:T(8,128)(2,1)} %collective-permute-done.1.mate, ...), custom_call_target="tpu_custom_call" | custom-call | flops 1000000 | bytes 12000000 | tf_op jit(solution)/shard_map/build_frames/pallas_call | solution.py:405
  23.4 2.6 %first_conv.1.pre_act_ref = f32[512,256]{1,0:T(8,128)S(1)} custom-call(s32[6]{0:T(128)S(1)} %stack.43.place_ref, bf16[1280,2304]{1,0:T(8,128)(2,1)S(1)} %get-tuple-element.34.frames, bf16[640,2304]{1,0:T(8,128)(2,1)S(1)} %get-tuple-element.35.spare, bf16[27,256,256]{2,1,0:T(8,128)(2,1)S(1)} %copy-done), custom_call_target="tpu_custom_call" | custom-call | flops 1811939328 | bytes 4000000 | tf_op jit(solution)/shard_map/first_conv/pallas_call | solution.py:409
  26.0 2.6 %grad_conv.1.both = bf16[2,512,256]{2,1,0:T(8,128)(2,1)S(1)} custom-call(s32[6]{0:T(128)S(1)} %stack.43.place_ref, bf16[1280,2304]{1,0:T(8,128)(2,1)S(1)} %get-tuple-element.34.frames, bf16[640,2304]{1,0:T(8,128)(2,1)S(1)} %get-tuple-element.35.spare, bf16[27,256,256]{2,1,0:T(8,128)(2,1)S(1)} %copy-done.1, f32[512,256]{1,0:T(8,128)S(1)} %first_conv.1.pre_act_ref), custom_call_target="tpu_custom_call" | custom-call | flops 1811939328 | bytes 4000000 | tf_op jit(solution)/shard_map/grad_conv/pallas_call | solution.py:413
  29.1 1.5 %collective-permute-done.6.both_mate.mate = bf16[2,512,256]{2,1,0:T(8,128)(2,1)S(1)} collective-permute-done((bf16[2,512,256]{2,1,0:T(8,128)(2,1)S(1)}, bf16[2,512,256]{2,1,0:T(8,128)(2,1)S(1)}, u32[]{:S(2)}, u32[]{:S(2)}) %collective-permute-start.6) | collective-permute-done | bytes 524320 | tf_op jit(solution)/shard_map/ppermute | solution.py:48
  30.6 5.1 %weight_grads.1 = (bf16[27,64,256]{2,1,0:T(8,128)(2,1)S(1)}, bf16[27,64,256]{2,1,0:T(8,128)(2,1)S(1)}, bf16[27,64,256]{2,1,0:T(8,128)(2,1)S(1)}, bf16[27,32,256]...) custom-call(s32[6]{0:T(128)S(1)} %stack.43.place_ref, ...), custom_call_target="tpu_custom_call", output_to_operand_aliasing={{5}: (4, {})} | custom-call | flops 3623878656 | bytes 10000000 | tf_op jit(solution)/shard_map/weight_grads/pallas_call | solution.py:419
  35.7 5.1 %collective-permute-start.9 = (bf16[27,32,256]{2,1,0:T(8,128)(2,1)S(1)}, bf16[27,32,256]{2,1,0:T(8,128)(2,1)S(1)}, u32[]{:S(2)}, u32[]{:S(2)}) collective-permute-start(bf16[27,32,256]{2,1,0:T(8,128)(2,1)S(1)} %get-tuple-element.40), channel_id=1, source_target_pairs={{0,2},{1,7},{2,0},{3,5},{4,6},{5,3},{6,4},{7,1},{8,10},{9,15},{10,... | collective-permute-start | bytes 1327112 | tf_op jit(solution)/shard_map/ppermute | solution.py:44
  40.8 2.0 %collective-permute-start.7 = (bf16[27,64,256]{2,1,0:T(8,128)(2,1)S(1)}, bf16[27,64,256]{2,1,0:T(8,128)(2,1)S(1)}, u32[]{:S(2)}, u32[]{:S(2)}) collective-permute-start(bf16[27,64,256]{2,1,0:T(8,128)(2,1)S(1)} %get-tuple-element.37), channel_id=1, source_target_pairs={{0,32},{1,9},{2,34},{3,11},{4,36},{5,13},{6,38},{7,15},{8,40},{9,1... | collective-permute-start | bytes 2654216 | tf_op jit(solution)/shard_map/ppermute | solution.py:44
  42.8 3.9 %collective-permute-start.8 = (bf16[27,64,256]{2,1,0:T(8,128)(2,1)S(1)}, bf16[27,64,256]{2,1,0:T(8,128)(2,1)S(1)}, u32[]{:S(2)}, u32[]{:S(2)}) collective-permute-start(bf16[27,64,256]{2,1,0:T(8,128)(2,1)S(1)} %get-tuple-element.38), channel_id=1, source_target_pairs={{0,96},{1,25},{2,98},{3,27},{4,100},{5,29},{6,102},{7,31},{8,104},... | collective-permute-start | bytes 2654216 | tf_op jit(solution)/shard_map/ppermute | solution.py:44
  46.8 6.7 %collective-permute-start.10 = (bf16[27,32,256]{2,1,0:T(8,128)(2,1)S(1)}, bf16[27,32,256]{2,1,0:T(8,128)(2,1)S(1)}, u32[]{:S(2)}, u32[]{:S(2)}) collective-permute-start(bf16[27,32,256]{2,1,0:T(8,128)(2,1)S(1)} %add_convert_fusion), channel_id=1, source_target_pairs={{0,64},{1,17},{2,66},{3,19},{4,68},{5,21},{6,70},{7,23},{8,72},{9,... | collective-permute-start | bytes 1327112 | tf_op jit(solution)/shard_map/ppermute | solution.py:44
  53.5 9.7 %collective-permute-done.10.across = bf16[27,32,256]{2,1,0:T(8,128)(2,1)S(1)} collective-permute-done((bf16[27,32,256]{2,1,0:T(8,128)(2,1)S(1)}, bf16[27,32,256]{2,1,0:T(8,128)(2,1)S(1)}, u32[]{:S(2)}, u32[]{:S(2)}) %collective-permute-start.10) | collective-permute-done | bytes 442400 | tf_op jit(solution)/shard_map/ppermute | solution.py:44
  64.4 1.4 %collective-permute-start.12 = (bf16[27,16,256]{2,1,0:T(8,128)(2,1)S(1)}, bf16[27,16,256]{2,1,0:T(8,128)(2,1)S(1)}, u32[]{:S(2)}, u32[]{:S(2)}) collective-permute-start(bf16[27,16,256]{2,1,0:T(8,128)(2,1)S(1)} %get-tuple-element.43), channel_id=1, source_target_pairs={{0,8},{1,3},{2,10},{3,5},{4,12},{5,7},{6,14},{7,1},{8,16},{9,11},{... | collective-permute-start | bytes 663560 | tf_op jit(solution)/shard_map/ppermute | solution.py:44
  67.2 3.6 %collective-permute-done.11 = bf16[27,16,256]{2,1,0:T(8,128)(2,1)S(1)} collective-permute-done((bf16[27,16,256]{2,1,0:T(8,128)(2,1)S(1)}, bf16[27,16,256]{2,1,0:T(8,128)(2,1)S(1)}, u32[]{:S(2)}, u32[]{:S(2)}) %collective-permute-start.11) | collective-permute-done | bytes 221216 | tf_op jit(solution)/shard_map/ppermute | solution.py:44
  70.8 2.1 %collective-permute-done.12 = bf16[27,16,256]{2,1,0:T(8,128)(2,1)S(1)} collective-permute-done((bf16[27,16,256]{2,1,0:T(8,128)(2,1)S(1)}, bf16[27,16,256]{2,1,0:T(8,128)(2,1)S(1)}, u32[]{:S(2)}, u32[]{:S(2)}) %collective-permute-start.12) | collective-permute-done | bytes 221216 | tf_op jit(solution)/shard_map/ppermute | solution.py:44
  73.0 8.1 %collective-permute-start.16 = (bf16[27,16,256]{2,1,0:T(8,128)(2,1)S(1)}, bf16[27,16,256]{2,1,0:T(8,128)(2,1)S(1)}, u32[]{:S(2)}, u32[]{:S(2)}) collective-permute-start(bf16[27,16,256]{2,1,0:T(8,128)(2,1)S(1)} %add_convert_fusion.1), channel_id=1, source_target_pairs={{0,6},{1,97},{2,0},{3,99},{4,2},{5,101},{6,4},{7,103},{8,14},{9,10... | collective-permute-start | bytes 663560 | tf_op jit(solution)/shard_map/ppermute | solution.py:44
  81.1 2.5 %collective-permute-start.14 = (bf16[27,16,256]{2,1,0:T(8,128)(2,1)S(1)}, bf16[27,16,256]{2,1,0:T(8,128)(2,1)S(1)}, u32[]{:S(2)}, u32[]{:S(2)}) collective-permute-start(bf16[27,16,256]{2,1,0:T(8,128)(2,1)S(1)} %add_convert_fusion.1), channel_id=1, source_target_pairs={{0,4},{1,65},{2,6},{3,67},{4,0},{5,69},{6,2},{7,71},{8,12},{9,73},... | collective-permute-start | bytes 663560 | tf_op jit(solution)/shard_map/ppermute | solution.py:44
  84.0 5.5 %collective-permute-done.15 = bf16[27,16,256]{2,1,0:T(8,128)(2,1)S(1)} collective-permute-done((bf16[27,16,256]{2,1,0:T(8,128)(2,1)S(1)}, bf16[27,16,256]{2,1,0:T(8,128)(2,1)S(1)}, u32[]{:S(2)}, u32[]{:S(2)}) %collective-permute-start.15) | collective-permute-done | bytes 221216 | tf_op jit(solution)/shard_map/ppermute | solution.py:44
  89.6 3.3 %collective-permute-start.19 = (bf16[27,16,256]{2,1,0:T(8,128)(2,1)S(1)}, bf16[27,16,256]{2,1,0:T(8,128)(2,1)S(1)}, u32[]{:S(2)}, u32[]{:S(2)}) collective-permute-start(bf16[27,16,256]{2,1,0:T(8,128)(2,1)S(1)} %multiply_convert_fusion.part0), channel_id=1, source_target_pairs={{0,24},{1,7},{2,26},{3,1},{4,28},{5,3},{6,30},{7,5},{8,0},{9,15},{... | collective-permute-start | bytes 663560 | tf_op jit(solution)/shard_map/ppermute | solution.py:44
  95.0 4.5 %collective-permute-start.20 = (bf16[2,320,256]{2,1,0:T(8,128)(2,1)S(1)}, bf16[2,320,256]{2,1,0:T(8,128)(2,1)S(1)}, u32[]{:S(2)}, u32[]{:S(2)}) collective-permute-start(bf16[2,320,256]{2,1,0:T(8,128)(2,1)S(1)} %pack_both.1.packed_own), channel_id=1, source_target_pairs={{0,2},{1,3},{2,4},{3,5},{4,6},{5,7},{6,8},{7,9},{8,10},{9,11},{10,... | collective-permute-start | bytes 983048 | tf_op jit(solution)/shard_map/ppermute | solution.py:52
  99.5 5.6 %collective-permute-done.19.part3 = bf16[27,16,256]{2,1,0:T(8,128)(2,1)S(1)} collective-permute-done((bf16[27,16,256]{2,1,0:T(8,128)(2,1)S(1)}, bf16[27,16,256]{2,1,0:T(8,128)(2,1)S(1)}, u32[]{:S(2)}, u32[]{:S(2)}) %collective-permute-start.19) | collective-permute-done | bytes 221216 | tf_op jit(solution)/shard_map/ppermute | solution.py:44
  106.0 1.5 %collective-permute-start.24 = (bf16[27,64,256]{2,1,0:T(8,128)(2,1)S(1)}, bf16[27,64,256]{2,1,0:T(8,128)(2,1)S(1)}, u32[]{:S(2)}, u32[]{:S(2)}) collective-permute-start(bf16[27,64,256]{2,1,0:T(8,128)(2,1)S(1)} %get-tuple-element.53.refs_0_), channel_id=1, source_target_pairs={{0,32},{1,9},{2,34},{3,11},{4,36},{5,13},{6,38},{7,15},{8,40},{9,1... | collective-permute-start | bytes 2654216 | tf_op jit(solution)/shard_map/ppermute | solution.py:44
  107.9 1.9 %collective-permute-start.26 = (bf16[27,32,256]{2,1,0:T(8,128)(2,1)S(1)}, bf16[27,32,256]{2,1,0:T(8,128)(2,1)S(1)}, u32[]{:S(2)}, u32[]{:S(2)}) collective-permute-start(bf16[27,32,256]{2,1,0:T(8,128)(2,1)S(1)} %get-tuple-element.54), channel_id=1, source_target_pairs={{0,64},{1,17},{2,66},{3,19},{4,68},{5,21},{6,70},{7,23},{8,72},{9,... | collective-permute-start | bytes 1327112 | tf_op jit(solution)/shard_map/ppermute | solution.py:44
  110.0 1.8 %outer_frames.1 = (bf16[640,2304]{1,0:T(8,128)(2,1)S(1)}, bf16[640,2304]{1,0:T(8,128)(2,1)S(1)}) custom-call(s32[2,27]{1,0:T(2,128)S(1)} %compare_select_fusion.3.pick_ref, bf16[2,512,256]{2,1,0:T(8,128)(2,1)S(1)} %get-tuple-element.46.own.waited_for, bf16[2,512,256]{2,1,0:T(8,128)(2,1)S(1)} %collective-permute-done.6.both_mate.mate, ...), custom_call_target="tpu_custom_call" | custom-call | flops 1000000 | bytes 8000000 | tf_op jit(solution)/shard_map/outer_frames/pallas_call | solution.py:464
  111.8 2.7 %output_conv.1 = (bf16[1,512,256]{2,1,0:T(8,128)(2,1)}, bf16[27,64,256]{2,1,0:T(8,128)(2,1)S(1)}) custom-call(bf16[640,2304]{1,0:T(8,128)(2,1)S(1)} %get-tuple-element.47.frame, bf16[27,256,256]{2,1,0:T(8,128)(2,1)S(1)} %copy-done.1, bf16[27,64,256]{2,1,0:T(8,128)(2,1)S(1)} %get-tuple-element.48.passed), custom_call_target="tpu_custom_call", output_to_operand_aliasing={{1}: (2, {})} | custom-call | flops 1811939328 | bytes 4000000 | tf_op jit(solution)/shard_map/output_conv/pallas_call | solution.py:468
  114.5 2.7 %grad_input_conv.1 = (bf16[1,512,256]{2,1,0:T(8,128)(2,1)}, bf16[27,64,256]{2,1,0:T(8,128)(2,1)S(1)}) custom-call(bf16[640,2304]{1,0:T(8,128)(2,1)S(1)} %get-tuple-element.50.frame, bf16[27,256,256]{2,1,0:T(8,128)(2,1)S(1)} %copy-done, bf16[27,64,256]{2,1,0:T(8,128)(2,1)S(1)} %get-tuple-element.51.passed), custom_call_target="tpu_custom_call", output_to_operand_aliasing={{1}: (2, {})} | custom-call | flops 1811939328 | bytes 4000000 | tf_op jit(solution)/shard_map/grad_input_conv/pallas_call | solution.py:472
  117.3 3.4 %collective-permute-start.31 = (bf16[27,64,256]{2,1,0:T(8,128)(2,1)S(1)}, bf16[27,64,256]{2,1,0:T(8,128)(2,1)S(1)}, u32[]{:S(2)}, u32[]{:S(2)}) collective-permute-start(bf16[27,64,256]{2,1,0:T(8,128)(2,1)S(1)} %get-tuple-element.55), channel_id=1, source_target_pairs={{0,1},{1,0},{2,3},{3,2},{4,5},{5,4},{6,7},{7,6},{8,9},{9,8},{10,11... | collective-permute-start | bytes 2654216 | tf_op jit(solution)/shard_map/ppermute | solution.py:48
  120.6 1.5 %collective-permute-done.26.refs_1_ = bf16[27,32,256]{2,1,0:T(8,128)(2,1)S(1)} collective-permute-done((bf16[27,32,256]{2,1,0:T(8,128)(2,1)S(1)}, bf16[27,32,256]{2,1,0:T(8,128)(2,1)S(1)}, u32[]{:S(2)}, u32[]{:S(2)}) %collective-permute-start.26) | collective-permute-done | bytes 442400 | tf_op jit(solution)/shard_map/ppermute | solution.py:44
  122.2 3.4 %collective-permute-start.27 = (bf16[27,32,256]{2,1,0:T(8,128)(2,1)S(1)}, bf16[27,32,256]{2,1,0:T(8,128)(2,1)S(1)}, u32[]{:S(2)}, u32[]{:S(2)}) collective-permute-start(bf16[27,32,256]{2,1,0:T(8,128)(2,1)S(1)} %collective-permute-done.26.refs_1_), channel_id=1, source_target_pairs={{0,2},{1,7},{2,0},{3,5},{4,6},{5,3},{6,4},{7,1},{8,10},{9,15},{10,... | collective-permute-start | bytes 1327112 | tf_op jit(solution)/shard_map/ppermute | solution.py:44
  126.2 5.1 %collective-permute-done.27.refs_2_ = bf16[27,32,256]{2,1,0:T(8,128)(2,1)S(1)} collective-permute-done((bf16[27,32,256]{2,1,0:T(8,128)(2,1)S(1)}, bf16[27,32,256]{2,1,0:T(8,128)(2,1)S(1)}, u32[]{:S(2)}, u32[]{:S(2)}) %collective-permute-start.27) | collective-permute-done | bytes 442400 | tf_op jit(solution)/shard_map/ppermute | solution.py:44
  131.3 2.1 %place_early.1 = (bf16[27,256,256]{2,1,0:T(8,128)(2,1)}, bf16[27,256,256]{2,1,0:T(8,128)(2,1)}) custom-call(s32[6]{0:T(128)S(1)} %stack.43.place_ref, bf16[27,64,256]{2,1,0:T(8,128)(2,1)S(1)} %get-tuple-element.53.refs_0_, bf16[27,32,256]{2,1,0:T(8,128)(2,1)S(1)} %collective-permute-done.26.refs_1_, ...), custom_call_target="tpu_custom_call" | custom-call | flops 1000 | bytes 5000000 | tf_op jit(solution)/shard_map/place_early/pallas_call | solution.py:478
  133.4 2.7 %place_late.1 = (bf16[27,256,256]{2,1,0:T(8,128)(2,1)}, bf16[27,256,256]{2,1,0:T(8,128)(2,1)}) custom-call(s32[6]{0:T(128)S(1)} %stack.43.place_ref, bf16[27,64,256]{2,1,0:T(8,128)(2,1)S(1)} %collective-permute-done.24.refs_0_, bf16[27,64,256]{2,1,0:T(8,128)(2,1)S(1)} %collective-permute-done.25.refs_1_, ...), custom_call_target="tpu_custom_call", output_to_operand_aliasing={{0}: (7, {}), {1}: (8, {})} | custom-call | flops 1000 | bytes 9000000 | tf_op jit(solution)/shard_map/place_late/pallas_call | solution.py:484
  (71 shorter events, 19.5 us)
Async XLA Ops:
  2.8 12.3 %collective-permute-start.3 = (bf16[2,320,256]{2,1,0:T(8,128)(2,1)}, bf16[2,320,256]{2,1,0:T(8,128)(2,1)}, u32[]{:S(2)}, u32[]{:S(2)}) collective-permute-start(bf16[2,320,256]{2,1,0:T(8,128)(2,1)} %get-tuple-element.33.packed_own), channel_id=1, source_target_pairs={{2,0},{3,1},{4,2},{5,3},{6,4},{7,5},{8,6},{9,7},{10,8},{11,9},{12,... | collective-permute-start | bytes 983048 | tf_op jit(solution)/shard_map/ppermute | solution.py:52
  4.1 11.7 %collective-permute-start.2 = (bf16[2,320,256]{2,1,0:T(8,128)(2,1)}, bf16[2,320,256]{2,1,0:T(8,128)(2,1)}, u32[]{:S(2)}, u32[]{:S(2)}) collective-permute-start(bf16[2,320,256]{2,1,0:T(8,128)(2,1)} %get-tuple-element.33.packed_own), channel_id=1, source_target_pairs={{0,2},{1,3},{2,4},{3,5},{4,6},{5,7},{6,8},{7,9},{8,10},{9,11},{10,... | collective-permute-start | bytes 983048 | tf_op jit(solution)/shard_map/ppermute | solution.py:52
  10.9 3.4 %collective-permute-start = (s32[1,27]{1,0:T(1,128)S(1)}, s32[1,27]{1,0:T(1,128)S(1)}, u32[]{:S(2)}, u32[]{:S(2)}) collective-permute-start(s32[1,27]{1,0:T(1,128)S(1)} %pad_add_fusion.2), channel_id=1, source_target_pairs={{0,1},{1,0},{2,3},{3,2},{4,5},{5,4},{6,7},{7,6},{8,9},{9,8},{10,11... | collective-permute-start | bytes 332 | tf_op jit(solution)/shard_map/ppermute | solution.py:48
  12.2 4.9 %collective-permute-start.1 = (bf16[2,512,256]{2,1,0:T(8,128)(2,1)}, bf16[2,512,256]{2,1,0:T(8,128)(2,1)}, u32[]{:S(2)}, u32[]{:S(2)}) collective-permute-start(bf16[2,512,256]{2,1,0:T(8,128)(2,1)} %get-tuple-element.32.own), channel_id=1, source_target_pairs={{0,1},{1,0},{2,3},{3,2},{4,5},{5,4},{6,7},{7,6},{8,9},{9,8},{10,11... | collective-permute-start | bytes 1572872 | tf_op jit(solution)/shard_map/ppermute | solution.py:48
  15.1 3.1 %collective-permute-start.5 = (bf16[2,320,256]{2,1,0:T(8,128)(2,1)}, bf16[2,320,256]{2,1,0:T(8,128)(2,1)S(1)}, u32[]{:S(2)}, u32[]{:S(2)}) collective-permute-start(bf16[2,320,256]{2,1,0:T(8,128)(2,1)} %collective-permute-done.3.after), channel_id=1, source_target_pairs={{0,1},{1,0},{2,3},{3,2},{4,5},{5,4},{6,7},{7,6},{8,9},{9,8},{10,11... | collective-permute-start | bytes 983048 | tf_op jit(solution)/shard_map/ppermute | solution.py:48
  15.8 2.6 %collective-permute-start.4 = (bf16[2,320,256]{2,1,0:T(8,128)(2,1)}, bf16[2,320,256]{2,1,0:T(8,128)(2,1)S(1)}, u32[]{:S(2)}, u32[]{:S(2)}) collective-permute-start(bf16[2,320,256]{2,1,0:T(8,128)(2,1)} %collective-permute-done.2.before), channel_id=1, source_target_pairs={{0,1},{1,0},{2,3},{3,2},{4,5},{5,4},{6,7},{7,6},{8,9},{9,8},{10,11... | collective-permute-start | bytes 983048 | tf_op jit(solution)/shard_map/ppermute | solution.py:48
  35.7 11.0 %collective-permute-start.9 = (bf16[27,32,256]{2,1,0:T(8,128)(2,1)S(1)}, bf16[27,32,256]{2,1,0:T(8,128)(2,1)S(1)}, u32[]{:S(2)}, u32[]{:S(2)}) collective-permute-start(bf16[27,32,256]{2,1,0:T(8,128)(2,1)S(1)} %get-tuple-element.40), channel_id=1, source_target_pairs={{0,2},{1,7},{2,0},{3,5},{4,6},{5,3},{6,4},{7,1},{8,10},{9,15},{10,... | collective-permute-start | bytes 1327112 | tf_op jit(solution)/shard_map/ppermute | solution.py:44
  40.8 22.5 %collective-permute-start.7 = (bf16[27,64,256]{2,1,0:T(8,128)(2,1)S(1)}, bf16[27,64,256]{2,1,0:T(8,128)(2,1)S(1)}, u32[]{:S(2)}, u32[]{:S(2)}) collective-permute-start(bf16[27,64,256]{2,1,0:T(8,128)(2,1)S(1)} %get-tuple-element.37), channel_id=1, source_target_pairs={{0,32},{1,9},{2,34},{3,11},{4,36},{5,13},{6,38},{7,15},{8,40},{9,1... | collective-permute-start | bytes 2654216 | tf_op jit(solution)/shard_map/ppermute | solution.py:44
  42.8 20.5 %collective-permute-start.8 = (bf16[27,64,256]{2,1,0:T(8,128)(2,1)S(1)}, bf16[27,64,256]{2,1,0:T(8,128)(2,1)S(1)}, u32[]{:S(2)}, u32[]{:S(2)}) collective-permute-start(bf16[27,64,256]{2,1,0:T(8,128)(2,1)S(1)} %get-tuple-element.38), channel_id=1, source_target_pairs={{0,96},{1,25},{2,98},{3,27},{4,100},{5,29},{6,102},{7,31},{8,104},... | collective-permute-start | bytes 2654216 | tf_op jit(solution)/shard_map/ppermute | solution.py:44
  46.8 16.5 %collective-permute-start.10 = (bf16[27,32,256]{2,1,0:T(8,128)(2,1)S(1)}, bf16[27,32,256]{2,1,0:T(8,128)(2,1)S(1)}, u32[]{:S(2)}, u32[]{:S(2)}) collective-permute-start(bf16[27,32,256]{2,1,0:T(8,128)(2,1)S(1)} %add_convert_fusion), channel_id=1, source_target_pairs={{0,64},{1,17},{2,66},{3,19},{4,68},{5,21},{6,70},{7,23},{8,72},{9,... | collective-permute-start | bytes 1327112 | tf_op jit(solution)/shard_map/ppermute | solution.py:44
  64.3 6.5 %collective-permute-start.11 = (bf16[27,16,256]{2,1,0:T(8,128)(2,1)S(1)}, bf16[27,16,256]{2,1,0:T(8,128)(2,1)S(1)}, u32[]{:S(2)}, u32[]{:S(2)}) collective-permute-start(bf16[27,16,256]{2,1,0:T(8,128)(2,1)S(1)} %get-tuple-element.42), channel_id=1, source_target_pairs={{0,16},{1,5},{2,18},{3,7},{4,20},{5,1},{6,22},{7,3},{8,24},{9,13},... | collective-permute-start | bytes 663560 | tf_op jit(solution)/shard_map/ppermute | solution.py:44
  64.4 8.4 %collective-permute-start.12 = (bf16[27,16,256]{2,1,0:T(8,128)(2,1)S(1)}, bf16[27,16,256]{2,1,0:T(8,128)(2,1)S(1)}, u32[]{:S(2)}, u32[]{:S(2)}) collective-permute-start(bf16[27,16,256]{2,1,0:T(8,128)(2,1)S(1)} %get-tuple-element.43), channel_id=1, source_target_pairs={{0,8},{1,3},{2,10},{3,5},{4,12},{5,7},{6,14},{7,1},{8,16},{9,11},{... | collective-permute-start | bytes 663560 | tf_op jit(solution)/shard_map/ppermute | solution.py:44
  65.8 7.0 %collective-permute-start.13 = (bf16[27,16,256]{2,1,0:T(8,128)(2,1)S(1)}, bf16[27,16,256]{2,1,0:T(8,128)(2,1)S(1)}, u32[]{:S(2)}, u32[]{:S(2)}) collective-permute-start(bf16[27,16,256]{2,1,0:T(8,128)(2,1)S(1)} %get-tuple-element.44), channel_id=1, source_target_pairs={{0,24},{1,7},{2,26},{3,1},{4,28},{5,3},{6,30},{7,5},{8,0},{9,15},{... | collective-permute-start | bytes 663560 | tf_op jit(solution)/shard_map/ppermute | solution.py:44
  73.0 11.0 %collective-permute-start.16 = (bf16[27,16,256]{2,1,0:T(8,128)(2,1)S(1)}, bf16[27,16,256]{2,1,0:T(8,128)(2,1)S(1)}, u32[]{:S(2)}, u32[]{:S(2)}) collective-permute-start(bf16[27,16,256]{2,1,0:T(8,128)(2,1)S(1)} %add_convert_fusion.1), channel_id=1, source_target_pairs={{0,6},{1,97},{2,0},{3,99},{4,2},{5,101},{6,4},{7,103},{8,14},{9,10... | collective-permute-start | bytes 663560 | tf_op jit(solution)/shard_map/ppermute | solution.py:44
  81.1 8.4 %collective-permute-start.15 = (bf16[27,16,256]{2,1,0:T(8,128)(2,1)S(1)}, bf16[27,16,256]{2,1,0:T(8,128)(2,1)S(1)}, u32[]{:S(2)}, u32[]{:S(2)}) collective-permute-start(bf16[27,16,256]{2,1,0:T(8,128)(2,1)S(1)} %add_convert_fusion.1), channel_id=1, source_target_pairs={{0,2},{1,33},{2,4},{3,35},{4,6},{5,37},{6,0},{7,39},{8,10},{9,41},... | collective-permute-start | bytes 663560 | tf_op jit(solution)/shard_map/ppermute | solution.py:44
  81.1 8.4 %collective-permute-start.14 = (bf16[27,16,256]{2,1,0:T(8,128)(2,1)S(1)}, bf16[27,16,256]{2,1,0:T(8,128)(2,1)S(1)}, u32[]{:S(2)}, u32[]{:S(2)}) collective-permute-start(bf16[27,16,256]{2,1,0:T(8,128)(2,1)S(1)} %add_convert_fusion.1), channel_id=1, source_target_pairs={{0,4},{1,65},{2,6},{3,67},{4,0},{5,69},{6,2},{7,71},{8,12},{9,73},... | collective-permute-start | bytes 663560 | tf_op jit(solution)/shard_map/ppermute | solution.py:44
  89.6 15.5 %collective-permute-start.19 = (bf16[27,16,256]{2,1,0:T(8,128)(2,1)S(1)}, bf16[27,16,256]{2,1,0:T(8,128)(2,1)S(1)}, u32[]{:S(2)}, u32[]{:S(2)}) collective-permute-start(bf16[27,16,256]{2,1,0:T(8,128)(2,1)S(1)} %multiply_convert_fusion.part0), channel_id=1, source_target_pairs={{0,24},{1,7},{2,26},{3,1},{4,28},{5,3},{6,30},{7,5},{8,0},{9,15},{... | collective-permute-start | bytes 663560 | tf_op jit(solution)/shard_map/ppermute | solution.py:44
  92.9 12.3 %collective-permute-start.18 = (bf16[27,16,256]{2,1,0:T(8,128)(2,1)S(1)}, bf16[27,16,256]{2,1,0:T(8,128)(2,1)S(1)}, u32[]{:S(2)}, u32[]{:S(2)}) collective-permute-start(bf16[27,16,256]{2,1,0:T(8,128)(2,1)S(1)} %multiply_convert_fusion.part0), channel_id=1, source_target_pairs={{0,16},{1,5},{2,18},{3,7},{4,20},{5,1},{6,22},{7,3},{8,24},{9,13},... | collective-permute-start | bytes 663560 | tf_op jit(solution)/shard_map/ppermute | solution.py:44
  92.9 12.3 %collective-permute-start.17 = (bf16[27,16,256]{2,1,0:T(8,128)(2,1)S(1)}, bf16[27,16,256]{2,1,0:T(8,128)(2,1)S(1)}, u32[]{:S(2)}, u32[]{:S(2)}) collective-permute-start(bf16[27,16,256]{2,1,0:T(8,128)(2,1)S(1)} %multiply_convert_fusion.part0), channel_id=1, source_target_pairs={{0,8},{1,3},{2,10},{3,5},{4,12},{5,7},{6,14},{7,1},{8,16},{9,11},{... | collective-permute-start | bytes 663560 | tf_op jit(solution)/shard_map/ppermute | solution.py:44
  93.7 13.8 %collective-permute-start.21 = (bf16[2,320,256]{2,1,0:T(8,128)(2,1)S(1)}, bf16[2,320,256]{2,1,0:T(8,128)(2,1)S(1)}, u32[]{:S(2)}, u32[]{:S(2)}) collective-permute-start(bf16[2,320,256]{2,1,0:T(8,128)(2,1)S(1)} %pack_both.1.packed_own), channel_id=1, source_target_pairs={{2,0},{3,1},{4,2},{5,3},{6,4},{7,5},{8,6},{9,7},{10,8},{11,9},{12,... | collective-permute-start | bytes 983048 | tf_op jit(solution)/shard_map/ppermute | solution.py:52
  95.0 12.5 %collective-permute-start.20 = (bf16[2,320,256]{2,1,0:T(8,128)(2,1)S(1)}, bf16[2,320,256]{2,1,0:T(8,128)(2,1)S(1)}, u32[]{:S(2)}, u32[]{:S(2)}) collective-permute-start(bf16[2,320,256]{2,1,0:T(8,128)(2,1)S(1)} %pack_both.1.packed_own), channel_id=1, source_target_pairs={{0,2},{1,3},{2,4},{3,5},{4,6},{5,7},{6,8},{7,9},{8,10},{9,11},{10,... | collective-permute-start | bytes 983048 | tf_op jit(solution)/shard_map/ppermute | solution.py:52
  105.9 19.7 %collective-permute-start.25 = (bf16[27,64,256]{2,1,0:T(8,128)(2,1)S(1)}, bf16[27,64,256]{2,1,0:T(8,128)(2,1)S(1)}, u32[]{:S(2)}, u32[]{:S(2)}) collective-permute-start(bf16[27,64,256]{2,1,0:T(8,128)(2,1)S(1)} %get-tuple-element.53.refs_0_), channel_id=1, source_target_pairs={{0,96},{1,25},{2,98},{3,27},{4,100},{5,29},{6,102},{7,31},{8,104},... | collective-permute-start | bytes 2654216 | tf_op jit(solution)/shard_map/ppermute | solution.py:44
  106.0 19.6 %collective-permute-start.24 = (bf16[27,64,256]{2,1,0:T(8,128)(2,1)S(1)}, bf16[27,64,256]{2,1,0:T(8,128)(2,1)S(1)}, u32[]{:S(2)}, u32[]{:S(2)}) collective-permute-start(bf16[27,64,256]{2,1,0:T(8,128)(2,1)S(1)} %get-tuple-element.53.refs_0_), channel_id=1, source_target_pairs={{0,32},{1,9},{2,34},{3,11},{4,36},{5,13},{6,38},{7,15},{8,40},{9,1... | collective-permute-start | bytes 2654216 | tf_op jit(solution)/shard_map/ppermute | solution.py:44
  107.4 2.5 %collective-permute-start.23 = (bf16[2,320,256]{2,1,0:T(8,128)(2,1)S(1)}, bf16[2,320,256]{2,1,0:T(8,128)(2,1)S(1)}, u32[]{:S(2)}, u32[]{:S(2)}) collective-permute-start(bf16[2,320,256]{2,1,0:T(8,128)(2,1)S(1)} %collective-permute-done.21.after), channel_id=1, source_target_pairs={{0,1},{1,0},{2,3},{3,2},{4,5},{5,4},{6,7},{7,6},{8,9},{9,8},{10,11... | collective-permute-start | bytes 983048 | tf_op jit(solution)/shard_map/ppermute | solution.py:48
  107.4 2.5 %collective-permute-start.22 = (bf16[2,320,256]{2,1,0:T(8,128)(2,1)S(1)}, bf16[2,320,256]{2,1,0:T(8,128)(2,1)S(1)}, u32[]{:S(2)}, u32[]{:S(2)}) collective-permute-start(bf16[2,320,256]{2,1,0:T(8,128)(2,1)S(1)} %collective-permute-done.20.before), channel_id=1, source_target_pairs={{0,1},{1,0},{2,3},{3,2},{4,5},{5,4},{6,7},{7,6},{8,9},{9,8},{10,11... | collective-permute-start | bytes 983048 | tf_op jit(solution)/shard_map/ppermute | solution.py:48
  107.9 14.2 %collective-permute-start.26 = (bf16[27,32,256]{2,1,0:T(8,128)(2,1)S(1)}, bf16[27,32,256]{2,1,0:T(8,128)(2,1)S(1)}, u32[]{:S(2)}, u32[]{:S(2)}) collective-permute-start(bf16[27,32,256]{2,1,0:T(8,128)(2,1)S(1)} %get-tuple-element.54), channel_id=1, source_target_pairs={{0,64},{1,17},{2,66},{3,19},{4,68},{5,21},{6,70},{7,23},{8,72},{9,... | collective-permute-start | bytes 1327112 | tf_op jit(solution)/shard_map/ppermute | solution.py:44
  117.3 14.0 %collective-permute-start.31 = (bf16[27,64,256]{2,1,0:T(8,128)(2,1)S(1)}, bf16[27,64,256]{2,1,0:T(8,128)(2,1)S(1)}, u32[]{:S(2)}, u32[]{:S(2)}) collective-permute-start(bf16[27,64,256]{2,1,0:T(8,128)(2,1)S(1)} %get-tuple-element.55), channel_id=1, source_target_pairs={{0,1},{1,0},{2,3},{3,2},{4,5},{5,4},{6,7},{7,6},{8,9},{9,8},{10,11... | collective-permute-start | bytes 2654216 | tf_op jit(solution)/shard_map/ppermute | solution.py:48
  122.2 9.1 %collective-permute-start.27 = (bf16[27,32,256]{2,1,0:T(8,128)(2,1)S(1)}, bf16[27,32,256]{2,1,0:T(8,128)(2,1)S(1)}, u32[]{:S(2)}, u32[]{:S(2)}) collective-permute-start(bf16[27,32,256]{2,1,0:T(8,128)(2,1)S(1)} %collective-permute-done.26.refs_1_), channel_id=1, source_target_pairs={{0,2},{1,7},{2,0},{3,5},{4,6},{5,3},{6,4},{7,1},{8,10},{9,15},{10,... | collective-permute-start | bytes 1327112 | tf_op jit(solution)/shard_map/ppermute | solution.py:44
  125.6 7.8 %collective-permute-start.29 = (bf16[27,64,256]{2,1,0:T(8,128)(2,1)S(1)}, bf16[27,64,256]{2,1,0:T(8,128)(2,1)S(1)}, u32[]{:S(2)}, u32[]{:S(2)}) collective-permute-start(bf16[27,64,256]{2,1,0:T(8,128)(2,1)S(1)} %collective-permute-done.25.refs_1_), channel_id=1, source_target_pairs={{0,1},{1,0},{2,3},{3,2},{4,5},{5,4},{6,7},{7,6},{8,9},{9,8},{10,11... | collective-permute-start | bytes 2654216 | tf_op jit(solution)/shard_map/ppermute | solution.py:48
  125.6 7.8 %collective-permute-start.28 = (bf16[27,64,256]{2,1,0:T(8,128)(2,1)S(1)}, bf16[27,64,256]{2,1,0:T(8,128)(2,1)S(1)}, u32[]{:S(2)}, u32[]{:S(2)}) collective-permute-start(bf16[27,64,256]{2,1,0:T(8,128)(2,1)S(1)} %collective-permute-done.24.refs_0_), channel_id=1, source_target_pairs={{0,1},{1,0},{2,3},{3,2},{4,5},{5,4},{6,7},{7,6},{8,9},{9,8},{10,11... | collective-permute-start | bytes 2654216 | tf_op jit(solution)/shard_map/ppermute | solution.py:48
  126.1 5.2 %collective-permute-start.32 = (bf16[27,32,256]{2,1,0:T(8,128)(2,1)S(1)}, bf16[27,32,256]{2,1,0:T(8,128)(2,1)S(1)}, u32[]{:S(2)}, u32[]{:S(2)}) collective-permute-start(bf16[27,32,256]{2,1,0:T(8,128)(2,1)S(1)} %collective-permute-done.26.refs_1_), channel_id=1, source_target_pairs={{0,1},{1,0},{2,3},{3,2},{4,5},{5,4},{6,7},{7,6},{8,9},{9,8},{10,11... | collective-permute-start | bytes 1327112 | tf_op jit(solution)/shard_map/ppermute | solution.py:48
  131.3 2.1 %collective-permute-start.30 = (bf16[27,32,256]{2,1,0:T(8,128)(2,1)S(1)}, bf16[27,32,256]{2,1,0:T(8,128)(2,1)S(1)}, u32[]{:S(2)}, u32[]{:S(2)}) collective-permute-start(bf16[27,32,256]{2,1,0:T(8,128)(2,1)S(1)} %collective-permute-done.27.refs_2_), channel_id=1, source_target_pairs={{0,1},{1,0},{2,3},{3,2},{4,5},{5,4},{6,7},{7,6},{8,9},{9,8},{10,11... | collective-permute-start | bytes 1327112 | tf_op jit(solution)/shard_map/ppermute | solution.py:48
  (5 other events, 29.4 us)

commit v5 on v4

--- a/solution.py
+++ b/solution.py
@@ -392,7 +392,7 @@
     rows64, rows32, rows16 = (27, 64, CH), (27, 32, CH), (27, 16, CH)
 
     fields, skins = call(
-        pack_kernel, "pack_fields", [pair, skin], [VMEM_SPEC] * 2, [VMEM_SPEC] * 2, [], 1000, 1_000_000, 60,
+        pack_kernel, "pack_fields", [pair, skin], [VMEM_SPEC] * 2, [VMEM_SPEC] * 2, [], 1000, 1_000_000, 8,
     )(features, cotangent)
     before, after = sent_halo(skins)
 

time: 137 us -> 136 us (level)
  no operation moved by 1% of the time
where the time goes in v5:
time: 136 us; the launch traced here: 135 us
  starting transfers between devices  62.5 us (46%)
  waiting for transfers between devices  35.3 us (26%)
  Pallas kernels  29.6 us (22%)
  local copies, waits for them, and re-layouts  4.15 us (3%)
  other arithmetic  2.1 us (2%)
  between operations  1.73 us (1%)
    ppermute x17, starting transfers between devices, ring_send(): return lax.ppermute(array, AXES, pairs)  41.9 us
    ppermute x17, waiting for transfers between devices, ring_send(): return lax.ppermute(array, AXES, pairs)  33.6 us
    ppermute x4, starting transfers between devices, shifted(): lax.ppermute(array, AXES, [(i, i + by) for i in range(128) if 0 <= i + by...  12.5 us
    ppermute x12, starting transfers between devices, swap(): lax.ppermute(array, AXES, [(index, index ^ 1) for index in range(128)])  8.1 us
    pallas_call x1, Pallas kernels, on_device(): call(gradient_kernel, 'weight_grads', [rows64] * 3 + [rows32] * 2 + [pair...  5.06 us
    pallas_call x1, Pallas kernels, on_device(): call(frames_kernel, 'build_frames', [(2 * FRAME_ROWS, TAPS), (FRAME_ROWS,...  3.2 us
    pallas_call x1, Pallas kernels, on_device(): call(grad_input_kernel, 'grad_input_conv', [(1, ROWS, CH), rows64], [VMEM...  2.73 us
  transfers between devices with their start and end apart: 33, of which 10 were waited for; matrix products, arithmetic and copies ran while one was open for 3% of the time, Pallas kernels for 8%

profile of v5, /device:TPU:1, one launch (start us, length us, event | category | flops | bytes accessed | tf_op | source)
XLA Modules:
  0.0 135.4 jit_solution(5536418206952073394)
XLA Ops:
  5.0 5.4 %collective-permute-start.2 = (bf16[2,320,256]{2,1,0:T(8,128)(2,1)}, bf16[2,320,256]{2,1,0:T(8,128)(2,1)}, u32[]{:S(2)}, u32[]{:S(2)}) collective-permute-start(bf16[2,320,256]{2,1,0:T(8,128)(2,1)} %get-tuple-element.33.packed_own), channel_id=1, source_target_pairs={{0,2},{1,3},{2,4},{3,5},{4,6},{5,7},{6,8},{7,9},{8,10},{9,11},{10,... | collective-permute-start | bytes 983048 | tf_op jit(solution)/shard_map/ppermute | solution.py:52
  19.4 3.2 %build_frames.1 = (bf16[1280,2304]{1,0:T(8,128)(2,1)S(1)}, bf16[640,2304]{1,0:T(8,128)(2,1)S(1)}) custom-call(s32[2,27]{1,0:T(2,128)S(1)} %compare_select_fusion.3.pick_ref, s32[6]{0:T(128)S(1)} %stack.43.place_ref, bf16[2,512,256]{2,1,0:T(8,128)(2,1)} %get-tuple-element.32.own, bf16[2,512,256]{2,1,0:T(8,128)(2,1)} %collective-permute-done.1.mate, ...), custom_call_target="tpu_custom_call" | custom-call | flops 1000000 | bytes 12000000 | tf_op jit(solution)/shard_map/build_frames/pallas_call | solution.py:405
  22.6 2.6 %first_conv.1.pre_act_ref = f32[512,256]{1,0:T(8,128)S(1)} custom-call(s32[6]{0:T(128)S(1)} %stack.43.place_ref, bf16[1280,2304]{1,0:T(8,128)(2,1)S(1)} %get-tuple-element.34.frames, bf16[640,2304]{1,0:T(8,128)(2,1)S(1)} %get-tuple-element.35.spare, bf16[27,256,256]{2,1,0:T(8,128)(2,1)S(1)} %copy-done), custom_call_target="tpu_custom_call" | custom-call | flops 1811939328 | bytes 4000000 | tf_op jit(solution)/shard_map/first_conv/pallas_call | solution.py:409
  25.2 2.6 %grad_conv.1.both = bf16[2,512,256]{2,1,0:T(8,128)(2,1)S(1)} custom-call(s32[6]{0:T(128)S(1)} %stack.43.place_ref, bf16[1280,2304]{1,0:T(8,128)(2,1)S(1)} %get-tuple-element.34.frames, bf16[640,2304]{1,0:T(8,128)(2,1)S(1)} %get-tuple-element.35.spare, bf16[27,256,256]{2,1,0:T(8,128)(2,1)S(1)} %copy-done.1, f32[512,256]{1,0:T(8,128)S(1)} %first_conv.1.pre_act_ref), custom_call_target="tpu_custom_call" | custom-call | flops 1811939328 | bytes 4000000 | tf_op jit(solution)/shard_map/grad_conv/pallas_call | solution.py:413
  28.3 1.5 %collective-permute-done.6.both_mate.mate = bf16[2,512,256]{2,1,0:T(8,128)(2,1)S(1)} collective-permute-done((bf16[2,512,256]{2,1,0:T(8,128)(2,1)S(1)}, bf16[2,512,256]{2,1,0:T(8,128)(2,1)S(1)}, u32[]{:S(2)}, u32[]{:S(2)}) %collective-permute-start.6) | collective-permute-done | bytes 524320 | tf_op jit(solution)/shard_map/ppermute | solution.py:48
  29.8 5.1 %weight_grads.1 = (bf16[27,64,256]{2,1,0:T(8,128)(2,1)S(1)}, bf16[27,64,256]{2,1,0:T(8,128)(2,1)S(1)}, bf16[27,64,256]{2,1,0:T(8,128)(2,1)S(1)}, bf16[27,32,256]...) custom-call(s32[6]{0:T(128)S(1)} %stack.43.place_ref, ...), custom_call_target="tpu_custom_call", output_to_operand_aliasing={{5}: (4, {})} | custom-call | flops 3623878656 | bytes 10000000 | tf_op jit(solution)/shard_map/weight_grads/pallas_call | solution.py:419
  34.8 5.1 %collective-permute-start.9 = (bf16[27,32,256]{2,1,0:T(8,128)(2,1)S(1)}, bf16[27,32,256]{2,1,0:T(8,128)(2,1)S(1)}, u32[]{:S(2)}, u32[]{:S(2)}) collective-permute-start(bf16[27,32,256]{2,1,0:T(8,128)(2,1)S(1)} %get-tuple-element.40), channel_id=1, source_target_pairs={{0,2},{1,7},{2,0},{3,5},{4,6},{5,3},{6,4},{7,1},{8,10},{9,15},{10,... | collective-permute-start | bytes 1327112 | tf_op jit(solution)/shard_map/ppermute | solution.py:44
  39.9 2.0 %collective-permute-start.7 = (bf16[27,64,256]{2,1,0:T(8,128)(2,1)S(1)}, bf16[27,64,256]{2,1,0:T(8,128)(2,1)S(1)}, u32[]{:S(2)}, u32[]{:S(2)}) collective-permute-start(bf16[27,64,256]{2,1,0:T(8,128)(2,1)S(1)} %get-tuple-element.37), channel_id=1, source_target_pairs={{0,32},{1,9},{2,34},{3,11},{4,36},{5,13},{6,38},{7,15},{8,40},{9,1... | collective-permute-start | bytes 2654216 | tf_op jit(solution)/shard_map/ppermute | solution.py:44
  41.9 3.9 %collective-permute-start.8 = (bf16[27,64,256]{2,1,0:T(8,128)(2,1)S(1)}, bf16[27,64,256]{2,1,0:T(8,128)(2,1)S(1)}, u32[]{:S(2)}, u32[]{:S(2)}) collective-permute-start(bf16[27,64,256]{2,1,0:T(8,128)(2,1)S(1)} %get-tuple-element.38), channel_id=1, source_target_pairs={{0,96},{1,25},{2,98},{3,27},{4,100},{5,29},{6,102},{7,31},{8,104},... | collective-permute-start | bytes 2654216 | tf_op jit(solution)/shard_map/ppermute | solution.py:44
  45.9 6.7 %collective-permute-start.10 = (bf16[27,32,256]{2,1,0:T(8,128)(2,1)S(1)}, bf16[27,32,256]{2,1,0:T(8,128)(2,1)S(1)}, u32[]{:S(2)}, u32[]{:S(2)}) collective-permute-start(bf16[27,32,256]{2,1,0:T(8,128)(2,1)S(1)} %add_convert_fusion), channel_id=1, source_target_pairs={{0,64},{1,17},{2,66},{3,19},{4,68},{5,21},{6,70},{7,23},{8,72},{9,... | collective-permute-start | bytes 1327112 | tf_op jit(solution)/shard_map/ppermute | solution.py:44
  52.7 9.7 %collective-permute-done.10.across = bf16[27,32,256]{2,1,0:T(8,128)(2,1)S(1)} collective-permute-done((bf16[27,32,256]{2,1,0:T(8,128)(2,1)S(1)}, bf16[27,32,256]{2,1,0:T(8,128)(2,1)S(1)}, u32[]{:S(2)}, u32[]{:S(2)}) %collective-permute-start.10) | collective-permute-done | bytes 442400 | tf_op jit(solution)/shard_map/ppermute | solution.py:44
  63.6 1.4 %collective-permute-start.12 = (bf16[27,16,256]{2,1,0:T(8,128)(2,1)S(1)}, bf16[27,16,256]{2,1,0:T(8,128)(2,1)S(1)}, u32[]{:S(2)}, u32[]{:S(2)}) collective-permute-start(bf16[27,16,256]{2,1,0:T(8,128)(2,1)S(1)} %get-tuple-element.43), channel_id=1, source_target_pairs={{0,8},{1,3},{2,10},{3,5},{4,12},{5,7},{6,14},{7,1},{8,16},{9,11},{... | collective-permute-start | bytes 663560 | tf_op jit(solution)/shard_map/ppermute | solution.py:44
  65.0 1.3 collective-permute-start.13
  66.3 3.6 %collective-permute-done.11 = bf16[27,16,256]{2,1,0:T(8,128)(2,1)S(1)} collective-permute-done((bf16[27,16,256]{2,1,0:T(8,128)(2,1)S(1)}, bf16[27,16,256]{2,1,0:T(8,128)(2,1)S(1)}, u32[]{:S(2)}, u32[]{:S(2)}) %collective-permute-start.11) | collective-permute-done | bytes 221216 | tf_op jit(solution)/shard_map/ppermute | solution.py:44
  69.9 2.1 %collective-permute-done.12 = bf16[27,16,256]{2,1,0:T(8,128)(2,1)S(1)} collective-permute-done((bf16[27,16,256]{2,1,0:T(8,128)(2,1)S(1)}, bf16[27,16,256]{2,1,0:T(8,128)(2,1)S(1)}, u32[]{:S(2)}, u32[]{:S(2)}) %collective-permute-start.12) | collective-permute-done | bytes 221216 | tf_op jit(solution)/shard_map/ppermute | solution.py:44
  72.1 8.1 %collective-permute-start.16 = (bf16[27,16,256]{2,1,0:T(8,128)(2,1)S(1)}, bf16[27,16,256]{2,1,0:T(8,128)(2,1)S(1)}, u32[]{:S(2)}, u32[]{:S(2)}) collective-permute-start(bf16[27,16,256]{2,1,0:T(8,128)(2,1)S(1)} %add_convert_fusion.1), channel_id=1, source_target_pairs={{0,6},{1,97},{2,0},{3,99},{4,2},{5,101},{6,4},{7,103},{8,14},{9,10... | collective-permute-start | bytes 663560 | tf_op jit(solution)/shard_map/ppermute | solution.py:44
  80.2 2.5 %collective-permute-start.14 = (bf16[27,16,256]{2,1,0:T(8,128)(2,1)S(1)}, bf16[27,16,256]{2,1,0:T(8,128)(2,1)S(1)}, u32[]{:S(2)}, u32[]{:S(2)}) collective-permute-start(bf16[27,16,256]{2,1,0:T(8,128)(2,1)S(1)} %add_convert_fusion.1), channel_id=1, source_target_pairs={{0,4},{1,65},{2,6},{3,67},{4,0},{5,69},{6,2},{7,71},{8,12},{9,73},... | collective-permute-start | bytes 663560 | tf_op jit(solution)/shard_map/ppermute | solution.py:44
  83.1 5.5 %collective-permute-done.15 = bf16[27,16,256]{2,1,0:T(8,128)(2,1)S(1)} collective-permute-done((bf16[27,16,256]{2,1,0:T(8,128)(2,1)S(1)}, bf16[27,16,256]{2,1,0:T(8,128)(2,1)S(1)}, u32[]{:S(2)}, u32[]{:S(2)}) %collective-permute-start.15) | collective-permute-done | bytes 221216 | tf_op jit(solution)/shard_map/ppermute | solution.py:44
  88.7 3.3 %collective-permute-start.19 = (bf16[27,16,256]{2,1,0:T(8,128)(2,1)S(1)}, bf16[27,16,256]{2,1,0:T(8,128)(2,1)S(1)}, u32[]{:S(2)}, u32[]{:S(2)}) collective-permute-start(bf16[27,16,256]{2,1,0:T(8,128)(2,1)S(1)} %multiply_convert_fusion.part0), channel_id=1, source_target_pairs={{0,24},{1,7},{2,26},{3,1},{4,28},{5,3},{6,30},{7,5},{8,0},{9,15},{... | collective-permute-start | bytes 663560 | tf_op jit(solution)/shard_map/ppermute | solution.py:44
  94.1 4.5 %collective-permute-start.20 = (bf16[2,320,256]{2,1,0:T(8,128)(2,1)S(1)}, bf16[2,320,256]{2,1,0:T(8,128)(2,1)S(1)}, u32[]{:S(2)}, u32[]{:S(2)}) collective-permute-start(bf16[2,320,256]{2,1,0:T(8,128)(2,1)S(1)} %pack_both.1.packed_own), channel_id=1, source_target_pairs={{0,2},{1,3},{2,4},{3,5},{4,6},{5,7},{6,8},{7,9},{8,10},{9,11},{10,... | collective-permute-start | bytes 983048 | tf_op jit(solution)/shard_map/ppermute | solution.py:52
  98.6 5.6 %collective-permute-done.19.part3 = bf16[27,16,256]{2,1,0:T(8,128)(2,1)S(1)} collective-permute-done((bf16[27,16,256]{2,1,0:T(8,128)(2,1)S(1)}, bf16[27,16,256]{2,1,0:T(8,128)(2,1)S(1)}, u32[]{:S(2)}, u32[]{:S(2)}) %collective-permute-start.19) | collective-permute-done | bytes 221216 | tf_op jit(solution)/shard_map/ppermute | solution.py:44
  105.1 1.5 %collective-permute-start.24 = (bf16[27,64,256]{2,1,0:T(8,128)(2,1)S(1)}, bf16[27,64,256]{2,1,0:T(8,128)(2,1)S(1)}, u32[]{:S(2)}, u32[]{:S(2)}) collective-permute-start(bf16[27,64,256]{2,1,0:T(8,128)(2,1)S(1)} %get-tuple-element.53.refs_0_), channel_id=1, source_target_pairs={{0,32},{1,9},{2,34},{3,11},{4,36},{5,13},{6,38},{7,15},{8,40},{9,1... | collective-permute-start | bytes 2654216 | tf_op jit(solution)/shard_map/ppermute | solution.py:44
  107.1 1.9 %collective-permute-start.26 = (bf16[27,32,256]{2,1,0:T(8,128)(2,1)S(1)}, bf16[27,32,256]{2,1,0:T(8,128)(2,1)S(1)}, u32[]{:S(2)}, u32[]{:S(2)}) collective-permute-start(bf16[27,32,256]{2,1,0:T(8,128)(2,1)S(1)} %get-tuple-element.54), channel_id=1, source_target_pairs={{0,64},{1,17},{2,66},{3,19},{4,68},{5,21},{6,70},{7,23},{8,72},{9,... | collective-permute-start | bytes 1327112 | tf_op jit(solution)/shard_map/ppermute | solution.py:44
  109.1 1.8 %outer_frames.1 = (bf16[640,2304]{1,0:T(8,128)(2,1)S(1)}, bf16[640,2304]{1,0:T(8,128)(2,1)S(1)}) custom-call(s32[2,27]{1,0:T(2,128)S(1)} %compare_select_fusion.3.pick_ref, bf16[2,512,256]{2,1,0:T(8,128)(2,1)S(1)} %get-tuple-element.46.own.waited_for, bf16[2,512,256]{2,1,0:T(8,128)(2,1)S(1)} %collective-permute-done.6.both_mate.mate, ...), custom_call_target="tpu_custom_call" | custom-call | flops 1000000 | bytes 8000000 | tf_op jit(solution)/shard_map/outer_frames/pallas_call | solution.py:464
  111.0 2.7 %output_conv.1 = (bf16[1,512,256]{2,1,0:T(8,128)(2,1)}, bf16[27,64,256]{2,1,0:T(8,128)(2,1)S(1)}) custom-call(bf16[640,2304]{1,0:T(8,128)(2,1)S(1)} %get-tuple-element.47.frame, bf16[27,256,256]{2,1,0:T(8,128)(2,1)S(1)} %copy-done.1, bf16[27,64,256]{2,1,0:T(8,128)(2,1)S(1)} %get-tuple-element.48.passed), custom_call_target="tpu_custom_call", output_to_operand_aliasing={{1}: (2, {})} | custom-call | flops 1811939328 | bytes 4000000 | tf_op jit(solution)/shard_map/output_conv/pallas_call | solution.py:468
  113.6 2.7 %grad_input_conv.1 = (bf16[1,512,256]{2,1,0:T(8,128)(2,1)}, bf16[27,64,256]{2,1,0:T(8,128)(2,1)S(1)}) custom-call(bf16[640,2304]{1,0:T(8,128)(2,1)S(1)} %get-tuple-element.50.frame, bf16[27,256,256]{2,1,0:T(8,128)(2,1)S(1)} %copy-done, bf16[27,64,256]{2,1,0:T(8,128)(2,1)S(1)} %get-tuple-element.51.passed), custom_call_target="tpu_custom_call", output_to_operand_aliasing={{1}: (2, {})} | custom-call | flops 1811939328 | bytes 4000000 | tf_op jit(solution)/shard_map/grad_input_conv/pallas_call | solution.py:472
  116.4 3.4 %collective-permute-start.31 = (bf16[27,64,256]{2,1,0:T(8,128)(2,1)S(1)}, bf16[27,64,256]{2,1,0:T(8,128)(2,1)S(1)}, u32[]{:S(2)}, u32[]{:S(2)}) collective-permute-start(bf16[27,64,256]{2,1,0:T(8,128)(2,1)S(1)} %get-tuple-element.55), channel_id=1, source_target_pairs={{0,1},{1,0},{2,3},{3,2},{4,5},{5,4},{6,7},{7,6},{8,9},{9,8},{10,11... | collective-permute-start | bytes 2654216 | tf_op jit(solution)/shard_map/ppermute | solution.py:48
  119.8 1.5 %collective-permute-done.26.refs_1_ = bf16[27,32,256]{2,1,0:T(8,128)(2,1)S(1)} collective-permute-done((bf16[27,32,256]{2,1,0:T(8,128)(2,1)S(1)}, bf16[27,32,256]{2,1,0:T(8,128)(2,1)S(1)}, u32[]{:S(2)}, u32[]{:S(2)}) %collective-permute-start.26) | collective-permute-done | bytes 442400 | tf_op jit(solution)/shard_map/ppermute | solution.py:44
  121.3 3.4 %collective-permute-start.27 = (bf16[27,32,256]{2,1,0:T(8,128)(2,1)S(1)}, bf16[27,32,256]{2,1,0:T(8,128)(2,1)S(1)}, u32[]{:S(2)}, u32[]{:S(2)}) collective-permute-start(bf16[27,32,256]{2,1,0:T(8,128)(2,1)S(1)} %collective-permute-done.26.refs_1_), channel_id=1, source_target_pairs={{0,2},{1,7},{2,0},{3,5},{4,6},{5,3},{6,4},{7,1},{8,10},{9,15},{10,... | collective-permute-start | bytes 1327112 | tf_op jit(solution)/shard_map/ppermute | solution.py:44
  125.3 5.1 %collective-permute-done.27.refs_2_ = bf16[27,32,256]{2,1,0:T(8,128)(2,1)S(1)} collective-permute-done((bf16[27,32,256]{2,1,0:T(8,128)(2,1)S(1)}, bf16[27,32,256]{2,1,0:T(8,128)(2,1)S(1)}, u32[]{:S(2)}, u32[]{:S(2)}) %collective-permute-start.27) | collective-permute-done | bytes 442400 | tf_op jit(solution)/shard_map/ppermute | solution.py:44
  130.4 2.1 %place_early.1 = (bf16[27,256,256]{2,1,0:T(8,128)(2,1)}, bf16[27,256,256]{2,1,0:T(8,128)(2,1)}) custom-call(s32[6]{0:T(128)S(1)} %stack.43.place_ref, bf16[27,64,256]{2,1,0:T(8,128)(2,1)S(1)} %get-tuple-element.53.refs_0_, bf16[27,32,256]{2,1,0:T(8,128)(2,1)S(1)} %collective-permute-done.26.refs_1_, ...), custom_call_target="tpu_custom_call" | custom-call | flops 1000 | bytes 5000000 | tf_op jit(solution)/shard_map/place_early/pallas_call | solution.py:478
  132.5 2.7 %place_late.1 = (bf16[27,256,256]{2,1,0:T(8,128)(2,1)}, bf16[27,256,256]{2,1,0:T(8,128)(2,1)}) custom-call(s32[6]{0:T(128)S(1)} %stack.43.place_ref, bf16[27,64,256]{2,1,0:T(8,128)(2,1)S(1)} %collective-permute-done.24.refs_0_, bf16[27,64,256]{2,1,0:T(8,128)(2,1)S(1)} %collective-permute-done.25.refs_1_, ...), custom_call_target="tpu_custom_call", output_to_operand_aliasing={{0}: (7, {}), {1}: (8, {})} | custom-call | flops 1000 | bytes 9000000 | tf_op jit(solution)/shard_map/place_late/pallas_call | solution.py:484
  (71 shorter events, 19.2 us)
Async XLA Ops:
  3.7 12.3 %collective-permute-start.3 = (bf16[2,320,256]{2,1,0:T(8,128)(2,1)}, bf16[2,320,256]{2,1,0:T(8,128)(2,1)}, u32[]{:S(2)}, u32[]{:S(2)}) collective-permute-start(bf16[2,320,256]{2,1,0:T(8,128)(2,1)} %get-tuple-element.33.packed_own), channel_id=1, source_target_pairs={{2,0},{3,1},{4,2},{5,3},{6,4},{7,5},{8,6},{9,7},{10,8},{11,9},{12,... | collective-permute-start | bytes 983048 | tf_op jit(solution)/shard_map/ppermute | solution.py:52
  5.0 11.7 %collective-permute-start.2 = (bf16[2,320,256]{2,1,0:T(8,128)(2,1)}, bf16[2,320,256]{2,1,0:T(8,128)(2,1)}, u32[]{:S(2)}, u32[]{:S(2)}) collective-permute-start(bf16[2,320,256]{2,1,0:T(8,128)(2,1)} %get-tuple-element.33.packed_own), channel_id=1, source_target_pairs={{0,2},{1,3},{2,4},{3,5},{4,6},{5,7},{6,8},{7,9},{8,10},{9,11},{10,... | collective-permute-start | bytes 983048 | tf_op jit(solution)/shard_map/ppermute | solution.py:52
  11.8 3.4 %collective-permute-start = (s32[1,27]{1,0:T(1,128)S(1)}, s32[1,27]{1,0:T(1,128)S(1)}, u32[]{:S(2)}, u32[]{:S(2)}) collective-permute-start(s32[1,27]{1,0:T(1,128)S(1)} %pad_add_fusion.2), channel_id=1, source_target_pairs={{0,1},{1,0},{2,3},{3,2},{4,5},{5,4},{6,7},{7,6},{8,9},{9,8},{10,11... | collective-permute-start | bytes 332 | tf_op jit(solution)/shard_map/ppermute | solution.py:48
  13.1 4.9 %collective-permute-start.1 = (bf16[2,512,256]{2,1,0:T(8,128)(2,1)}, bf16[2,512,256]{2,1,0:T(8,128)(2,1)}, u32[]{:S(2)}, u32[]{:S(2)}) collective-permute-start(bf16[2,512,256]{2,1,0:T(8,128)(2,1)} %get-tuple-element.32.own), channel_id=1, source_target_pairs={{0,1},{1,0},{2,3},{3,2},{4,5},{5,4},{6,7},{7,6},{8,9},{9,8},{10,11... | collective-permute-start | bytes 1572872 | tf_op jit(solution)/shard_map/ppermute | solution.py:48
  16.0 3.1 %collective-permute-start.5 = (bf16[2,320,256]{2,1,0:T(8,128)(2,1)}, bf16[2,320,256]{2,1,0:T(8,128)(2,1)S(1)}, u32[]{:S(2)}, u32[]{:S(2)}) collective-permute-start(bf16[2,320,256]{2,1,0:T(8,128)(2,1)} %collective-permute-done.3.after), channel_id=1, source_target_pairs={{0,1},{1,0},{2,3},{3,2},{4,5},{5,4},{6,7},{7,6},{8,9},{9,8},{10,11... | collective-permute-start | bytes 983048 | tf_op jit(solution)/shard_map/ppermute | solution.py:48
  16.7 2.6 %collective-permute-start.4 = (bf16[2,320,256]{2,1,0:T(8,128)(2,1)}, bf16[2,320,256]{2,1,0:T(8,128)(2,1)S(1)}, u32[]{:S(2)}, u32[]{:S(2)}) collective-permute-start(bf16[2,320,256]{2,1,0:T(8,128)(2,1)} %collective-permute-done.2.before), channel_id=1, source_target_pairs={{0,1},{1,0},{2,3},{3,2},{4,5},{5,4},{6,7},{7,6},{8,9},{9,8},{10,11... | collective-permute-start | bytes 983048 | tf_op jit(solution)/shard_map/ppermute | solution.py:48
  34.8 11.0 %collective-permute-start.9 = (bf16[27,32,256]{2,1,0:T(8,128)(2,1)S(1)}, bf16[27,32,256]{2,1,0:T(8,128)(2,1)S(1)}, u32[]{:S(2)}, u32[]{:S(2)}) collective-permute-start(bf16[27,32,256]{2,1,0:T(8,128)(2,1)S(1)} %get-tuple-element.40), channel_id=1, source_target_pairs={{0,2},{1,7},{2,0},{3,5},{4,6},{5,3},{6,4},{7,1},{8,10},{9,15},{10,... | collective-permute-start | bytes 1327112 | tf_op jit(solution)/shard_map/ppermute | solution.py:44
  39.9 22.5 %collective-permute-start.7 = (bf16[27,64,256]{2,1,0:T(8,128)(2,1)S(1)}, bf16[27,64,256]{2,1,0:T(8,128)(2,1)S(1)}, u32[]{:S(2)}, u32[]{:S(2)}) collective-permute-start(bf16[27,64,256]{2,1,0:T(8,128)(2,1)S(1)} %get-tuple-element.37), channel_id=1, source_target_pairs={{0,32},{1,9},{2,34},{3,11},{4,36},{5,13},{6,38},{7,15},{8,40},{9,1... | collective-permute-start | bytes 2654216 | tf_op jit(solution)/shard_map/ppermute | solution.py:44
  41.9 20.5 %collective-permute-start.8 = (bf16[27,64,256]{2,1,0:T(8,128)(2,1)S(1)}, bf16[27,64,256]{2,1,0:T(8,128)(2,1)S(1)}, u32[]{:S(2)}, u32[]{:S(2)}) collective-permute-start(bf16[27,64,256]{2,1,0:T(8,128)(2,1)S(1)} %get-tuple-element.38), channel_id=1, source_target_pairs={{0,96},{1,25},{2,98},{3,27},{4,100},{5,29},{6,102},{7,31},{8,104},... | collective-permute-start | bytes 2654216 | tf_op jit(solution)/shard_map/ppermute | solution.py:44
  45.9 16.5 %collective-permute-start.10 = (bf16[27,32,256]{2,1,0:T(8,128)(2,1)S(1)}, bf16[27,32,256]{2,1,0:T(8,128)(2,1)S(1)}, u32[]{:S(2)}, u32[]{:S(2)}) collective-permute-start(bf16[27,32,256]{2,1,0:T(8,128)(2,1)S(1)} %add_convert_fusion), channel_id=1, source_target_pairs={{0,64},{1,17},{2,66},{3,19},{4,68},{5,21},{6,70},{7,23},{8,72},{9,... | collective-permute-start | bytes 1327112 | tf_op jit(solution)/shard_map/ppermute | solution.py:44
  63.5 6.5 %collective-permute-start.11 = (bf16[27,16,256]{2,1,0:T(8,128)(2,1)S(1)}, bf16[27,16,256]{2,1,0:T(8,128)(2,1)S(1)}, u32[]{:S(2)}, u32[]{:S(2)}) collective-permute-start(bf16[27,16,256]{2,1,0:T(8,128)(2,1)S(1)} %get-tuple-element.42), channel_id=1, source_target_pairs={{0,16},{1,5},{2,18},{3,7},{4,20},{5,1},{6,22},{7,3},{8,24},{9,13},... | collective-permute-start | bytes 663560 | tf_op jit(solution)/shard_map/ppermute | solution.py:44
  63.6 8.4 %collective-permute-start.12 = (bf16[27,16,256]{2,1,0:T(8,128)(2,1)S(1)}, bf16[27,16,256]{2,1,0:T(8,128)(2,1)S(1)}, u32[]{:S(2)}, u32[]{:S(2)}) collective-permute-start(bf16[27,16,256]{2,1,0:T(8,128)(2,1)S(1)} %get-tuple-element.43), channel_id=1, source_target_pairs={{0,8},{1,3},{2,10},{3,5},{4,12},{5,7},{6,14},{7,1},{8,16},{9,11},{... | collective-permute-start | bytes 663560 | tf_op jit(solution)/shard_map/ppermute | solution.py:44
  65.0 7.0 %collective-permute-start.13 = (bf16[27,16,256]{2,1,0:T(8,128)(2,1)S(1)}, bf16[27,16,256]{2,1,0:T(8,128)(2,1)S(1)}, u32[]{:S(2)}, u32[]{:S(2)}) collective-permute-start(bf16[27,16,256]{2,1,0:T(8,128)(2,1)S(1)} %get-tuple-element.44), channel_id=1, source_target_pairs={{0,24},{1,7},{2,26},{3,1},{4,28},{5,3},{6,30},{7,5},{8,0},{9,15},{... | collective-permute-start | bytes 663560 | tf_op jit(solution)/shard_map/ppermute | solution.py:44
  72.1 11.0 %collective-permute-start.16 = (bf16[27,16,256]{2,1,0:T(8,128)(2,1)S(1)}, bf16[27,16,256]{2,1,0:T(8,128)(2,1)S(1)}, u32[]{:S(2)}, u32[]{:S(2)}) collective-permute-start(bf16[27,16,256]{2,1,0:T(8,128)(2,1)S(1)} %add_convert_fusion.1), channel_id=1, source_target_pairs={{0,6},{1,97},{2,0},{3,99},{4,2},{5,101},{6,4},{7,103},{8,14},{9,10... | collective-permute-start | bytes 663560 | tf_op jit(solution)/shard_map/ppermute | solution.py:44
  80.2 8.4 %collective-permute-start.15 = (bf16[27,16,256]{2,1,0:T(8,128)(2,1)S(1)}, bf16[27,16,256]{2,1,0:T(8,128)(2,1)S(1)}, u32[]{:S(2)}, u32[]{:S(2)}) collective-permute-start(bf16[27,16,256]{2,1,0:T(8,128)(2,1)S(1)} %add_convert_fusion.1), channel_id=1, source_target_pairs={{0,2},{1,33},{2,4},{3,35},{4,6},{5,37},{6,0},{7,39},{8,10},{9,41},... | collective-permute-start | bytes 663560 | tf_op jit(solution)/shard_map/ppermute | solution.py:44
  80.2 8.4 %collective-permute-start.14 = (bf16[27,16,256]{2,1,0:T(8,128)(2,1)S(1)}, bf16[27,16,256]{2,1,0:T(8,128)(2,1)S(1)}, u32[]{:S(2)}, u32[]{:S(2)}) collective-permute-start(bf16[27,16,256]{2,1,0:T(8,128)(2,1)S(1)} %add_convert_fusion.1), channel_id=1, source_target_pairs={{0,4},{1,65},{2,6},{3,67},{4,0},{5,69},{6,2},{7,71},{8,12},{9,73},... | collective-permute-start | bytes 663560 | tf_op jit(solution)/shard_map/ppermute | solution.py:44
  88.7 15.5 %collective-permute-start.19 = (bf16[27,16,256]{2,1,0:T(8,128)(2,1)S(1)}, bf16[27,16,256]{2,1,0:T(8,128)(2,1)S(1)}, u32[]{:S(2)}, u32[]{:S(2)}) collective-permute-start(bf16[27,16,256]{2,1,0:T(8,128)(2,1)S(1)} %multiply_convert_fusion.part0), channel_id=1, source_target_pairs={{0,24},{1,7},{2,26},{3,1},{4,28},{5,3},{6,30},{7,5},{8,0},{9,15},{... | collective-permute-start | bytes 663560 | tf_op jit(solution)/shard_map/ppermute | solution.py:44
  92.0 12.3 %collective-permute-start.18 = (bf16[27,16,256]{2,1,0:T(8,128)(2,1)S(1)}, bf16[27,16,256]{2,1,0:T(8,128)(2,1)S(1)}, u32[]{:S(2)}, u32[]{:S(2)}) collective-permute-start(bf16[27,16,256]{2,1,0:T(8,128)(2,1)S(1)} %multiply_convert_fusion.part0), channel_id=1, source_target_pairs={{0,16},{1,5},{2,18},{3,7},{4,20},{5,1},{6,22},{7,3},{8,24},{9,13},... | collective-permute-start | bytes 663560 | tf_op jit(solution)/shard_map/ppermute | solution.py:44
  92.0 12.3 %collective-permute-start.17 = (bf16[27,16,256]{2,1,0:T(8,128)(2,1)S(1)}, bf16[27,16,256]{2,1,0:T(8,128)(2,1)S(1)}, u32[]{:S(2)}, u32[]{:S(2)}) collective-permute-start(bf16[27,16,256]{2,1,0:T(8,128)(2,1)S(1)} %multiply_convert_fusion.part0), channel_id=1, source_target_pairs={{0,8},{1,3},{2,10},{3,5},{4,12},{5,7},{6,14},{7,1},{8,16},{9,11},{... | collective-permute-start | bytes 663560 | tf_op jit(solution)/shard_map/ppermute | solution.py:44
  92.8 13.8 %collective-permute-start.21 = (bf16[2,320,256]{2,1,0:T(8,128)(2,1)S(1)}, bf16[2,320,256]{2,1,0:T(8,128)(2,1)S(1)}, u32[]{:S(2)}, u32[]{:S(2)}) collective-permute-start(bf16[2,320,256]{2,1,0:T(8,128)(2,1)S(1)} %pack_both.1.packed_own), channel_id=1, source_target_pairs={{2,0},{3,1},{4,2},{5,3},{6,4},{7,5},{8,6},{9,7},{10,8},{11,9},{12,... | collective-permute-start | bytes 983048 | tf_op jit(solution)/shard_map/ppermute | solution.py:52
  94.1 12.5 %collective-permute-start.20 = (bf16[2,320,256]{2,1,0:T(8,128)(2,1)S(1)}, bf16[2,320,256]{2,1,0:T(8,128)(2,1)S(1)}, u32[]{:S(2)}, u32[]{:S(2)}) collective-permute-start(bf16[2,320,256]{2,1,0:T(8,128)(2,1)S(1)} %pack_both.1.packed_own), channel_id=1, source_target_pairs={{0,2},{1,3},{2,4},{3,5},{4,6},{5,7},{6,8},{7,9},{8,10},{9,11},{10,... | collective-permute-start | bytes 983048 | tf_op jit(solution)/shard_map/ppermute | solution.py:52
  105.0 19.7 %collective-permute-start.25 = (bf16[27,64,256]{2,1,0:T(8,128)(2,1)S(1)}, bf16[27,64,256]{2,1,0:T(8,128)(2,1)S(1)}, u32[]{:S(2)}, u32[]{:S(2)}) collective-permute-start(bf16[27,64,256]{2,1,0:T(8,128)(2,1)S(1)} %get-tuple-element.53.refs_0_), channel_id=1, source_target_pairs={{0,96},{1,25},{2,98},{3,27},{4,100},{5,29},{6,102},{7,31},{8,104},... | collective-permute-start | bytes 2654216 | tf_op jit(solution)/shard_map/ppermute | solution.py:44
  105.1 19.6 %collective-permute-start.24 = (bf16[27,64,256]{2,1,0:T(8,128)(2,1)S(1)}, bf16[27,64,256]{2,1,0:T(8,128)(2,1)S(1)}, u32[]{:S(2)}, u32[]{:S(2)}) collective-permute-start(bf16[27,64,256]{2,1,0:T(8,128)(2,1)S(1)} %get-tuple-element.53.refs_0_), channel_id=1, source_target_pairs={{0,32},{1,9},{2,34},{3,11},{4,36},{5,13},{6,38},{7,15},{8,40},{9,1... | collective-permute-start | bytes 2654216 | tf_op jit(solution)/shard_map/ppermute | solution.py:44
  106.6 2.5 %collective-permute-start.23 = (bf16[2,320,256]{2,1,0:T(8,128)(2,1)S(1)}, bf16[2,320,256]{2,1,0:T(8,128)(2,1)S(1)}, u32[]{:S(2)}, u32[]{:S(2)}) collective-permute-start(bf16[2,320,256]{2,1,0:T(8,128)(2,1)S(1)} %collective-permute-done.21.after), channel_id=1, source_target_pairs={{0,1},{1,0},{2,3},{3,2},{4,5},{5,4},{6,7},{7,6},{8,9},{9,8},{10,11... | collective-permute-start | bytes 983048 | tf_op jit(solution)/shard_map/ppermute | solution.py:48
  106.6 2.6 %collective-permute-start.22 = (bf16[2,320,256]{2,1,0:T(8,128)(2,1)S(1)}, bf16[2,320,256]{2,1,0:T(8,128)(2,1)S(1)}, u32[]{:S(2)}, u32[]{:S(2)}) collective-permute-start(bf16[2,320,256]{2,1,0:T(8,128)(2,1)S(1)} %collective-permute-done.20.before), channel_id=1, source_target_pairs={{0,1},{1,0},{2,3},{3,2},{4,5},{5,4},{6,7},{7,6},{8,9},{9,8},{10,11... | collective-permute-start | bytes 983048 | tf_op jit(solution)/shard_map/ppermute | solution.py:48
  107.1 14.2 %collective-permute-start.26 = (bf16[27,32,256]{2,1,0:T(8,128)(2,1)S(1)}, bf16[27,32,256]{2,1,0:T(8,128)(2,1)S(1)}, u32[]{:S(2)}, u32[]{:S(2)}) collective-permute-start(bf16[27,32,256]{2,1,0:T(8,128)(2,1)S(1)} %get-tuple-element.54), channel_id=1, source_target_pairs={{0,64},{1,17},{2,66},{3,19},{4,68},{5,21},{6,70},{7,23},{8,72},{9,... | collective-permute-start | bytes 1327112 | tf_op jit(solution)/shard_map/ppermute | solution.py:44
  116.4 14.0 %collective-permute-start.31 = (bf16[27,64,256]{2,1,0:T(8,128)(2,1)S(1)}, bf16[27,64,256]{2,1,0:T(8,128)(2,1)S(1)}, u32[]{:S(2)}, u32[]{:S(2)}) collective-permute-start(bf16[27,64,256]{2,1,0:T(8,128)(2,1)S(1)} %get-tuple-element.55), channel_id=1, source_target_pairs={{0,1},{1,0},{2,3},{3,2},{4,5},{5,4},{6,7},{7,6},{8,9},{9,8},{10,11... | collective-permute-start | bytes 2654216 | tf_op jit(solution)/shard_map/ppermute | solution.py:48
  121.3 9.1 %collective-permute-start.27 = (bf16[27,32,256]{2,1,0:T(8,128)(2,1)S(1)}, bf16[27,32,256]{2,1,0:T(8,128)(2,1)S(1)}, u32[]{:S(2)}, u32[]{:S(2)}) collective-permute-start(bf16[27,32,256]{2,1,0:T(8,128)(2,1)S(1)} %collective-permute-done.26.refs_1_), channel_id=1, source_target_pairs={{0,2},{1,7},{2,0},{3,5},{4,6},{5,3},{6,4},{7,1},{8,10},{9,15},{10,... | collective-permute-start | bytes 1327112 | tf_op jit(solution)/shard_map/ppermute | solution.py:44
  124.7 7.8 %collective-permute-start.29 = (bf16[27,64,256]{2,1,0:T(8,128)(2,1)S(1)}, bf16[27,64,256]{2,1,0:T(8,128)(2,1)S(1)}, u32[]{:S(2)}, u32[]{:S(2)}) collective-permute-start(bf16[27,64,256]{2,1,0:T(8,128)(2,1)S(1)} %collective-permute-done.25.refs_1_), channel_id=1, source_target_pairs={{0,1},{1,0},{2,3},{3,2},{4,5},{5,4},{6,7},{7,6},{8,9},{9,8},{10,11... | collective-permute-start | bytes 2654216 | tf_op jit(solution)/shard_map/ppermute | solution.py:48
  124.7 7.8 %collective-permute-start.28 = (bf16[27,64,256]{2,1,0:T(8,128)(2,1)S(1)}, bf16[27,64,256]{2,1,0:T(8,128)(2,1)S(1)}, u32[]{:S(2)}, u32[]{:S(2)}) collective-permute-start(bf16[27,64,256]{2,1,0:T(8,128)(2,1)S(1)} %collective-permute-done.24.refs_0_), channel_id=1, source_target_pairs={{0,1},{1,0},{2,3},{3,2},{4,5},{5,4},{6,7},{7,6},{8,9},{9,8},{10,11... | collective-permute-start | bytes 2654216 | tf_op jit(solution)/shard_map/ppermute | solution.py:48
  125.2 5.2 %collective-permute-start.32 = (bf16[27,32,256]{2,1,0:T(8,128)(2,1)S(1)}, bf16[27,32,256]{2,1,0:T(8,128)(2,1)S(1)}, u32[]{:S(2)}, u32[]{:S(2)}) collective-permute-start(bf16[27,32,256]{2,1,0:T(8,128)(2,1)S(1)} %collective-permute-done.26.refs_1_), channel_id=1, source_target_pairs={{0,1},{1,0},{2,3},{3,2},{4,5},{5,4},{6,7},{7,6},{8,9},{9,8},{10,11... | collective-permute-start | bytes 1327112 | tf_op jit(solution)/shard_map/ppermute | solution.py:48
  130.4 2.1 %collective-permute-start.30 = (bf16[27,32,256]{2,1,0:T(8,128)(2,1)S(1)}, bf16[27,32,256]{2,1,0:T(8,128)(2,1)S(1)}, u32[]{:S(2)}, u32[]{:S(2)}) collective-permute-start(bf16[27,32,256]{2,1,0:T(8,128)(2,1)S(1)} %collective-permute-done.27.refs_2_), channel_id=1, source_target_pairs={{0,1},{1,0},{2,3},{3,2},{4,5},{5,4},{6,7},{7,6},{8,9},{9,8},{10,11... | collective-permute-start | bytes 1327112 | tf_op jit(solution)/shard_map/ppermute | solution.py:48
  (5 other events, 28.6 us)

commit v6 on v5

--- a/solution.py
+++ b/solution.py
@@ -473,19 +473,20 @@
         grad_input_kernel, "grad_input_conv", [(1, ROWS, CH), rows64], [VMEM_SPEC] * 2 + [ANY_SPEC],
         [VMEM_SPEC, ANY_SPEC], [], flops, 4_000_000, 14, {2: 1},
     )(frame_grad, weight_one, again)
-    early = [(0, 0), (2, 0)]
-    late = [(3, 0), (1, 0), (2, 1)]
+    hows = [(0, 0), (2, 0), (3, 0), (1, 0), (2, 1)]
+    mates = [swap(again), swap(half)]
     grad_one, grad_two = call(
-        partial(place_kernel, early), "place_early", [(27, CH, CH)] * 2,
+        partial(place_kernel, []), "place_early", [(27, CH, CH)] * 2,
         [SMEM_SPEC] + [VMEM_SPEC] * 4, [ANY_SPEC] * 2,
         [pltpu.SemaphoreType.DMA((2, 2))], 1000, 5_000_000, 12,
-    )(place, wide, half, swap(again), swap(half))
+    )(place, wide, half, *mates)
     chunks = [from_before, from_after, other_half]
+    mates += [swap(chunk) for chunk in chunks]
     grad_one, grad_two = call(
-        partial(place_kernel, late), "place_late", [(27, CH, CH)] * 2,
-        [SMEM_SPEC] + [VMEM_SPEC] * 6 + [ANY_SPEC] * 2, [ANY_SPEC] * 2,
-        [pltpu.SemaphoreType.DMA((2, 3))], 1000, 9_000_000, 12, {7: 0, 8: 1},
-    )(place, *chunks, *[swap(chunk) for chunk in chunks], grad_one, grad_two)
+        partial(place_kernel, hows), "place_late", [(27, CH, CH)] * 2,
+        [SMEM_SPEC] + [VMEM_SPEC] * 10 + [ANY_SPEC] * 2, [ANY_SPEC] * 2,
+        [pltpu.SemaphoreType.DMA((2, 5))], 1000, 14_000_000, 16, {11: 0, 12: 1},
+    )(place, wide, half, *chunks, *mates, grad_one, grad_two)
     return output, grad_input, grad_one, grad_two
 
 

time: 136 us -> 136 us (level)
  transfers between devices with their start and end apart: 33 -> 33, of which waited for: 10 -> 11; matrix products, arithmetic and copies ran while one was open for 3% -> 3% of each run, Pallas kernels for 8% -> 7%
where the time goes in v6:
time: 136 us
  starting transfers between devices  62.5 us (46%)
  waiting for transfers between devices  36.5 us (27%)
  Pallas kernels  28.9 us (21%)
  local copies, waits for them, and re-layouts  4.15 us (3%)
  other arithmetic  2.1 us (2%)
  between operations  1.71 us (1%)
    ppermute x17, starting transfers between devices, ring_send(): return lax.ppermute(array, AXES, pairs)  41.9 us
    ppermute x17, waiting for transfers between devices, ring_send(): return lax.ppermute(array, AXES, pairs)  33.6 us
    ppermute x4, starting transfers between devices, shifted(): lax.ppermute(array, AXES, [(i, i + by) for i in range(128) if 0 <= i + by...  12.5 us
    ppermute x12, starting transfers between devices, swap(): lax.ppermute(array, AXES, [(index, index ^ 1) for index in range(128)])  8.11 us
    pallas_call x1, Pallas kernels, on_device(): call(gradient_kernel, 'weight_grads', [rows64] * 3 + [rows32] * 2 + [pair...  5.06 us
    pallas_call x1, Pallas kernels, on_device(): call(partial(place_kernel, hows), 'place_late', [(27, CH, CH)] * 2, [SMEM...  3.53 us
    pallas_call x1, Pallas kernels, on_device(): call(frames_kernel, 'build_frames', [(2 * FRAME_ROWS, TAPS), (FRAME_ROWS,...  3.2 us
    ppermute x12, waiting for transfers between devices, swap(): lax.ppermute(array, AXES, [(index, index ^ 1) for index in range(128)])  2.9 us
  transfers between devices with their start and end apart: 33, of which 11 were waited for; matrix products, arithmetic and copies ran while one was open for 3% of the time, Pallas kernels for 7%

profile of v6, /device:TPU:1, one launch (start us, length us, event | category | flops | bytes accessed | tf_op | source)
XLA Modules:
  0.0 135.9 jit_solution(2104898566313147688)
XLA Ops:
  5.0 5.4 %collective-permute-start.2 = (bf16[2,320,256]{2,1,0:T(8,128)(2,1)}, bf16[2,320,256]{2,1,0:T(8,128)(2,1)}, u32[]{:S(2)}, u32[]{:S(2)}) collective-permute-start(bf16[2,320,256]{2,1,0:T(8,128)(2,1)} %get-tuple-element.33.packed_own), channel_id=1, source_target_pairs={{0,2},{1,3},{2,4},{3,5},{4,6},{5,7},{6,8},{7,9},{8,10},{9,11},{10,... | collective-permute-start | bytes 983048 | tf_op jit(solution)/shard_map/ppermute | solution.py:52
  11.8 1.3 collective-permute-start
  19.4 3.2 %build_frames.1 = (bf16[1280,2304]{1,0:T(8,128)(2,1)S(1)}, bf16[640,2304]{1,0:T(8,128)(2,1)S(1)}) custom-call(s32[2,27]{1,0:T(2,128)S(1)} %compare_select_fusion.3.pick_ref, s32[6]{0:T(128)S(1)} %stack.43.place_ref, bf16[2,512,256]{2,1,0:T(8,128)(2,1)} %get-tuple-element.32.own, bf16[2,512,256]{2,1,0:T(8,128)(2,1)} %collective-permute-done.1.mate, ...), custom_call_target="tpu_custom_call" | custom-call | flops 1000000 | bytes 12000000 | tf_op jit(solution)/shard_map/build_frames/pallas_call | solution.py:405
  22.6 2.6 %first_conv.1.pre_act_ref = f32[512,256]{1,0:T(8,128)S(1)} custom-call(s32[6]{0:T(128)S(1)} %stack.43.place_ref, bf16[1280,2304]{1,0:T(8,128)(2,1)S(1)} %get-tuple-element.34.frames, bf16[640,2304]{1,0:T(8,128)(2,1)S(1)} %get-tuple-element.35.spare, bf16[27,256,256]{2,1,0:T(8,128)(2,1)S(1)} %copy-done), custom_call_target="tpu_custom_call" | custom-call | flops 1811939328 | bytes 4000000 | tf_op jit(solution)/shard_map/first_conv/pallas_call | solution.py:409
  25.2 2.6 %grad_conv.1.both = bf16[2,512,256]{2,1,0:T(8,128)(2,1)S(1)} custom-call(s32[6]{0:T(128)S(1)} %stack.43.place_ref, bf16[1280,2304]{1,0:T(8,128)(2,1)S(1)} %get-tuple-element.34.frames, bf16[640,2304]{1,0:T(8,128)(2,1)S(1)} %get-tuple-element.35.spare, bf16[27,256,256]{2,1,0:T(8,128)(2,1)S(1)} %copy-done.1, f32[512,256]{1,0:T(8,128)S(1)} %first_conv.1.pre_act_ref), custom_call_target="tpu_custom_call" | custom-call | flops 1811939328 | bytes 4000000 | tf_op jit(solution)/shard_map/grad_conv/pallas_call | solution.py:413
  28.3 1.5 %collective-permute-done.6.both_mate.mate = bf16[2,512,256]{2,1,0:T(8,128)(2,1)S(1)} collective-permute-done((bf16[2,512,256]{2,1,0:T(8,128)(2,1)S(1)}, bf16[2,512,256]{2,1,0:T(8,128)(2,1)S(1)}, u32[]{:S(2)}, u32[]{:S(2)}) %collective-permute-start.6) | collective-permute-done | bytes 524320 | tf_op jit(solution)/shard_map/ppermute | solution.py:48
  29.8 5.1 %weight_grads.1 = (bf16[27,64,256]{2,1,0:T(8,128)(2,1)S(1)}, bf16[27,64,256]{2,1,0:T(8,128)(2,1)S(1)}, bf16[27,64,256]{2,1,0:T(8,128)(2,1)S(1)}, bf16[27,32,256]...) custom-call(s32[6]{0:T(128)S(1)} %stack.43.place_ref, ...), custom_call_target="tpu_custom_call", output_to_operand_aliasing={{5}: (4, {})} | custom-call | flops 3623878656 | bytes 10000000 | tf_op jit(solution)/shard_map/weight_grads/pallas_call | solution.py:419
  34.8 5.1 %collective-permute-start.9 = (bf16[27,32,256]{2,1,0:T(8,128)(2,1)S(1)}, bf16[27,32,256]{2,1,0:T(8,128)(2,1)S(1)}, u32[]{:S(2)}, u32[]{:S(2)}) collective-permute-start(bf16[27,32,256]{2,1,0:T(8,128)(2,1)S(1)} %get-tuple-element.40), channel_id=1, source_target_pairs={{0,2},{1,7},{2,0},{3,5},{4,6},{5,3},{6,4},{7,1},{8,10},{9,15},{10,... | collective-permute-start | bytes 1327112 | tf_op jit(solution)/shard_map/ppermute | solution.py:44
  39.9 2.0 %collective-permute-start.7 = (bf16[27,64,256]{2,1,0:T(8,128)(2,1)S(1)}, bf16[27,64,256]{2,1,0:T(8,128)(2,1)S(1)}, u32[]{:S(2)}, u32[]{:S(2)}) collective-permute-start(bf16[27,64,256]{2,1,0:T(8,128)(2,1)S(1)} %get-tuple-element.37), channel_id=1, source_target_pairs={{0,32},{1,9},{2,34},{3,11},{4,36},{5,13},{6,38},{7,15},{8,40},{9,1... | collective-permute-start | bytes 2654216 | tf_op jit(solution)/shard_map/ppermute | solution.py:44
  41.9 3.9 %collective-permute-start.8 = (bf16[27,64,256]{2,1,0:T(8,128)(2,1)S(1)}, bf16[27,64,256]{2,1,0:T(8,128)(2,1)S(1)}, u32[]{:S(2)}, u32[]{:S(2)}) collective-permute-start(bf16[27,64,256]{2,1,0:T(8,128)(2,1)S(1)} %get-tuple-element.38), channel_id=1, source_target_pairs={{0,96},{1,25},{2,98},{3,27},{4,100},{5,29},{6,102},{7,31},{8,104},... | collective-permute-start | bytes 2654216 | tf_op jit(solution)/shard_map/ppermute | solution.py:44
  45.9 6.7 %collective-permute-start.10 = (bf16[27,32,256]{2,1,0:T(8,128)(2,1)S(1)}, bf16[27,32,256]{2,1,0:T(8,128)(2,1)S(1)}, u32[]{:S(2)}, u32[]{:S(2)}) collective-permute-start(bf16[27,32,256]{2,1,0:T(8,128)(2,1)S(1)} %add_convert_fusion), channel_id=1, source_target_pairs={{0,64},{1,17},{2,66},{3,19},{4,68},{5,21},{6,70},{7,23},{8,72},{9,... | collective-permute-start | bytes 1327112 | tf_op jit(solution)/shard_map/ppermute | solution.py:44
  52.7 9.7 %collective-permute-done.10.across = bf16[27,32,256]{2,1,0:T(8,128)(2,1)S(1)} collective-permute-done((bf16[27,32,256]{2,1,0:T(8,128)(2,1)S(1)}, bf16[27,32,256]{2,1,0:T(8,128)(2,1)S(1)}, u32[]{:S(2)}, u32[]{:S(2)}) %collective-permute-start.10) | collective-permute-done | bytes 442400 | tf_op jit(solution)/shard_map/ppermute | solution.py:44
  63.6 1.4 %collective-permute-start.12 = (bf16[27,16,256]{2,1,0:T(8,128)(2,1)S(1)}, bf16[27,16,256]{2,1,0:T(8,128)(2,1)S(1)}, u32[]{:S(2)}, u32[]{:S(2)}) collective-permute-start(bf16[27,16,256]{2,1,0:T(8,128)(2,1)S(1)} %get-tuple-element.43), channel_id=1, source_target_pairs={{0,8},{1,3},{2,10},{3,5},{4,12},{5,7},{6,14},{7,1},{8,16},{9,11},{... | collective-permute-start | bytes 663560 | tf_op jit(solution)/shard_map/ppermute | solution.py:44
  65.0 1.3 collective-permute-start.13
  66.3 3.6 %collective-permute-done.11 = bf16[27,16,256]{2,1,0:T(8,128)(2,1)S(1)} collective-permute-done((bf16[27,16,256]{2,1,0:T(8,128)(2,1)S(1)}, bf16[27,16,256]{2,1,0:T(8,128)(2,1)S(1)}, u32[]{:S(2)}, u32[]{:S(2)}) %collective-permute-start.11) | collective-permute-done | bytes 221216 | tf_op jit(solution)/shard_map/ppermute | solution.py:44
  69.9 2.1 %collective-permute-done.12 = bf16[27,16,256]{2,1,0:T(8,128)(2,1)S(1)} collective-permute-done((bf16[27,16,256]{2,1,0:T(8,128)(2,1)S(1)}, bf16[27,16,256]{2,1,0:T(8,128)(2,1)S(1)}, u32[]{:S(2)}, u32[]{:S(2)}) %collective-permute-start.12) | collective-permute-done | bytes 221216 | tf_op jit(solution)/shard_map/ppermute | solution.py:44
  72.1 8.1 %collective-permute-start.16 = (bf16[27,16,256]{2,1,0:T(8,128)(2,1)S(1)}, bf16[27,16,256]{2,1,0:T(8,128)(2,1)S(1)}, u32[]{:S(2)}, u32[]{:S(2)}) collective-permute-start(bf16[27,16,256]{2,1,0:T(8,128)(2,1)S(1)} %add_convert_fusion.1), channel_id=1, source_target_pairs={{0,6},{1,97},{2,0},{3,99},{4,2},{5,101},{6,4},{7,103},{8,14},{9,10... | collective-permute-start | bytes 663560 | tf_op jit(solution)/shard_map/ppermute | solution.py:44
  80.2 2.5 %collective-permute-start.14 = (bf16[27,16,256]{2,1,0:T(8,128)(2,1)S(1)}, bf16[27,16,256]{2,1,0:T(8,128)(2,1)S(1)}, u32[]{:S(2)}, u32[]{:S(2)}) collective-permute-start(bf16[27,16,256]{2,1,0:T(8,128)(2,1)S(1)} %add_convert_fusion.1), channel_id=1, source_target_pairs={{0,4},{1,65},{2,6},{3,67},{4,0},{5,69},{6,2},{7,71},{8,12},{9,73},... | collective-permute-start | bytes 663560 | tf_op jit(solution)/shard_map/ppermute | solution.py:44
  83.1 5.5 %collective-permute-done.15 = bf16[27,16,256]{2,1,0:T(8,128)(2,1)S(1)} collective-permute-done((bf16[27,16,256]{2,1,0:T(8,128)(2,1)S(1)}, bf16[27,16,256]{2,1,0:T(8,128)(2,1)S(1)}, u32[]{:S(2)}, u32[]{:S(2)}) %collective-permute-start.15) | collective-permute-done | bytes 221216 | tf_op jit(solution)/shard_map/ppermute | solution.py:44
  88.7 3.3 %collective-permute-start.19 = (bf16[27,16,256]{2,1,0:T(8,128)(2,1)S(1)}, bf16[27,16,256]{2,1,0:T(8,128)(2,1)S(1)}, u32[]{:S(2)}, u32[]{:S(2)}) collective-permute-start(bf16[27,16,256]{2,1,0:T(8,128)(2,1)S(1)} %multiply_convert_fusion.part0), channel_id=1, source_target_pairs={{0,24},{1,7},{2,26},{3,1},{4,28},{5,3},{6,30},{7,5},{8,0},{9,15},{... | collective-permute-start | bytes 663560 | tf_op jit(solution)/shard_map/ppermute | solution.py:44
  94.1 4.5 %collective-permute-start.20 = (bf16[2,320,256]{2,1,0:T(8,128)(2,1)S(1)}, bf16[2,320,256]{2,1,0:T(8,128)(2,1)S(1)}, u32[]{:S(2)}, u32[]{:S(2)}) collective-permute-start(bf16[2,320,256]{2,1,0:T(8,128)(2,1)S(1)} %pack_both.1.packed_own), channel_id=1, source_target_pairs={{0,2},{1,3},{2,4},{3,5},{4,6},{5,7},{6,8},{7,9},{8,10},{9,11},{10,... | collective-permute-start | bytes 983048 | tf_op jit(solution)/shard_map/ppermute | solution.py:52
  98.7 5.6 %collective-permute-done.19.part3 = bf16[27,16,256]{2,1,0:T(8,128)(2,1)S(1)} collective-permute-done((bf16[27,16,256]{2,1,0:T(8,128)(2,1)S(1)}, bf16[27,16,256]{2,1,0:T(8,128)(2,1)S(1)}, u32[]{:S(2)}, u32[]{:S(2)}) %collective-permute-start.19) | collective-permute-done | bytes 221216 | tf_op jit(solution)/shard_map/ppermute | solution.py:44
  105.1 1.5 %collective-permute-start.25 = (bf16[27,64,256]{2,1,0:T(8,128)(2,1)S(1)}, bf16[27,64,256]{2,1,0:T(8,128)(2,1)S(1)}, u32[]{:S(2)}, u32[]{:S(2)}) collective-permute-start(bf16[27,64,256]{2,1,0:T(8,128)(2,1)S(1)} %get-tuple-element.53.refs_0_), channel_id=1, source_target_pairs={{0,32},{1,9},{2,34},{3,11},{4,36},{5,13},{6,38},{7,15},{8,40},{9,1... | collective-permute-start | bytes 2654216 | tf_op jit(solution)/shard_map/ppermute | solution.py:44
  107.1 1.9 %collective-permute-start.24 = (bf16[27,32,256]{2,1,0:T(8,128)(2,1)S(1)}, bf16[27,32,256]{2,1,0:T(8,128)(2,1)S(1)}, u32[]{:S(2)}, u32[]{:S(2)}) collective-permute-start(bf16[27,32,256]{2,1,0:T(8,128)(2,1)S(1)} %get-tuple-element.54), channel_id=1, source_target_pairs={{0,64},{1,17},{2,66},{3,19},{4,68},{5,21},{6,70},{7,23},{8,72},{9,... | collective-permute-start | bytes 1327112 | tf_op jit(solution)/shard_map/ppermute | solution.py:44
  109.1 1.8 %outer_frames.1 = (bf16[640,2304]{1,0:T(8,128)(2,1)S(1)}, bf16[640,2304]{1,0:T(8,128)(2,1)S(1)}) custom-call(s32[2,27]{1,0:T(2,128)S(1)} %compare_select_fusion.3.pick_ref, bf16[2,512,256]{2,1,0:T(8,128)(2,1)S(1)} %get-tuple-element.46.own.waited_for, bf16[2,512,256]{2,1,0:T(8,128)(2,1)S(1)} %collective-permute-done.6.both_mate.mate, ...), custom_call_target="tpu_custom_call" | custom-call | flops 1000000 | bytes 8000000 | tf_op jit(solution)/shard_map/outer_frames/pallas_call | solution.py:464
  111.0 2.7 %output_conv.1 = (bf16[1,512,256]{2,1,0:T(8,128)(2,1)}, bf16[27,64,256]{2,1,0:T(8,128)(2,1)S(1)}) custom-call(bf16[640,2304]{1,0:T(8,128)(2,1)S(1)} %get-tuple-element.47.frame, bf16[27,256,256]{2,1,0:T(8,128)(2,1)S(1)} %copy-done.1, bf16[27,64,256]{2,1,0:T(8,128)(2,1)S(1)} %get-tuple-element.48.passed), custom_call_target="tpu_custom_call", output_to_operand_aliasing={{1}: (2, {})} | custom-call | flops 1811939328 | bytes 4000000 | tf_op jit(solution)/shard_map/output_conv/pallas_call | solution.py:468
  113.6 2.7 %grad_input_conv.1 = (bf16[1,512,256]{2,1,0:T(8,128)(2,1)}, bf16[27,64,256]{2,1,0:T(8,128)(2,1)S(1)}) custom-call(bf16[640,2304]{1,0:T(8,128)(2,1)S(1)} %get-tuple-element.50.frame, bf16[27,256,256]{2,1,0:T(8,128)(2,1)S(1)} %copy-done, bf16[27,64,256]{2,1,0:T(8,128)(2,1)S(1)} %get-tuple-element.51.passed), custom_call_target="tpu_custom_call", output_to_operand_aliasing={{1}: (2, {})} | custom-call | flops 1811939328 | bytes 4000000 | tf_op jit(solution)/shard_map/grad_input_conv/pallas_call | solution.py:472
  116.4 3.4 %collective-permute-start.28 = (bf16[27,64,256]{2,1,0:T(8,128)(2,1)S(1)}, bf16[27,64,256]{2,1,0:T(8,128)(2,1)S(1)}, u32[]{:S(2)}, u32[]{:S(2)}) collective-permute-start(bf16[27,64,256]{2,1,0:T(8,128)(2,1)S(1)} %get-tuple-element.55), channel_id=1, source_target_pairs={{0,1},{1,0},{2,3},{3,2},{4,5},{5,4},{6,7},{7,6},{8,9},{9,8},{10,11... | collective-permute-start | bytes 2654216 | tf_op jit(solution)/shard_map/ppermute | solution.py:48
  119.8 1.5 %collective-permute-done.24.refs_1_ = bf16[27,32,256]{2,1,0:T(8,128)(2,1)S(1)} collective-permute-done((bf16[27,32,256]{2,1,0:T(8,128)(2,1)S(1)}, bf16[27,32,256]{2,1,0:T(8,128)(2,1)S(1)}, u32[]{:S(2)}, u32[]{:S(2)}) %collective-permute-start.24) | collective-permute-done | bytes 442400 | tf_op jit(solution)/shard_map/ppermute | solution.py:44
  121.3 3.4 %collective-permute-start.27 = (bf16[27,32,256]{2,1,0:T(8,128)(2,1)S(1)}, bf16[27,32,256]{2,1,0:T(8,128)(2,1)S(1)}, u32[]{:S(2)}, u32[]{:S(2)}) collective-permute-start(bf16[27,32,256]{2,1,0:T(8,128)(2,1)S(1)} %collective-permute-done.24.refs_1_), channel_id=1, source_target_pairs={{0,2},{1,7},{2,0},{3,5},{4,6},{5,3},{6,4},{7,1},{8,10},{9,15},{10,... | collective-permute-start | bytes 1327112 | tf_op jit(solution)/shard_map/ppermute | solution.py:44
  125.3 5.1 %collective-permute-done.27.refs_4_ = bf16[27,32,256]{2,1,0:T(8,128)(2,1)S(1)} collective-permute-done((bf16[27,32,256]{2,1,0:T(8,128)(2,1)S(1)}, bf16[27,32,256]{2,1,0:T(8,128)(2,1)S(1)}, u32[]{:S(2)}, u32[]{:S(2)}) %collective-permute-start.27) | collective-permute-done | bytes 442400 | tf_op jit(solution)/shard_map/ppermute | solution.py:44
  132.2 3.5 %place_late.1 = (bf16[27,256,256]{2,1,0:T(8,128)(2,1)}, bf16[27,256,256]{2,1,0:T(8,128)(2,1)}) custom-call(s32[6]{0:T(128)S(1)} %stack.43.place_ref, bf16[27,64,256]{2,1,0:T(8,128)(2,1)S(1)} %get-tuple-element.53.refs_0_, bf16[27,32,256]{2,1,0:T(8,128)(2,1)S(1)} %collective-permute-done.24.refs_1_, ...), custom_call_target="tpu_custom_call", output_to_operand_aliasing={{0}: (11, {}), {1}: (12, {})} | custom-call | flops 1000 | bytes 14000000 | tf_op jit(solution)/shard_map/place_late/pallas_call | solution.py:485
  (71 shorter events, 19.6 us)
Async XLA Ops:
  3.7 12.3 %collective-permute-start.3 = (bf16[2,320,256]{2,1,0:T(8,128)(2,1)}, bf16[2,320,256]{2,1,0:T(8,128)(2,1)}, u32[]{:S(2)}, u32[]{:S(2)}) collective-permute-start(bf16[2,320,256]{2,1,0:T(8,128)(2,1)} %get-tuple-element.33.packed_own), channel_id=1, source_target_pairs={{2,0},{3,1},{4,2},{5,3},{6,4},{7,5},{8,6},{9,7},{10,8},{11,9},{12,... | collective-permute-start | bytes 983048 | tf_op jit(solution)/shard_map/ppermute | solution.py:52
  5.0 11.7 %collective-permute-start.2 = (bf16[2,320,256]{2,1,0:T(8,128)(2,1)}, bf16[2,320,256]{2,1,0:T(8,128)(2,1)}, u32[]{:S(2)}, u32[]{:S(2)}) collective-permute-start(bf16[2,320,256]{2,1,0:T(8,128)(2,1)} %get-tuple-element.33.packed_own), channel_id=1, source_target_pairs={{0,2},{1,3},{2,4},{3,5},{4,6},{5,7},{6,8},{7,9},{8,10},{9,11},{10,... | collective-permute-start | bytes 983048 | tf_op jit(solution)/shard_map/ppermute | solution.py:52
  11.8 3.4 %collective-permute-start = (s32[1,27]{1,0:T(1,128)S(1)}, s32[1,27]{1,0:T(1,128)S(1)}, u32[]{:S(2)}, u32[]{:S(2)}) collective-permute-start(s32[1,27]{1,0:T(1,128)S(1)} %pad_add_fusion.2), channel_id=1, source_target_pairs={{0,1},{1,0},{2,3},{3,2},{4,5},{5,4},{6,7},{7,6},{8,9},{9,8},{10,11... | collective-permute-start | bytes 332 | tf_op jit(solution)/shard_map/ppermute | solution.py:48
  13.1 4.9 %collective-permute-start.1 = (bf16[2,512,256]{2,1,0:T(8,128)(2,1)}, bf16[2,512,256]{2,1,0:T(8,128)(2,1)}, u32[]{:S(2)}, u32[]{:S(2)}) collective-permute-start(bf16[2,512,256]{2,1,0:T(8,128)(2,1)} %get-tuple-element.32.own), channel_id=1, source_target_pairs={{0,1},{1,0},{2,3},{3,2},{4,5},{5,4},{6,7},{7,6},{8,9},{9,8},{10,11... | collective-permute-start | bytes 1572872 | tf_op jit(solution)/shard_map/ppermute | solution.py:48
  16.0 3.1 %collective-permute-start.5 = (bf16[2,320,256]{2,1,0:T(8,128)(2,1)}, bf16[2,320,256]{2,1,0:T(8,128)(2,1)S(1)}, u32[]{:S(2)}, u32[]{:S(2)}) collective-permute-start(bf16[2,320,256]{2,1,0:T(8,128)(2,1)} %collective-permute-done.3.after), channel_id=1, source_target_pairs={{0,1},{1,0},{2,3},{3,2},{4,5},{5,4},{6,7},{7,6},{8,9},{9,8},{10,11... | collective-permute-start | bytes 983048 | tf_op jit(solution)/shard_map/ppermute | solution.py:48
  16.7 2.6 %collective-permute-start.4 = (bf16[2,320,256]{2,1,0:T(8,128)(2,1)}, bf16[2,320,256]{2,1,0:T(8,128)(2,1)S(1)}, u32[]{:S(2)}, u32[]{:S(2)}) collective-permute-start(bf16[2,320,256]{2,1,0:T(8,128)(2,1)} %collective-permute-done.2.before), channel_id=1, source_target_pairs={{0,1},{1,0},{2,3},{3,2},{4,5},{5,4},{6,7},{7,6},{8,9},{9,8},{10,11... | collective-permute-start | bytes 983048 | tf_op jit(solution)/shard_map/ppermute | solution.py:48
  27.8 2.0 %collective-permute-start.6 = (bf16[2,512,256]{2,1,0:T(8,128)(2,1)S(1)}, bf16[2,512,256]{2,1,0:T(8,128)(2,1)S(1)}, u32[]{:S(2)}, u32[]{:S(2)}) collective-permute-start(bf16[2,512,256]{2,1,0:T(8,128)(2,1)S(1)} %grad_conv.1.both), channel_id=1, source_target_pairs={{0,1},{1,0},{2,3},{3,2},{4,5},{5,4},{6,7},{7,6},{8,9},{9,8},{10,11... | collective-permute-start | bytes 1572872 | tf_op jit(solution)/shard_map/ppermute | solution.py:48
  34.8 11.0 %collective-permute-start.9 = (bf16[27,32,256]{2,1,0:T(8,128)(2,1)S(1)}, bf16[27,32,256]{2,1,0:T(8,128)(2,1)S(1)}, u32[]{:S(2)}, u32[]{:S(2)}) collective-permute-start(bf16[27,32,256]{2,1,0:T(8,128)(2,1)S(1)} %get-tuple-element.40), channel_id=1, source_target_pairs={{0,2},{1,7},{2,0},{3,5},{4,6},{5,3},{6,4},{7,1},{8,10},{9,15},{10,... | collective-permute-start | bytes 1327112 | tf_op jit(solution)/shard_map/ppermute | solution.py:44
  39.9 22.5 %collective-permute-start.7 = (bf16[27,64,256]{2,1,0:T(8,128)(2,1)S(1)}, bf16[27,64,256]{2,1,0:T(8,128)(2,1)S(1)}, u32[]{:S(2)}, u32[]{:S(2)}) collective-permute-start(bf16[27,64,256]{2,1,0:T(8,128)(2,1)S(1)} %get-tuple-element.37), channel_id=1, source_target_pairs={{0,32},{1,9},{2,34},{3,11},{4,36},{5,13},{6,38},{7,15},{8,40},{9,1... | collective-permute-start | bytes 2654216 | tf_op jit(solution)/shard_map/ppermute | solution.py:44
  41.9 20.5 %collective-permute-start.8 = (bf16[27,64,256]{2,1,0:T(8,128)(2,1)S(1)}, bf16[27,64,256]{2,1,0:T(8,128)(2,1)S(1)}, u32[]{:S(2)}, u32[]{:S(2)}) collective-permute-start(bf16[27,64,256]{2,1,0:T(8,128)(2,1)S(1)} %get-tuple-element.38), channel_id=1, source_target_pairs={{0,96},{1,25},{2,98},{3,27},{4,100},{5,29},{6,102},{7,31},{8,104},... | collective-permute-start | bytes 2654216 | tf_op jit(solution)/shard_map/ppermute | solution.py:44
  45.9 16.5 %collective-permute-start.10 = (bf16[27,32,256]{2,1,0:T(8,128)(2,1)S(1)}, bf16[27,32,256]{2,1,0:T(8,128)(2,1)S(1)}, u32[]{:S(2)}, u32[]{:S(2)}) collective-permute-start(bf16[27,32,256]{2,1,0:T(8,128)(2,1)S(1)} %add_convert_fusion), channel_id=1, source_target_pairs={{0,64},{1,17},{2,66},{3,19},{4,68},{5,21},{6,70},{7,23},{8,72},{9,... | collective-permute-start | bytes 1327112 | tf_op jit(solution)/shard_map/ppermute | solution.py:44
  63.5 6.5 %collective-permute-start.11 = (bf16[27,16,256]{2,1,0:T(8,128)(2,1)S(1)}, bf16[27,16,256]{2,1,0:T(8,128)(2,1)S(1)}, u32[]{:S(2)}, u32[]{:S(2)}) collective-permute-start(bf16[27,16,256]{2,1,0:T(8,128)(2,1)S(1)} %get-tuple-element.42), channel_id=1, source_target_pairs={{0,16},{1,5},{2,18},{3,7},{4,20},{5,1},{6,22},{7,3},{8,24},{9,13},... | collective-permute-start | bytes 663560 | tf_op jit(solution)/shard_map/ppermute | solution.py:44
  63.6 8.4 %collective-permute-start.12 = (bf16[27,16,256]{2,1,0:T(8,128)(2,1)S(1)}, bf16[27,16,256]{2,1,0:T(8,128)(2,1)S(1)}, u32[]{:S(2)}, u32[]{:S(2)}) collective-permute-start(bf16[27,16,256]{2,1,0:T(8,128)(2,1)S(1)} %get-tuple-element.43), channel_id=1, source_target_pairs={{0,8},{1,3},{2,10},{3,5},{4,12},{5,7},{6,14},{7,1},{8,16},{9,11},{... | collective-permute-start | bytes 663560 | tf_op jit(solution)/shard_map/ppermute | solution.py:44
  65.0 7.0 %collective-permute-start.13 = (bf16[27,16,256]{2,1,0:T(8,128)(2,1)S(1)}, bf16[27,16,256]{2,1,0:T(8,128)(2,1)S(1)}, u32[]{:S(2)}, u32[]{:S(2)}) collective-permute-start(bf16[27,16,256]{2,1,0:T(8,128)(2,1)S(1)} %get-tuple-element.44), channel_id=1, source_target_pairs={{0,24},{1,7},{2,26},{3,1},{4,28},{5,3},{6,30},{7,5},{8,0},{9,15},{... | collective-permute-start | bytes 663560 | tf_op jit(solution)/shard_map/ppermute | solution.py:44
  72.1 11.0 %collective-permute-start.16 = (bf16[27,16,256]{2,1,0:T(8,128)(2,1)S(1)}, bf16[27,16,256]{2,1,0:T(8,128)(2,1)S(1)}, u32[]{:S(2)}, u32[]{:S(2)}) collective-permute-start(bf16[27,16,256]{2,1,0:T(8,128)(2,1)S(1)} %add_convert_fusion.1), channel_id=1, source_target_pairs={{0,6},{1,97},{2,0},{3,99},{4,2},{5,101},{6,4},{7,103},{8,14},{9,10... | collective-permute-start | bytes 663560 | tf_op jit(solution)/shard_map/ppermute | solution.py:44
  80.2 8.4 %collective-permute-start.15 = (bf16[27,16,256]{2,1,0:T(8,128)(2,1)S(1)}, bf16[27,16,256]{2,1,0:T(8,128)(2,1)S(1)}, u32[]{:S(2)}, u32[]{:S(2)}) collective-permute-start(bf16[27,16,256]{2,1,0:T(8,128)(2,1)S(1)} %add_convert_fusion.1), channel_id=1, source_target_pairs={{0,2},{1,33},{2,4},{3,35},{4,6},{5,37},{6,0},{7,39},{8,10},{9,41},... | collective-permute-start | bytes 663560 | tf_op jit(solution)/shard_map/ppermute | solution.py:44
  80.2 8.4 %collective-permute-start.14 = (bf16[27,16,256]{2,1,0:T(8,128)(2,1)S(1)}, bf16[27,16,256]{2,1,0:T(8,128)(2,1)S(1)}, u32[]{:S(2)}, u32[]{:S(2)}) collective-permute-start(bf16[27,16,256]{2,1,0:T(8,128)(2,1)S(1)} %add_convert_fusion.1), channel_id=1, source_target_pairs={{0,4},{1,65},{2,6},{3,67},{4,0},{5,69},{6,2},{7,71},{8,12},{9,73},... | collective-permute-start | bytes 663560 | tf_op jit(solution)/shard_map/ppermute | solution.py:44
  88.7 15.6 %collective-permute-start.19 = (bf16[27,16,256]{2,1,0:T(8,128)(2,1)S(1)}, bf16[27,16,256]{2,1,0:T(8,128)(2,1)S(1)}, u32[]{:S(2)}, u32[]{:S(2)}) collective-permute-start(bf16[27,16,256]{2,1,0:T(8,128)(2,1)S(1)} %multiply_convert_fusion.part0), channel_id=1, source_target_pairs={{0,24},{1,7},{2,26},{3,1},{4,28},{5,3},{6,30},{7,5},{8,0},{9,15},{... | collective-permute-start | bytes 663560 | tf_op jit(solution)/shard_map/ppermute | solution.py:44
  92.0 12.3 %collective-permute-start.18 = (bf16[27,16,256]{2,1,0:T(8,128)(2,1)S(1)}, bf16[27,16,256]{2,1,0:T(8,128)(2,1)S(1)}, u32[]{:S(2)}, u32[]{:S(2)}) collective-permute-start(bf16[27,16,256]{2,1,0:T(8,128)(2,1)S(1)} %multiply_convert_fusion.part0), channel_id=1, source_target_pairs={{0,16},{1,5},{2,18},{3,7},{4,20},{5,1},{6,22},{7,3},{8,24},{9,13},... | collective-permute-start | bytes 663560 | tf_op jit(solution)/shard_map/ppermute | solution.py:44
  92.0 12.3 %collective-permute-start.17 = (bf16[27,16,256]{2,1,0:T(8,128)(2,1)S(1)}, bf16[27,16,256]{2,1,0:T(8,128)(2,1)S(1)}, u32[]{:S(2)}, u32[]{:S(2)}) collective-permute-start(bf16[27,16,256]{2,1,0:T(8,128)(2,1)S(1)} %multiply_convert_fusion.part0), channel_id=1, source_target_pairs={{0,8},{1,3},{2,10},{3,5},{4,12},{5,7},{6,14},{7,1},{8,16},{9,11},{... | collective-permute-start | bytes 663560 | tf_op jit(solution)/shard_map/ppermute | solution.py:44
  92.8 13.8 %collective-permute-start.21 = (bf16[2,320,256]{2,1,0:T(8,128)(2,1)S(1)}, bf16[2,320,256]{2,1,0:T(8,128)(2,1)S(1)}, u32[]{:S(2)}, u32[]{:S(2)}) collective-permute-start(bf16[2,320,256]{2,1,0:T(8,128)(2,1)S(1)} %pack_both.1.packed_own), channel_id=1, source_target_pairs={{2,0},{3,1},{4,2},{5,3},{6,4},{7,5},{8,6},{9,7},{10,8},{11,9},{12,... | collective-permute-start | bytes 983048 | tf_op jit(solution)/shard_map/ppermute | solution.py:52
  94.1 12.5 %collective-permute-start.20 = (bf16[2,320,256]{2,1,0:T(8,128)(2,1)S(1)}, bf16[2,320,256]{2,1,0:T(8,128)(2,1)S(1)}, u32[]{:S(2)}, u32[]{:S(2)}) collective-permute-start(bf16[2,320,256]{2,1,0:T(8,128)(2,1)S(1)} %pack_both.1.packed_own), channel_id=1, source_target_pairs={{0,2},{1,3},{2,4},{3,5},{4,6},{5,7},{6,8},{7,9},{8,10},{9,11},{10,... | collective-permute-start | bytes 983048 | tf_op jit(solution)/shard_map/ppermute | solution.py:52
  105.0 19.7 %collective-permute-start.26 = (bf16[27,64,256]{2,1,0:T(8,128)(2,1)S(1)}, bf16[27,64,256]{2,1,0:T(8,128)(2,1)S(1)}, u32[]{:S(2)}, u32[]{:S(2)}) collective-permute-start(bf16[27,64,256]{2,1,0:T(8,128)(2,1)S(1)} %get-tuple-element.53.refs_0_), channel_id=1, source_target_pairs={{0,96},{1,25},{2,98},{3,27},{4,100},{5,29},{6,102},{7,31},{8,104},... | collective-permute-start | bytes 2654216 | tf_op jit(solution)/shard_map/ppermute | solution.py:44
  105.1 19.6 %collective-permute-start.25 = (bf16[27,64,256]{2,1,0:T(8,128)(2,1)S(1)}, bf16[27,64,256]{2,1,0:T(8,128)(2,1)S(1)}, u32[]{:S(2)}, u32[]{:S(2)}) collective-permute-start(bf16[27,64,256]{2,1,0:T(8,128)(2,1)S(1)} %get-tuple-element.53.refs_0_), channel_id=1, source_target_pairs={{0,32},{1,9},{2,34},{3,11},{4,36},{5,13},{6,38},{7,15},{8,40},{9,1... | collective-permute-start | bytes 2654216 | tf_op jit(solution)/shard_map/ppermute | solution.py:44
  106.6 2.5 %collective-permute-start.23 = (bf16[2,320,256]{2,1,0:T(8,128)(2,1)S(1)}, bf16[2,320,256]{2,1,0:T(8,128)(2,1)S(1)}, u32[]{:S(2)}, u32[]{:S(2)}) collective-permute-start(bf16[2,320,256]{2,1,0:T(8,128)(2,1)S(1)} %collective-permute-done.21.after), channel_id=1, source_target_pairs={{0,1},{1,0},{2,3},{3,2},{4,5},{5,4},{6,7},{7,6},{8,9},{9,8},{10,11... | collective-permute-start | bytes 983048 | tf_op jit(solution)/shard_map/ppermute | solution.py:48
  106.6 2.5 %collective-permute-start.22 = (bf16[2,320,256]{2,1,0:T(8,128)(2,1)S(1)}, bf16[2,320,256]{2,1,0:T(8,128)(2,1)S(1)}, u32[]{:S(2)}, u32[]{:S(2)}) collective-permute-start(bf16[2,320,256]{2,1,0:T(8,128)(2,1)S(1)} %collective-permute-done.20.before), channel_id=1, source_target_pairs={{0,1},{1,0},{2,3},{3,2},{4,5},{5,4},{6,7},{7,6},{8,9},{9,8},{10,11... | collective-permute-start | bytes 983048 | tf_op jit(solution)/shard_map/ppermute | solution.py:48
  107.1 14.2 %collective-permute-start.24 = (bf16[27,32,256]{2,1,0:T(8,128)(2,1)S(1)}, bf16[27,32,256]{2,1,0:T(8,128)(2,1)S(1)}, u32[]{:S(2)}, u32[]{:S(2)}) collective-permute-start(bf16[27,32,256]{2,1,0:T(8,128)(2,1)S(1)} %get-tuple-element.54), channel_id=1, source_target_pairs={{0,64},{1,17},{2,66},{3,19},{4,68},{5,21},{6,70},{7,23},{8,72},{9,... | collective-permute-start | bytes 1327112 | tf_op jit(solution)/shard_map/ppermute | solution.py:44
  116.4 14.0 %collective-permute-start.28 = (bf16[27,64,256]{2,1,0:T(8,128)(2,1)S(1)}, bf16[27,64,256]{2,1,0:T(8,128)(2,1)S(1)}, u32[]{:S(2)}, u32[]{:S(2)}) collective-permute-start(bf16[27,64,256]{2,1,0:T(8,128)(2,1)S(1)} %get-tuple-element.55), channel_id=1, source_target_pairs={{0,1},{1,0},{2,3},{3,2},{4,5},{5,4},{6,7},{7,6},{8,9},{9,8},{10,11... | collective-permute-start | bytes 2654216 | tf_op jit(solution)/shard_map/ppermute | solution.py:48
  121.3 9.1 %collective-permute-start.27 = (bf16[27,32,256]{2,1,0:T(8,128)(2,1)S(1)}, bf16[27,32,256]{2,1,0:T(8,128)(2,1)S(1)}, u32[]{:S(2)}, u32[]{:S(2)}) collective-permute-start(bf16[27,32,256]{2,1,0:T(8,128)(2,1)S(1)} %collective-permute-done.24.refs_1_), channel_id=1, source_target_pairs={{0,2},{1,7},{2,0},{3,5},{4,6},{5,3},{6,4},{7,1},{8,10},{9,15},{10,... | collective-permute-start | bytes 1327112 | tf_op jit(solution)/shard_map/ppermute | solution.py:44
  124.7 7.5 %collective-permute-start.31 = (bf16[27,64,256]{2,1,0:T(8,128)(2,1)S(1)}, bf16[27,64,256]{2,1,0:T(8,128)(2,1)S(1)}, u32[]{:S(2)}, u32[]{:S(2)}) collective-permute-start(bf16[27,64,256]{2,1,0:T(8,128)(2,1)S(1)} %collective-permute-done.26.refs_3_), channel_id=1, source_target_pairs={{0,1},{1,0},{2,3},{3,2},{4,5},{5,4},{6,7},{7,6},{8,9},{9,8},{10,11... | collective-permute-start | bytes 2654216 | tf_op jit(solution)/shard_map/ppermute | solution.py:48
  124.7 7.5 %collective-permute-start.30 = (bf16[27,64,256]{2,1,0:T(8,128)(2,1)S(1)}, bf16[27,64,256]{2,1,0:T(8,128)(2,1)S(1)}, u32[]{:S(2)}, u32[]{:S(2)}) collective-permute-start(bf16[27,64,256]{2,1,0:T(8,128)(2,1)S(1)} %collective-permute-done.25.refs_2_), channel_id=1, source_target_pairs={{0,1},{1,0},{2,3},{3,2},{4,5},{5,4},{6,7},{7,6},{8,9},{9,8},{10,11... | collective-permute-start | bytes 2654216 | tf_op jit(solution)/shard_map/ppermute | solution.py:48
  125.2 5.2 %collective-permute-start.29 = (bf16[27,32,256]{2,1,0:T(8,128)(2,1)S(1)}, bf16[27,32,256]{2,1,0:T(8,128)(2,1)S(1)}, u32[]{:S(2)}, u32[]{:S(2)}) collective-permute-start(bf16[27,32,256]{2,1,0:T(8,128)(2,1)S(1)} %collective-permute-done.24.refs_1_), channel_id=1, source_target_pairs={{0,1},{1,0},{2,3},{3,2},{4,5},{5,4},{6,7},{7,6},{8,9},{9,8},{10,11... | collective-permute-start | bytes 1327112 | tf_op jit(solution)/shard_map/ppermute | solution.py:48
  (5 other events, 28.4 us)
